TPU v7x, 32 devices: a whole 2x2x4 slice. The times are simulated.
32 devices in a mesh: pipe: 2 (over y), dp: 16 (over z, x, core).
Axes of the slice: x: 2, y: 2, z: 4, core: 2. Of those that a mesh axis runs over, the one named last changes fastest.
Arguments:
- history_codes: int32 [1024, 80], P('dp'), may hold values from 0 to 255
- user_ids: int32 [1024], P('dp'), may hold values from 0 to 1999
- targets: int32 [1024, 4], P('dp'), may hold values from 0 to 255
- domains: int32 [1024], P('dp'), may hold values from 0 to 2
- mixer: float32 [2, 128, 2304], P('pipe'), may hold values from -0.5 to 0.5
- mixer_moment: float32 [2, 128, 2304], P('pipe'), may hold values from -0.00024414062 to 0.00024414062
- mixer_square: float32 [2, 128, 2304], P('pipe'), may hold values from 1.6639334e-10 to 6.655734e-10
- feed: float32 [2, 128, 2048], P('pipe'), may hold values from -0.5 to 0.5
- feed_moment: float32 [2, 128, 2048], P('pipe'), may hold values from -0.00024414062 to 0.00024414062
- feed_square: float32 [2, 128, 2048], P('pipe'), may hold values from 1.6639334e-10 to 6.655734e-10
- embedding: float32 [3024, 128], replicated, may hold values from -0.6 to 0.6
- embedding_moment: float32 [3024, 128], replicated, may hold values from -0.00024414062 to 0.00024414062
- embedding_square: float32 [3024, 128], replicated, may hold values from 1.6639334e-10 to 6.655734e-10
- gains: float32 [7, 128], replicated, may hold values from 0.5 to 1.5
- gains_moment: float32 [7, 128], replicated, may hold values from -0.0014648438 to 0.0014648438
- gains_square: float32 [7, 128], replicated, may hold values from 4.1598334e-09 to 1.6639333e-08
- position_bias: float32 [2, 32, 6], replicated, may hold values from -3 to 3
- bias_moment: float32 [2, 32, 6], replicated, may hold values from -0.00024414062 to 0.00024414062
- bias_square: float32 [2, 32, 6], replicated, may hold values from 1.3311467e-10 to 5.324587e-10
Outputs:
- loss: float32 [], replicated
- gradient_norm: float32 [], replicated
- section_norms: float32 [2], replicated
- histograms: float32 [4, 256], replicated
- new_mixer: float32 [2, 128, 2304], P('pipe')
- new_mixer_moment: float32 [2, 128, 2304], P('pipe')
- new_mixer_square: float32 [2, 128, 2304], P('pipe')
- new_feed: float32 [2, 128, 2048], P('pipe')
- new_feed_moment: float32 [2, 128, 2048], P('pipe')
- new_feed_square: float32 [2, 128, 2048], P('pipe')
- new_embedding: float32 [3024, 128], replicated
- new_embedding_moment: float32 [3024, 128], replicated
- new_embedding_square: float32 [3024, 128], replicated
- new_gains: float32 [7, 128], replicated
- new_gains_moment: float32 [7, 128], replicated
- new_gains_square: float32 [7, 128], replicated
- new_bias: float32 [2, 32, 6], replicated
- new_bias_moment: float32 [2, 32, 6], replicated
- new_bias_square: float32 [2, 32, 6], replicated
- mixer_copy: bfloat16 [2, 128, 2304], P('pipe')
- feed_copy: bfloat16 [2, 128, 2048], P('pipe')
- embedding_copy: bfloat16 [3024, 128], replicated
All inputs are finite; a program needn't handle non-finite values.
Results may differ from a plain program's by a relative error of at most 0.03.
Values may be sent and summed in bfloat16 or wider, within the bound.
A program may use at most 384 MiB of HBM per device.

v0:
```python
import jax
import jax.numpy as jnp
from jax import lax
from jax.sharding import PartitionSpec as P

D = 128
HEADS = 6
HEAD_DIM = 64
FF = 1024
CODEBOOK = 256
LEVELS = 4
BUCKETS = 32
DOMAINS = 3
HIST_LEN = 81
MICRO = 4
STEP = 5
CODES = 1024
VOCAB = 3024


highest = lax.Precision.HIGHEST
norm_eps = 1e-06
beta_one = 0.9
beta_two = 0.999
adam_eps = 1e-08
clip_norm = 0.5
rate_matrix = 0.04
rate_gain = 0.8
rate_small = 0.3
decay_matrix = 0.01


def shifted(block, axis, distance):
    devices = range(lax.axis_size(axis))
    route = [(i - distance, i) for i in devices if i - distance in devices]
    return lax.ppermute(block, axis, route)


def encoder_buckets():
    places = jnp.arange(HIST_LEN)
    offset = places[None, :] - places[:, None]
    distance = jnp.abs(offset)
    remote = jnp.zeros_like(distance)
    for edge in (12, 16, 23, 32, 46, 64, 91):
        remote = remote + (distance >= edge).astype(jnp.int32)
    nearby = jnp.minimum(jnp.where(distance < 8, distance, 8 + remote), 15)
    return nearby + 16 * (offset > 0).astype(jnp.int32)


def history_ids(codes, users):
    level = jnp.arange(codes.shape[1]) % LEVELS
    return jnp.concatenate([CODES + users[:, None], level[None, :] * CODEBOOK + codes], 1).reshape(
        -1
    )


def causal_mask():
    places = jnp.arange(LEVELS)
    return places[:, None] >= places[None, :]


def blank_array(shape, dtype=jnp.float32):
    return jnp.zeros(shape, dtype)


def attention_blank(count, length):
    size = count * length
    heads = (count, length, HEADS, HEAD_DIM)
    return (
        blank_array((size, D)),
        blank_array((size, 1)),
        blank_array((size, D), jnp.bfloat16),
        blank_array(heads, jnp.bfloat16),
        blank_array(heads, jnp.bfloat16),
        blank_array(heads, jnp.bfloat16),
        blank_array((count, HEADS, length)),
        blank_array((size, HEADS * HEAD_DIM), jnp.bfloat16),
    )


def feed_blank(size):
    return (
        blank_array((size, D)),
        blank_array((size, 1)),
        blank_array((size, D), jnp.bfloat16),
        blank_array((size, FF)),
        blank_array((size, FF), jnp.bfloat16),
    )


def encoder_blank(count):
    size = count * HIST_LEN
    return (
        blank_array((size,), jnp.int32),
        attention_blank(count, HIST_LEN),
        feed_blank(size),
        blank_array((size, D)),
        blank_array((size, 1)),
    )


def product(left, right):
    return jnp.dot(left, right, preferred_element_type=jnp.float32)


def product_back(left, right):
    return lax.dot_general(
        left, right, (((1,), (1,)), ((), ())), preferred_element_type=jnp.float32
    )


def product_outer(left, right):
    return lax.dot_general(
        left, right, (((0,), (0,)), ((), ())), preferred_element_type=jnp.float32
    )


def norm_forward(rows, gain):
    inverse = lax.rsqrt(jnp.mean(rows * rows, -1, keepdims=True) + norm_eps)
    return (rows * inverse * gain, inverse)


def norm_backward(rows, gain, inverse, upstream):
    scaled = rows * inverse
    back_gain = jnp.sum(upstream * scaled, 0)
    inner = upstream * gain
    return (inverse * (inner - scaled * jnp.mean(inner * scaled, -1, keepdims=True)), back_gain)


def split_heads(table, count):
    return table.reshape(count, -1, HEADS, HEAD_DIM)


def bias_lookup(table, buckets):
    size = buckets.shape[0]
    onehot = (buckets.reshape(-1)[:, None] == jnp.arange(table.shape[0])[None, :]).astype(
        jnp.float32
    )
    looked = jnp.dot(onehot, table, precision=highest).reshape(size, size, -1)
    return (jnp.transpose(looked, (2, 0, 1)), onehot)


def bias_back(onehot, bias_sum):
    flat = jnp.transpose(bias_sum, (1, 2, 0)).reshape(onehot.shape[0], -1)
    return lax.dot_general(onehot, flat, (((0,), (0,)), ((), ())), precision=highest)


def attention_scores(query, keys, bias, mask):
    scores = (
        HEAD_DIM ** (-0.5)
        * jnp.einsum("nqhd,nkhd->nhqk", query, keys, preferred_element_type=jnp.float32)
        + bias
    )
    if mask is not None:
        scores = jnp.where(mask, scores, -1e30)
    return scores


def attention_forward(query, keys, values, bias, mask):
    scores = attention_scores(query, keys, bias, mask)
    log_total = jax.nn.logsumexp(scores, -1)
    chance = jnp.exp(scores - log_total[..., None]).astype(jnp.bfloat16)
    output = jnp.einsum("nhqk,nkhd->nqhd", chance, values, preferred_element_type=jnp.float32)
    return (output.astype(jnp.bfloat16), log_total)


def attention_backward(query, keys, values, bias, mask, log_total, back_out):
    scores = attention_scores(query, keys, bias, mask)
    chance = jnp.exp(scores - log_total[..., None])
    back_chance = jnp.einsum(
        "nqhd,nkhd->nhqk", back_out, values, preferred_element_type=jnp.float32
    )
    inner = jnp.sum(back_chance * chance, -1, keepdims=True)
    back_scores = (chance * (back_chance - inner)).astype(jnp.bfloat16)
    scale = HEAD_DIM ** (-0.5)
    back_query = scale * jnp.einsum(
        "nhqk,nkhd->nqhd", back_scores, keys, preferred_element_type=jnp.float32
    )
    back_keys = scale * jnp.einsum(
        "nhqk,nqhd->nkhd", back_scores, query, preferred_element_type=jnp.float32
    )
    back_values = jnp.einsum(
        "nhqk,nqhd->nkhd", chance.astype(jnp.bfloat16), back_out, preferred_element_type=jnp.float32
    )
    bias_sum = jnp.sum(back_scores.astype(jnp.float32), 0)
    return (back_query, back_keys, back_values, bias_sum)


def attention_block(rows, gain, w_in, w_out, bias, mask, count):
    normed, inverse = norm_forward(rows, gain)
    normed_low = normed.astype(jnp.bfloat16)
    projected = product(normed_low, w_in).astype(jnp.bfloat16)
    width = w_out.shape[1]
    query = split_heads(projected[:, :width], count)
    keys = split_heads(projected[:, width : 2 * width], count)
    values = split_heads(projected[:, 2 * width :], count)
    output, log_total = attention_forward(query, keys, values, bias, mask)
    output = output.reshape(rows.shape[0], width)
    kept = (rows, inverse, normed_low, query, keys, values, log_total, output)
    return (rows + product_back(output, w_out), kept)


def attention_block_back(kept, upstream, gain, w_in, w_out, bias, mask, count):
    rows, inverse, normed_low, query, keys, values, log_total, output = kept
    width = w_out.shape[1]
    branch = upstream.astype(jnp.bfloat16)
    back_w_out = product_outer(branch, output)
    back_output = split_heads(product(branch, w_out).astype(jnp.bfloat16), count)
    back_query, back_keys, back_values, bias_sum = attention_backward(
        query, keys, values, bias, mask, log_total, back_output
    )
    back_projected = jnp.concatenate(
        [
            back_query.reshape(-1, width),
            back_keys.reshape(-1, width),
            back_values.reshape(-1, width),
        ],
        1,
    ).astype(jnp.bfloat16)
    back_w_in = product_outer(normed_low, back_projected)
    back_normed = product_back(back_projected, w_in)
    back_rows, back_gain = norm_backward(rows, gain, inverse, back_normed)
    return (upstream + back_rows, back_gain, back_w_in, back_w_out, bias_sum)


def cross_forward(query_low, memory, count):
    width = HEADS * HEAD_DIM
    output, log_total = attention_forward(
        split_heads(query_low, count),
        split_heads(memory[:, :width], count),
        split_heads(memory[:, width:], count),
        0.0,
        None,
    )
    return (output.reshape(query_low.shape[0], width), log_total)


def cross_backward(query_low, memory, log_total, back_output, count):
    width = HEADS * HEAD_DIM
    back_query, back_keys, back_values, unused = attention_backward(
        split_heads(query_low, count),
        split_heads(memory[:, :width], count),
        split_heads(memory[:, width:], count),
        0.0,
        None,
        log_total,
        split_heads(back_output, count),
    )
    back_memory = jnp.concatenate(
        [back_keys.reshape(-1, width), back_values.reshape(-1, width)], 1
    ).astype(jnp.bfloat16)
    return (back_query.reshape(query_low.shape[0], width).astype(jnp.bfloat16), back_memory)


def feed_block(rows, gain, w_up, w_down):
    normed, inverse = norm_forward(rows, gain)
    normed_low = normed.astype(jnp.bfloat16)
    lifted = product(normed_low, w_up)
    active = jnp.maximum(lifted, 0.0).astype(jnp.bfloat16)
    return (rows + product_back(active, w_down), (rows, inverse, normed_low, lifted, active))


def feed_block_back(kept, upstream, gain, w_up, w_down):
    rows, inverse, normed_low, lifted, active = kept
    branch = upstream.astype(jnp.bfloat16)
    back_down = product_outer(branch, active)
    back_active = product(branch, w_down)
    back_lifted = jnp.where(lifted > 0, back_active, 0.0).astype(jnp.bfloat16)
    back_up = product_outer(normed_low, back_lifted)
    back_normed = product_back(back_lifted, w_up)
    back_rows, back_gain = norm_backward(rows, gain, inverse, back_normed)
    return (upstream + back_rows, back_gain, back_up, back_down)


def encoder_forward(codes, users, embedding, gains, enc_bias, weights_low, feed_low):
    count = codes.shape[0]
    width = HEADS * HEAD_DIM
    token_ids = history_ids(codes, users)
    start = embedding[token_ids]
    middle, kept_attention = attention_block(
        start,
        gains[0],
        weights_low[:, : 3 * width],
        weights_low[:, 3 * width : 4 * width],
        enc_bias,
        None,
        count,
    )
    after, kept_feed = feed_block(middle, gains[1], feed_low[:, :FF], feed_low[:, FF:])
    final, inverse = norm_forward(after, gains[2])
    return (final.astype(jnp.bfloat16), (token_ids, kept_attention, kept_feed, after, inverse))


def encoder_backward(kept, back_final, gains, enc_bias, enc_onehot, weights_low, feed_low, count):
    token_ids, kept_attention, kept_feed, after, inverse = kept
    width = HEADS * HEAD_DIM
    back_after, gain_last = norm_backward(after, gains[2], inverse, back_final)
    back_middle, gain_feed, back_up, back_down = feed_block_back(
        kept_feed, back_after, gains[1], feed_low[:, :FF], feed_low[:, FF:]
    )
    back_start, gain_first, back_in, back_out, bias_sum = attention_block_back(
        kept_attention,
        back_middle,
        gains[0],
        weights_low[:, : 3 * width],
        weights_low[:, 3 * width : 4 * width],
        enc_bias,
        None,
        count,
    )
    embed_grad = jax.ops.segment_sum(back_start, token_ids, VOCAB)
    gain_grad = jnp.concatenate(
        [jnp.stack([gain_first, gain_feed, gain_last]), jnp.zeros((4, gains.shape[1]), jnp.float32)]
    )
    bias_grad = jnp.stack(
        [bias_back(enc_onehot, bias_sum), jnp.zeros((BUCKETS, HEADS), jnp.float32)]
    )
    return (
        jnp.concatenate([back_in, back_out], 1),
        jnp.concatenate([back_up, back_down], 1),
        embed_grad,
        gain_grad,
        bias_grad,
    )


def decoder_front(goal, embedding, gains, dec_bias, weights_low):
    count = goal.shape[0]
    width = HEADS * HEAD_DIM
    start_ids = jnp.concatenate([jnp.zeros((count, 1), jnp.int32), goal[:, :-1]], 1).reshape(-1)
    start = embedding[start_ids]
    first, kept_self = attention_block(
        start,
        gains[3],
        weights_low[:, : 3 * width],
        weights_low[:, 3 * width : 4 * width],
        dec_bias,
        causal_mask(),
        count,
    )
    normed, inverse = norm_forward(first, gains[4])
    normed_low = normed.astype(jnp.bfloat16)
    query_low = product(normed_low, weights_low[:, 4 * width : 5 * width]).astype(jnp.bfloat16)
    return (query_low, (start_ids, kept_self, first, inverse, normed_low))


def decoder_rest(front_kept, output, goal, weight, table, gains, weights_low, feed_low):
    start_ids, kept_self, first, inverse_cross, normed_cross = front_kept
    width = HEADS * HEAD_DIM
    w_out = weights_low[:, 5 * width :]
    second = first + product_back(output, w_out)
    third, kept_feed = feed_block(second, gains[5], feed_low[:, :FF], feed_low[:, FF:])
    final, inverse = norm_forward(third, gains[6])
    final_low = final.astype(jnp.bfloat16)
    logits = product_back(final_low, table)
    log_total = jax.nn.logsumexp(logits, -1)
    match = goal.reshape(-1)[:, None] == jnp.arange(table.shape[0])[None, :]
    picked = jnp.sum(jnp.where(match, logits, 0.0), -1)
    loss_part = jnp.sum(weight * (log_total - picked))
    back_logits = (
        weight[:, None] * (jnp.exp(logits - log_total[:, None]) - match.astype(jnp.float32))
    ).astype(jnp.bfloat16)
    back_final = product(back_logits, table)
    table_grad = product_outer(back_logits, final_low)
    back_third, gain_out = norm_backward(third, gains[6], inverse, back_final)
    back_second, gain_feed, back_up, back_down = feed_block_back(
        kept_feed, back_third, gains[5], feed_low[:, :FF], feed_low[:, FF:]
    )
    branch = back_second.astype(jnp.bfloat16)
    cross_out = product_outer(branch, output)
    back_output = product(branch, w_out).astype(jnp.bfloat16)
    return (
        back_output,
        back_second,
        (
            cross_out,
            jnp.concatenate([back_up, back_down], 1),
            gain_feed,
            gain_out,
            table_grad,
            loss_part,
        ),
    )


def decoder_finish(
    front_kept,
    back_second,
    back_query,
    partial_value,
    gains,
    dec_bias,
    dec_onehot,
    weights_low,
    count,
):
    start_ids, kept_self, first, inverse_cross, normed_cross = front_kept
    cross_out, feed_grad, gain_feed, gain_out, table_grad, loss_part = partial_value
    width = HEADS * HEAD_DIM
    cross_in = product_outer(normed_cross, back_query)
    back_rows, gain_cross = norm_backward(
        first,
        gains[4],
        inverse_cross,
        product_back(back_query, weights_low[:, 4 * width : 5 * width]),
    )
    back_first = back_second + back_rows
    back_start, gain_self, self_in, self_out, bias_sum = attention_block_back(
        kept_self,
        back_first,
        gains[3],
        weights_low[:, : 3 * width],
        weights_low[:, 3 * width : 4 * width],
        dec_bias,
        causal_mask(),
        count,
    )
    embed_grad = jax.ops.segment_sum(back_start, start_ids, VOCAB).at[:CODES].add(table_grad)
    gain_grad = jnp.concatenate(
        [
            jnp.zeros((3, gains.shape[1]), jnp.float32),
            jnp.stack([gain_self, gain_cross, gain_feed, gain_out]),
        ]
    )
    bias_grad = jnp.stack(
        [jnp.zeros((BUCKETS, HEADS), jnp.float32), bias_back(dec_onehot, bias_sum)]
    )
    mixer_grad = jnp.concatenate([self_in, self_out, cross_in, cross_out], 1)
    return (mixer_grad, feed_grad, embed_grad, gain_grad, bias_grad, loss_part)


def zero_grads(mixer, feed, embedding, gains, position_bias):
    return (
        jnp.zeros(mixer.shape[1:], jnp.float32),
        jnp.zeros(feed.shape[1:], jnp.float32),
        jnp.zeros(embedding.shape, jnp.float32),
        jnp.zeros(gains.shape, jnp.float32),
        jnp.zeros(position_bias.shape, jnp.float32),
        jnp.zeros((), jnp.float32),
    )


def adam_step(weight, moment, square, slope, rate, decay):
    moment = beta_one * moment + (1 - beta_one) * slope
    square = beta_two * square + (1 - beta_two) * slope * slope
    unbiased_moment = moment / (1 - beta_one**STEP)
    unbiased_square = square / (1 - beta_two**STEP)
    return (
        weight - rate * (unbiased_moment / (jnp.sqrt(unbiased_square) + adam_eps) + decay * weight),
        moment,
        square,
    )


def shards(
    history_codes,
    user_ids,
    targets,
    domains,
    mixer,
    mixer_moment,
    mixer_square,
    feed,
    feed_moment,
    feed_square,
    embedding,
    embedding_moment,
    embedding_square,
    gains,
    gains_moment,
    gains_square,
    position_bias,
    bias_moment,
    bias_square,
):
    width = HEADS * HEAD_DIM
    model_width = mixer.shape[1]
    section = lax.axis_index("pipe")
    weights_low = mixer[0].astype(jnp.bfloat16)
    feed_low = feed[0].astype(jnp.bfloat16)
    table = embedding[:CODES].astype(jnp.bfloat16)
    hits = (domains[:, None] == jnp.arange(DOMAINS)[None, :]).astype(jnp.float32)
    local_counts = LEVELS * jnp.sum(hits, 0)
    local_histograms = jnp.sum(
        (targets[:, :, None] == jnp.arange(CODEBOOK)[None, None, :]).astype(jnp.float32), 0
    )
    counts, histograms = lax.psum((local_counts, local_histograms), "dp")
    share = 1.0 / (DOMAINS * jnp.maximum(counts, 1.0))
    history_weight = jnp.sum(hits * share[None, :], 1)
    goals = jnp.arange(LEVELS)[None, :] * CODEBOOK + targets
    enc_bias, enc_onehot = bias_lookup(position_bias[0], encoder_buckets())
    places = jnp.arange(LEVELS)
    dec_bias, dec_onehot = bias_lookup(
        position_bias[1], jnp.maximum(places[:, None] - places[None, :], 0)
    )
    count = history_codes.shape[0] // MICRO
    rows = count * HIST_LEN
    sent_width = 2 * width
    back_type = jnp.bfloat16
    cross_shape = ()

    def blank():
        return zero_grads(mixer, feed, embedding, gains, position_bias)

    totals = blank()
    for part in range(MICRO):
        codes = history_codes[part * count : (part + 1) * count]
        users = user_ids[part * count : (part + 1) * count]
        goal = goals[part * count : (part + 1) * count]
        weight = jnp.broadcast_to(
            history_weight[part * count : (part + 1) * count, None], (count, LEVELS)
        ).reshape(-1)

        def encode():
            final_low, kept = encoder_forward(
                codes, users, embedding, gains, enc_bias, weights_low, feed_low
            )
            sent = product(final_low, weights_low[:, 4 * width :]).astype(jnp.bfloat16)
            return (sent, final_low, kept)

        def skip_encode():
            return (
                blank_array((rows, sent_width), jnp.bfloat16),
                blank_array((rows, model_width), jnp.bfloat16),
                encoder_blank(count),
            )

        encoded, final_low, enc_kept = lax.cond(section == 0, encode, skip_encode)

        def encoder_grads(back_final, cross_part):
            attention_grad, feed_grad, embed_grad, gain_grad, bias_grad = encoder_backward(
                enc_kept, back_final, gains, enc_bias, enc_onehot, weights_low, feed_low, count
            )
            return (
                jnp.concatenate([attention_grad, cross_part], 1),
                feed_grad,
                embed_grad,
                gain_grad,
                bias_grad,
                jnp.zeros((), jnp.float32),
            )

        def memory_back(back_memory):
            return encoder_grads(
                product_back(back_memory, weights_low[:, 4 * width :]),
                product_outer(final_low, back_memory),
            )

        arrived = shifted(encoded, "pipe", 1)

        def decode():
            query_low, front_kept = decoder_front(goal, embedding, gains, dec_bias, weights_low)
            answer, answer_total = cross_forward(query_low, arrived, count)
            back_output, back_second, partial_value = decoder_rest(
                front_kept, answer, goal, weight, table, gains, weights_low, feed_low
            )
            back_query, back_memory = cross_backward(
                query_low, arrived, answer_total, back_output, count
            )
            decoded = decoder_finish(
                front_kept,
                back_second,
                back_query,
                partial_value,
                gains,
                dec_bias,
                dec_onehot,
                weights_low,
                count,
            )
            cross_grad = jnp.zeros(cross_shape, jnp.float32)
            return (back_memory, decoded, cross_grad)

        def skip_decode():
            return (
                jnp.zeros((rows, sent_width), back_type),
                blank(),
                jnp.zeros(cross_shape, jnp.float32),
            )

        returned, decoded, cross_grad = lax.cond(section == 1, decode, skip_decode)
        back = shifted(returned, "pipe", -1)

        def encode_back():
            return memory_back(back)

        encoded_grads = lax.cond(section == 0, encode_back, blank)
        totals = jax.tree.map(
            lambda left, right, more: left + right + more, totals, decoded, encoded_grads
        )
    mixer_grad, feed_grad, embed_grad, gain_grad, bias_grad, loss_part = totals
    embed_grad, gain_grad, bias_grad, loss = lax.psum(
        (embed_grad, gain_grad, bias_grad, loss_part), ("pipe", "dp")
    )
    small_squares = (
        jnp.sum(embed_grad * embed_grad)
        + jnp.sum(gain_grad * gain_grad)
        + jnp.sum(bias_grad * bias_grad)
    )
    mixer_grad, feed_grad = lax.psum((mixer_grad, feed_grad), "dp")
    own_squares = jnp.sum(mixer_grad * mixer_grad) + jnp.sum(feed_grad * feed_grad)
    section_squares = lax.all_gather(own_squares[None], "pipe", axis=0, tiled=True)
    section_norms = jnp.sqrt(section_squares)
    gradient_norm = jnp.sqrt(jnp.sum(section_squares) + small_squares)
    factor = jnp.minimum(1.0, clip_norm / (gradient_norm + 1e-06))
    new_mixer, new_mixer_moment, new_mixer_square = adam_step(
        mixer[0], mixer_moment[0], mixer_square[0], factor * mixer_grad, rate_matrix, decay_matrix
    )
    new_feed, new_feed_moment, new_feed_square = adam_step(
        feed[0], feed_moment[0], feed_square[0], factor * feed_grad, rate_matrix, decay_matrix
    )
    new_embedding, new_embedding_moment, new_embedding_square = adam_step(
        embedding,
        embedding_moment,
        embedding_square,
        factor * embed_grad,
        rate_matrix,
        decay_matrix,
    )
    new_gains, new_gains_moment, new_gains_square = adam_step(
        gains, gains_moment, gains_square, factor * gain_grad, rate_gain, 0.0
    )
    new_bias, new_bias_moment, new_bias_square = adam_step(
        position_bias, bias_moment, bias_square, factor * bias_grad, rate_small, 0.0
    )
    return (
        loss,
        gradient_norm,
        section_norms,
        histograms,
        new_mixer[None],
        new_mixer_moment[None],
        new_mixer_square[None],
        new_feed[None],
        new_feed_moment[None],
        new_feed_square[None],
        new_embedding,
        new_embedding_moment,
        new_embedding_square,
        new_gains,
        new_gains_moment,
        new_gains_square,
        new_bias,
        new_bias_moment,
        new_bias_square,
        new_mixer[None].astype(jnp.bfloat16),
        new_feed[None].astype(jnp.bfloat16),
        new_embedding.astype(jnp.bfloat16),
    )


def solution(mesh):
    return jax.shard_map(
        shards,
        mesh=mesh,
        in_specs=(
            P("dp", None),
            P("dp"),
            P("dp", None),
            P("dp"),
            P("pipe", None, None),
            P("pipe", None, None),
            P("pipe", None, None),
            P("pipe", None, None),
            P("pipe", None, None),
            P("pipe", None, None),
            P(),
            P(),
            P(),
            P(),
            P(),
            P(),
            P(),
            P(),
            P(),
        ),
        out_specs=(
            P(),
            P(),
            P(),
            P(),
            P("pipe", None, None),
            P("pipe", None, None),
            P("pipe", None, None),
            P("pipe", None, None),
            P("pipe", None, None),
            P("pipe", None, None),
            P(),
            P(),
            P(),
            P(),
            P(),
            P(),
            P(),
            P(),
            P(),
            P("pipe", None, None),
            P("pipe", None, None),
            P(),
        ),
        check_vma=False,
    )
```

profile of v0, /device:TPU:0, one launch (start us, length us, event | category | flops | bytes accessed | tf_op | source)
XLA Modules:
  0.0 1066.3 jit_solution(12608064701757978507)
XLA Ops:
  10.2 59.0 %conditional.21 = (bf16[1296,768]{1,0:T(8,128)(2,1)}, bf16[1296,128]{1,0:T(8,128)(2,1)}, s32[1296]{0:T(1024)S(1)}, f32[1296,128]{1,0:T(8,128)}, f32[1296,1]{0,1:...) conditional(s32[]{:T(128)} %convert_element_type.813, ...), branch_computations={%region_135.136_spmd, %region_136.0_spmd} | conditional | flops 1620564992 | bytes 81033528 | solution.py:528
  71.9 58.4 %conditional.18 = (bf16[1296,768]{1,0:T(8,128)(2,1)}, bf16[1296,128]{1,0:T(8,128)(2,1)}, s32[1296]{0:T(1024)S(1)}, f32[1296,128]{1,0:T(8,128)}, f32[1296,1]{0,1:...) conditional(s32[]{:T(128)} %convert_element_type.813, ...), branch_computations={%region_91.92_spmd, %region_92.0_spmd} | conditional | flops 1620564992 | bytes 81033528 | solution.py:528
  133.0 58.7 %conditional.15 = (bf16[1296,768]{1,0:T(8,128)(2,1)}, bf16[1296,128]{1,0:T(8,128)(2,1)}, s32[1296]{0:T(1024)S(1)}, f32[1296,128]{1,0:T(8,128)}, f32[1296,1]{0,1:...) conditional(s32[]{:T(128)} %convert_element_type.813, ...), branch_computations={%region_47.48_spmd, %region_48.0_spmd} | conditional | flops 1620564992 | bytes 81033528 | solution.py:528
  160.4 5.4 reshape.1745
  194.4 65.2 %conditional.12 = (bf16[1296,768]{1,0:T(8,128)(2,1)}, bf16[1296,128]{1,0:T(8,128)(2,1)}, s32[1296]{0:T(1024)S(1)}, f32[1296,128]{1,0:T(8,128)}, f32[1296,1]{0,1:...) conditional(s32[]{:T(128)} %convert_element_type.813, ...), branch_computations={%region_0.0_spmd, %region_1.7_spmd} | conditional | flops 1620564992 | bytes 63781056 | solution.py:528
  262.5 36.0 %all-reduce.14 = (f32[3]{0:T(128)S(1)}, f32[4,256]{1,0:T(4,128)}) all-reduce(f32[3]{0:T(128)S(1)} %broadcast_multiply_fusion.28, f32[4,256]{1,0:T(4,128)S(1)} %convert_reduce_fusion.8), channel_id=1, replica_groups=mesh['pipe'=2,'dp'=16] {'dp'}, use_global_device_ids=true, to_apply=%region_8.9 | all-reduce | flops 1027 | bytes 8216 | tf_op jit(solution)/shard_map/psum | solution.py:487
  301.0 11.3 %conditional.22 = (bf16[1296,768]{0,1:T(8,128)(2,1)}, f32[128,2304]{1,0:T(8,128)}, f32[128,2048]{1,0:T(8,128)}, f32[3024,128]{1,0:T(8,128)}, f32[7,128]{1,0:T(8,128)}, /*index=5*/f32[]{:T(128)}, f32[2,32,6]{1,0,2:T(2,128)}) conditional(s32[]{:T(128)} %convert_element_type.811, () %tuple.148, (s32[64,4]{1,0:T(8,128)S(1)}, ...), branch_computations={%region_142.143_spmd, %region_143.168_spmd} | conditional | flops 299333440 | bytes 62007940 | solution.py:581
  317.9 11.6 %conditional.19 = (bf16[1296,768]{0,1:T(8,128)(2,1)}, f32[128,2304]{1,0:T(8,128)}, f32[128,2048]{1,0:T(8,128)}, f32[3024,128]{1,0:T(8,128)}, f32[7,128]{1,0:T(8,128)}, /*index=5*/f32[]{:T(128)}, f32[2,32,6]{1,0,2:T(2,128)}) conditional(s32[]{:T(128)} %convert_element_type.811, () %tuple.143, (s32[64,4]{1,0:T(8,128)S(1)}, ...), branch_computations={%region_98.99_spmd, %region_99.124_spmd} | conditional | flops 299333440 | bytes 62007940 | solution.py:581
  334.9 11.3 %conditional.16 = (bf16[1296,768]{0,1:T(8,128)(2,1)}, f32[128,2304]{1,0:T(8,128)}, f32[128,2048]{1,0:T(8,128)}, f32[3024,128]{1,0:T(8,128)}, f32[7,128]{1,0:T(8,128)}, /*index=5*/f32[]{:T(128)}, f32[2,32,6]{1,0,2:T(2,128)}) conditional(s32[]{:T(128)} %convert_element_type.811, () %tuple.138, (s32[64,4]{1,0:T(8,128)S(1)}, ...), branch_computations={%region_54.55_spmd, %region_55.80_spmd} | conditional | flops 299333440 | bytes 62007940 | solution.py:581
  351.7 11.8 %conditional.13 = (bf16[1296,768]{0,1:T(8,128)(2,1)}, f32[128,2304]{1,0:T(8,128)S(1)}, f32[128,2048]{1,0:T(8,128)}, f32[3024,128]{1,0:T(8,128)}, f32[7,128]{1,0:T(8,128)}, /*index=5*/f32[]{:T(128)}, f32[2,32,6]{1,0,2:T(2,128)}) conditional(s32[]{:T(128)} %convert_element_type.811, () %tuple.132, (s32[64,4]{1,0:T(8,128)S(1)}, ...), branch_computations={%region_10.11_spmd, %region_11.36_spmd} | conditional | flops 299333440 | bytes 58961188 | solution.py:581
  374.1 98.9 %conditional.23 = (f32[3024,128]{1,0:T(8,128)}, f32[7,128]{1,0:T(8,128)S(1)}, f32[]{:T(128)}, f32[128,2304]{1,0:T(8,128)}, f32[128,2048]{1,0:T(8,128)}, /*index=5*/f32[2,32,6]{1,0,2:T(2,128)S(1)}) conditional(s32[]{:T(128)} %convert_element_type.813, () %tuple.151, (bf16[16,81,6,64]{1,0,3,2:T(8,128)(2,1)}, bf16[16,81,6,64]{1,0,3,2:T(8,128)(2,1)}, ...), branch_computations={%region_168.169_spmd, %region_169.179_spmd} | conditional | flops 3331120128 | bytes 185826384 | solution.py:587
  461.3 11.4 %scatter_custom_fusion.7 = f32[3024,128]{1,0:T(8,128)} fusion(s32[1296]{0:T(1024)} %get-tuple-element.632, f32[]{:T(128)} %copy.1933, f32[1296,128]{1,0:T(8,128)} %copy-done.42, f32[1296,128]{1,0:T(8,128)} %get-tuple-element.2034, f32[1296,128]{1,0:T(8,128)S(1)} %copy-done.30, f32[1296]{0:T(1024)S(1)} %broadcast_multiply_fusion.25, ...), kind=kCustom, calls=%fused_computation.1124 | custom fusion | flops 1161216 | bytes 3550336 | tf_op jit(solution)/shard_map/cond/branch_1_fun/scatter-add | solution.py:311
  473.0 7.2 collective-permute-done.5
  480.2 98.9 %conditional.20 = (f32[3024,128]{1,0:T(8,128)}, f32[7,128]{1,0:T(8,128)S(1)}, f32[]{:T(128)}, f32[128,2304]{1,0:T(8,128)}, f32[128,2048]{1,0:T(8,128)}, /*index=5*/f32[2,32,6]{1,0,2:T(2,128)S(1)}) conditional(s32[]{:T(128)} %convert_element_type.813, () %tuple.146, (bf16[16,81,6,64]{1,0,3,2:T(8,128)(2,1)}, bf16[16,81,6,64]{1,0,3,2:T(8,128)(2,1)}, ...), branch_computations={%region_124.125_spmd, %region_125.135_spmd} | conditional | flops 3331120128 | bytes 185826384 | solution.py:587
  567.5 11.4 %scatter_custom_fusion.5 = f32[3024,128]{1,0:T(8,128)} fusion(s32[1296]{0:T(1024)} %get-tuple-element.592, f32[]{:T(128)} %copy.1930, f32[1296,128]{1,0:T(8,128)} %copy-done.43, f32[1296,128]{1,0:T(8,128)} %get-tuple-element.2026, f32[1296,128]{1,0:T(8,128)S(1)} %copy-done.31, f32[1296]{0:T(1024)S(1)} %broadcast_multiply_fusion.22, ...), kind=kCustom, calls=%fused_computation.1051 | custom fusion | flops 1161216 | bytes 3550336 | tf_op jit(solution)/shard_map/cond/branch_1_fun/scatter-add | solution.py:311
  579.1 21.1 %collective-permute-done.3 = bf16[1296,768]{1,0:T(8,128)(2,1)} collective-permute-done((bf16[1296,768]{1,0:T(8,128)(2,1)}, bf16[1296,768]{1,0:T(8,128)(2,1)}, u32[]{:S(2)}, u32[]{:S(2)}) %collective-permute-start.3) | collective-permute-done | bytes 1990688 | tf_op jit(solution)/shard_map/ppermute | solution.py:36
  600.3 99.9 %conditional.17 = (f32[3024,128]{1,0:T(8,128)}, f32[7,128]{1,0:T(8,128)S(1)}, f32[]{:T(128)}, f32[128,2304]{1,0:T(8,128)}, f32[128,2048]{1,0:T(8,128)}, /*index=5*/f32[2,32,6]{1,0,2:T(2,128)S(1)}) conditional(s32[]{:T(128)} %convert_element_type.813, () %tuple.141, (bf16[16,81,6,64]{1,0,3,2:T(8,128)(2,1)}, bf16[16,81,6,64]{1,0,3,2:T(8,128)(2,1)}, ...), branch_computations={%region_80.81_spmd, %region_81.91_spmd} | conditional | flops 3331120128 | bytes 185828592 | solution.py:587
  688.6 11.3 %scatter_custom_fusion.3 = f32[3024,128]{1,0:T(8,128)} fusion(s32[1296]{0:T(1024)} %get-tuple-element.552, f32[]{:T(128)} %copy.1927, f32[1296,128]{1,0:T(8,128)} %copy-done.44, f32[1296,128]{1,0:T(8,128)} %get-tuple-element.2018, f32[1296,128]{1,0:T(8,128)S(1)} %copy-done.32, f32[1296]{0:T(1024)S(1)} %broadcast_multiply_fusion.19, ...), kind=kCustom, calls=%fused_computation.978 | custom fusion | flops 1161216 | bytes 3550336 | tf_op jit(solution)/shard_map/cond/branch_1_fun/scatter-add | solution.py:311
  700.7 93.1 %conditional.14 = (f32[3024,128]{1,0:T(8,128)S(1)}, f32[7,128]{1,0:T(8,128)S(1)}, f32[]{:T(128)}, f32[128,2304]{1,0:T(8,128)}, f32[128,2048]{1,0:T(8,128)S(1)}, /*index=5*/f32[2,32,6]{1,0,2:T(2,128)S(1)}) conditional(s32[]{:T(128)} %convert_element_type.813, () %tuple.136, (bf16[16,81,6,64]{1,0,3,2:T(8,128)(2,1)}, ...), branch_computations={%region_36.37_spmd, %region_37.47_spmd} | conditional | flops 3331120128 | bytes 153495536 | solution.py:587
  783.0 10.5 scatter_custom_fusion.1
  793.8 5.8 add_add_fusion
  813.8 37.1 %all-reduce.13 = (f32[]{:T(128)}, f32[7,128]{1,0:T(8,128)S(1)}, f32[2,32,6]{1,0,2:T(2,128)S(1)}) all-reduce(f32[]{:T(128)S(6)} %add.1350, f32[7,128]{1,0:T(8,128)S(1)} %add_add_fusion.4, f32[2,32,6]{1,0,2:T(2,128)S(1)} %add_add_fusion.3), channel_id=1, replica_groups=mesh['pipe'=2,'dp'=16] {'pipe','dp'}, use_global_device_ids=true, to_apply=%region_179.180 | all-reduce | flops 1281 | bytes 10248 | tf_op jit(solution)/shard_map/psum | solution.py:592
  852.1 77.0 %all-reduce.19.cloned.1.call-done = f32[3024,128]{1,0:T(8,128)} async-done(((f32[3024,128]{1,0:T(8,128)}), f32[3024,128]{1,0:T(8,128)}) %all-reduce.19.cloned.1.call-update) | async-done | bytes 1548304 | tf_op jit(solution)/shard_map/psum | solution.py:592
  932.7 98.3 %all-reduce.21.cloned.1.call-done = (f32[128,2304]{1,0:T(8,128)}, f32[128,2048]{1,0:T(8,128)}) async-done(((f32[128,2304]{1,0:T(8,128)}, f32[128,2048]{1,0:T(8,128)}), (f32[128,2304]{1,0:T(8,128)}, f32[128,2048]{1,0:T(8,128)})) %all-reduce.21.cloned.1.call-update) | async-done | bytes 2228240 | tf_op jit(solution)/shard_map/psum | solution.py:600
  (792 shorter events, 686.7 us)
Async XLA Ops:
  7.2 921.8 %all-reduce.19.cloned.1.call-start = ((), (), s32[]{:S(2)}) async-start(), calls=%async_computation | async-start | bytes 3096576 | tf_op jit(solution)/shard_map/psum | solution.py:592
  69.3 231.2 %collective-permute-start.6 = (bf16[1296,768]{1,0:T(8,128)(2,1)}, bf16[1296,768]{1,0:T(8,128)(2,1)}, u32[]{:S(2)}, u32[]{:S(2)}) collective-permute-start(bf16[1296,768]{1,0:T(8,128)(2,1)} %get-tuple-element.845), channel_id=1, source_target_pairs={{0,16},{1,17},{2,18},{3,19},{4,20},{5,21},{6,22},{7,23},{8,24},{9,... | collective-permute-start | bytes 5971976 | tf_op jit(solution)/shard_map/ppermute | solution.py:36
  130.4 187.4 %collective-permute-start.4 = (bf16[1296,768]{1,0:T(8,128)(2,1)}, bf16[1296,768]{1,0:T(8,128)(2,1)}, u32[]{:S(2)}, u32[]{:S(2)}) collective-permute-start(bf16[1296,768]{1,0:T(8,128)(2,1)} %get-tuple-element.824), channel_id=1, source_target_pairs={{0,16},{1,17},{2,18},{3,19},{4,20},{5,21},{6,22},{7,23},{8,24},{9,... | collective-permute-start | bytes 5971976 | tf_op jit(solution)/shard_map/ppermute | solution.py:36
  191.7 143.1 %collective-permute-start.2 = (bf16[1296,768]{1,0:T(8,128)(2,1)}, bf16[1296,768]{1,0:T(8,128)(2,1)}, u32[]{:S(2)}, u32[]{:S(2)}) collective-permute-start(bf16[1296,768]{1,0:T(8,128)(2,1)} %get-tuple-element.803), channel_id=1, source_target_pairs={{0,16},{1,17},{2,18},{3,19},{4,20},{5,21},{6,22},{7,23},{8,24},{9,... | collective-permute-start | bytes 5971976 | tf_op jit(solution)/shard_map/ppermute | solution.py:36
  259.7 92.0 %collective-permute-start = (bf16[1296,768]{1,0:T(8,128)(2,1)}, bf16[1296,768]{1,0:T(8,128)(2,1)}, u32[]{:S(2)}, u32[]{:S(2)}) collective-permute-start(bf16[1296,768]{1,0:T(8,128)(2,1)} %get-tuple-element.782), channel_id=1, source_target_pairs={{0,16},{1,17},{2,18},{3,19},{4,20},{5,21},{6,22},{7,23},{8,24},{9,... | collective-permute-start | bytes 5971976 | tf_op jit(solution)/shard_map/ppermute | solution.py:36
  316.5 57.4 %collective-permute-start.7 = (bf16[1296,768]{1,0:T(8,128)(2,1)}, bf16[1296,768]{1,0:T(8,128)(2,1)}, u32[]{:S(2)}, u32[]{:S(2)}) collective-permute-start(bf16[1296,768]{1,0:T(8,128)(2,1)} %copy.1178), channel_id=1, source_target_pairs={{16,0},{17,1},{18,2},{19,3},{20,4},{21,5},{22,6},{23,7},{24,8},{25... | collective-permute-start | bytes 5971976 | tf_op jit(solution)/shard_map/ppermute | solution.py:36
  333.6 146.5 %collective-permute-start.5 = (bf16[1296,768]{1,0:T(8,128)(2,1)}, bf16[1296,768]{1,0:T(8,128)(2,1)}, u32[]{:S(2)}, u32[]{:S(2)}) collective-permute-start(bf16[1296,768]{1,0:T(8,128)(2,1)} %copy.1169), channel_id=1, source_target_pairs={{16,0},{17,1},{18,2},{19,3},{20,4},{21,5},{22,6},{23,7},{24,8},{25... | collective-permute-start | bytes 5971976 | tf_op jit(solution)/shard_map/ppermute | solution.py:36
  350.4 249.8 %collective-permute-start.3 = (bf16[1296,768]{1,0:T(8,128)(2,1)}, bf16[1296,768]{1,0:T(8,128)(2,1)}, u32[]{:S(2)}, u32[]{:S(2)}) collective-permute-start(bf16[1296,768]{1,0:T(8,128)(2,1)} %copy.1160), channel_id=1, source_target_pairs={{16,0},{17,1},{18,2},{19,3},{20,4},{21,5},{22,6},{23,7},{24,8},{25... | collective-permute-start | bytes 5971976 | tf_op jit(solution)/shard_map/ppermute | solution.py:36
  368.0 332.1 %collective-permute-start.1 = (bf16[1296,768]{1,0:T(8,128)(2,1)}, bf16[1296,768]{1,0:T(8,128)(2,1)}, u32[]{:S(2)}, u32[]{:S(2)}) collective-permute-start(bf16[1296,768]{1,0:T(8,128)(2,1)} %copy.1151), channel_id=1, source_target_pairs={{16,0},{17,1},{18,2},{19,3},{20,4},{21,5},{22,6},{23,7},{24,8},{25... | collective-permute-start | bytes 5971976 | tf_op jit(solution)/shard_map/ppermute | solution.py:36
  374.0 106.1 %copy-start.15 = (f32[1296,128]{1,0:T(8,128)S(1)}, f32[1296,128]{1,0:T(8,128)}, u32[]{:S(2)}) copy-start(f32[1296,128]{1,0:T(8,128)} %get-tuple-element.834) | copy-start | bytes 1990660
  374.0 106.1 %copy-start.96 = (f32[16,6,81]{2,1,0:T(8,128)S(1)}, f32[16,6,81]{2,1,0:T(8,128)}, u32[]{:S(2)}) copy-start(f32[16,6,81]{2,1,0:T(8,128)} %get-tuple-element.828) | copy-start | bytes 93316
  374.0 106.1 %copy-start.208 = (f32[1296,1]{0,1:T(1,128)S(1)}, f32[1296,1]{0,1:T(1,128)}, u32[]{:S(2)}) copy-start(f32[1296,1]{0,1:T(1,128)} %copy-done.207) | copy-start | bytes 15556
  480.2 120.0 %copy-start.17 = (f32[1296,128]{1,0:T(8,128)S(1)}, f32[1296,128]{1,0:T(8,128)}, u32[]{:S(2)}) copy-start(f32[1296,128]{1,0:T(8,128)} %get-tuple-element.813) | copy-start | bytes 1990660
  480.2 120.0 %copy-start.98 = (f32[16,6,81]{2,1,0:T(8,128)S(1)}, f32[16,6,81]{2,1,0:T(8,128)}, u32[]{:S(2)}) copy-start(f32[16,6,81]{2,1,0:T(8,128)} %get-tuple-element.807) | copy-start | bytes 93316
  480.2 120.0 %copy-start.214 = (f32[1296,1]{0,1:T(1,128)S(1)}, f32[1296,1]{0,1:T(1,128)}, u32[]{:S(2)}) copy-start(f32[1296,1]{0,1:T(1,128)} %copy-done.213) | copy-start | bytes 15556
  480.2 120.0 %copy-start.216 = (f32[1296,1]{0,1:T(1,128)S(1)}, f32[1296,1]{0,1:T(1,128)}, u32[]{:S(2)}) copy-start(f32[1296,1]{0,1:T(1,128)} %copy-done.215) | copy-start | bytes 15556
  480.2 120.0 %copy-start.218 = (f32[1296,1]{0,1:T(1,128)S(1)}, f32[1296,1]{0,1:T(1,128)}, u32[]{:S(2)}) copy-start(f32[1296,1]{0,1:T(1,128)} %copy-done.217) | copy-start | bytes 15556
  799.7 231.3 %all-reduce.21.cloned.1.call-start = ((), (), s32[]{:S(2)}) async-start(), calls=%async_computation.1 | async-start | bytes 4456448 | tf_op jit(solution)/shard_map/psum | solution.py:600
  852.0 192.8 %copy-start.310 = (f32[7,128]{1,0:T(8,128)S(1)}, f32[7,128]{1,0:T(8,128)}, u32[]{:S(2)}) copy-start(f32[7,128]{1,0:T(8,128)} %param.65) | copy-start | bytes 10756
  852.0 192.8 %copy-start.311 = (f32[7,128]{1,0:T(8,128)S(1)}, f32[7,128]{1,0:T(8,128)}, u32[]{:S(2)}) copy-start(f32[7,128]{1,0:T(8,128)} %param.66) | copy-start | bytes 10756
  852.0 193.5 %copy-start.200 = (f32[2,32,6]{1,0,2:T(2,128)S(1)}, f32[2,32,6]{1,0,2:T(2,128)}, u32[]{:S(2)}) copy-start(f32[2,32,6]{1,0,2:T(2,128)} %param.67) | copy-start | bytes 4612
  852.0 193.5 %copy-start.292 = (f32[2,32,6]{1,0,2:T(2,128)S(1)}, f32[2,32,6]{1,0,2:T(2,128)}, u32[]{:S(2)}) copy-start(f32[2,32,6]{1,0,2:T(2,128)} %param.68) | copy-start | bytes 4612
  852.0 193.5 %copy-start.293 = (f32[2,32,6]{1,0,2:T(2,128)S(1)}, f32[2,32,6]{1,0,2:T(2,128)}, u32[]{:S(2)}) copy-start(f32[2,32,6]{1,0,2:T(2,128)} %param.69) | copy-start | bytes 4612
  852.0 194.1 %copy-start.63 = (f32[1,128,2048]{2,1,0:T(8,128)S(1)}, f32[1,128,2048]{2,1,0:T(8,128)}, u32[]{:S(2)}) copy-start(f32[1,128,2048]{2,1,0:T(8,128)} %param.58) | copy-start | bytes 3145732
  (156 other events, 1528.2 us)
Sparse Core Ops, SparseCore 0:
  799.8 129.1 all-reduce.18
  933.2 97.7 all-reduce.20
where the time goes:
time: 1080 us; the launch traced here: 1070 us
  local copies, waits for them, and re-layouts  337 us (31%)
  matrix products  234 us (22%)
  waiting for transfers between devices  204 us (19%)
  other arithmetic  151 us (14%)
  blocking collectives  78 us (7%)
  loops' own time  26.7 us (2%)
  between operations  20.7 us (2%)
  starting transfers between devices  15.6 us (1%)
    psum x1, waiting for transfers between devices, shards(): mixer_grad, feed_grad = lax.psum((mixer_grad, feed_grad), 'dp')  98.3 us
    reshape x20, local copies, waits for them, and re-layouts, split_heads(): return table.reshape(count, -1, HEADS, HEAD_DIM)  93.9 us
    psum x1, waiting for transfers between devices, shards(): lax.psum((embed_grad, gain_grad, bias_grad, loss_part), ('pipe', 'dp'))  77 us
    dot_general x20, matrix products, product(): return jnp.dot(left, right, preferred_element_type=jnp.float32)  50.3 us
    scatter-add x4, other arithmetic, encoder_backward(): embed_grad = jax.ops.segment_sum(back_start, token_ids, VOCAB)  44.7 us
    dot_general x20, matrix products, product_back(): lax.dot_general(left, right, (((1,), (1,)), ((), ())), preferred_element_...  43.4 us
    psum x1, blocking collectives, shards(): lax.psum((embed_grad, gain_grad, bias_grad, loss_part), ('pipe', 'dp'))  37.1 us
    psum x1, blocking collectives, shards(): counts, histograms = lax.psum((local_counts, local_histograms), 'dp')  36 us
  transfers between devices with their start and end apart: 10, of which 4 were waited for; matrix products, arithmetic and copies ran while one was open for 50% of the time, Pallas kernels for 0%

commit v1 on v0

v1 whole, which is shorter than its diff:
```python
import functools

import jax
import jax.numpy as jnp
from jax import lax
from jax.experimental import pallas as pl
from jax.experimental.pallas import tpu as pltpu
from jax.sharding import PartitionSpec as P

D = 128
HEADS = 6
HEAD_DIM = 64
FF = 1024
CODEBOOK = 256
LEVELS = 4
BUCKETS = 32
DOMAINS = 3
HIST_LEN = 81
STEP = 5
CODES = 1024
LANES = 128
WIDTH = HEADS * HEAD_DIM
MIXW = 6 * WIDTH
COLS = MIXW + 2 * FF
BLOCKS = COLS // LANES
KEYS = 96
PAIRS = HEADS // 2
ROWS = 32

norm_eps = 1e-06
beta_one = 0.9
beta_two = 0.999
adam_eps = 1e-08
clip_norm = 0.5
rate_matrix = 0.04
rate_gain = 0.8
rate_small = 0.3
decay_matrix = 0.01

f32 = jnp.float32
bf16 = jnp.bfloat16


def iota(shape, axis):
    return lax.broadcasted_iota(jnp.int32, shape, axis)


def mul(left, right):
    return jnp.dot(left, right, preferred_element_type=f32)


def mul_t(left, right):
    return lax.dot_general(left, right, (((1,), (1,)), ((), ())), preferred_element_type=f32)


def mul_exact(left, right):
    return jnp.dot(left, right, preferred_element_type=f32, precision=lax.Precision.HIGHEST)


def onehot(ids, rows):
    return jnp.where(iota((rows, ids.shape[1]), 0) == ids, 1.0, 0.0).astype(bf16)


def inverse_rms(x):
    return lax.rsqrt(jnp.mean(x * x, axis=0, keepdims=True) + norm_eps)


def norm_low(x, inverse, gain):
    return (x * inverse * gain).astype(bf16)


def norm_back(x, inverse, gain, upstream):
    scaled = x * inverse
    inner = upstream * gain
    back = inverse * (inner - scaled * jnp.mean(inner * scaled, axis=0, keepdims=True))
    return back, upstream * scaled


def block_diag(pair):
    zero = jnp.zeros((HEAD_DIM, LANES), pair.dtype)
    left = jnp.concatenate([pair[:HEAD_DIM], zero], 0)
    right = jnp.concatenate([zero, pair[HEAD_DIM:]], 0)
    return jnp.concatenate([left, right], 1)


def diagonal(both):
    return jnp.concatenate([both[:HEAD_DIM, :LANES], both[HEAD_DIM:, LANES:]], 0)


def pad_keys(table):
    if table.shape[0] == LANES:
        return table
    zero = jnp.zeros((LANES - table.shape[0], table.shape[1]), table.dtype)
    return jnp.concatenate([table, zero], 0)


def attend(keys, query, values, bias):
    scores = mul(keys, block_diag(query)) + bias
    top = jnp.max(scores, axis=0, keepdims=True)
    chance = jnp.exp(scores - top)
    total = jnp.sum(chance, axis=0, keepdims=True)
    chance = (chance * (1.0 / total)).astype(bf16)
    mixed = diagonal(mul(values, pad_keys(chance))).astype(bf16)
    return chance, mixed


def attend_back(keys_t, query, values, back_mixed, chance):
    exact = chance.astype(f32)
    spread = block_diag(back_mixed)
    back_chance = mul(values, spread)
    inner = jnp.sum(back_chance * exact, axis=0, keepdims=True)
    back_scores = exact * (back_chance - inner)
    low = pad_keys(back_scores.astype(bf16))
    back_query = diagonal(mul(keys_t, low)).astype(bf16)
    back_keys = mul_t(block_diag(query), low).astype(bf16)
    back_values = mul_t(spread, pad_keys(chance)).astype(bf16)
    return back_query, back_keys, back_values, back_scores


def add_blocks(ref, first, value):
    for block in range(value.shape[1] // LANES):
        ref[first + block] += value[:, block * LANES : (block + 1) * LANES]


def put_blocks(ref, first, value):
    for block in range(value.shape[1] // LANES):
        rows = slice((first + block) * D, (first + block + 1) * D)
        ref[1, rows, :] = value[:, block * LANES : (block + 1) * LANES].astype(ref.dtype)


def split_low(x):
    high = x.astype(bf16)
    return jnp.concatenate([high, (x - high.astype(f32)).astype(bf16)], 0)


def compute_kernel(
    n,
    users_ref,
    bias_ref,
    ids_ref,
    start_ref,
    goal_ref,
    domain_ref,
    count_ref,
    gains_ref,
    embed_ref,
    wn_s,
    grad_ref,
    grad_embed_ref,
    grad_user_ref,
    small_ref,
    x0_s,
    x1_s,
    x2_s,
    qkv_s,
    p_s,
    o_s,
    r_s,
    mem_s,
    dz_s,
    wt_s,
    ext_s,
    table_s,
    gain_s,
    ebias_s,
    dbias_s,
    g0_s,
    ge_s,
    gbias_s,
    ggain_s,
    rows_s,
    user_s,
    qbd_s,
    qbdt_s,
    dobd_s,
    dobdt_s,
    pc_s,
    oc_s,
):
    chunks = n // 2
    groups = n // 4
    wide = 2 * LANES
    eye = jnp.where(iota((LANES, LANES), 0) == iota((LANES, LANES), 1), 1.0, 0.0).astype(bf16)

    for section in range(2):
        for block in range(BLOCKS):
            place = slice(block * LANES, (block + 1) * LANES)
            wt_s[section, place, :] = mul_t(eye, wn_s[section, :, place]).astype(bf16)

    def fetch(i, carry):
        user_s[pl.ds(i, 1), :] = embed_ref[pl.ds(CODES + users_ref[i], 1), :]
        return carry

    lax.fori_loop(0, n, fetch, 0)
    for block in range(CODES // LANES + 1):
        if block < CODES // LANES:
            rows = embed_ref[block * LANES : (block + 1) * LANES, :]
            table_s[block * LANES : (block + 1) * LANES, :] = rows.astype(bf16)
            span = LANES
        else:
            rows = user_s[...]
            span = n
        high = rows.astype(bf16)
        rest = (rows - high.astype(f32)).astype(bf16)
        place = slice(block * LANES, block * LANES + span)
        ext_s[:D, place] = mul_t(eye, high).astype(bf16)
        ext_s[D:, place] = mul_t(eye, rest).astype(bf16)

    for g in range(7):
        gain_s[g] = jnp.broadcast_to(gains_ref[g : g + 1, :], (LANES, LANES)).T

    key, query = iota((KEYS, LANES), 0), iota((KEYS, LANES), 1)
    distance = jnp.abs(query - key)
    remote = jnp.zeros_like(distance)
    for edge in (12, 16, 23, 32, 46, 64, 91):
        remote = remote + (distance >= edge).astype(jnp.int32)
    nearby = jnp.minimum(jnp.where(distance < 8, distance, 8 + remote), 15)
    buckets = nearby + jnp.where(key > query, 16, 0)
    for head in range(HEADS):
        lanes = slice((head % 2) * LANES, (head % 2 + 1) * LANES)

        def choose(b, table):
            return jnp.where(buckets == b, bias_ref[b, head], table)

        table = lax.fori_loop(0, BUCKETS, choose, jnp.zeros((KEYS, LANES), f32))
        ebias_s[head // 2, :, lanes] = jnp.where(key < HIST_LEN, table, -1e30)
    key, query = iota((LANES, LANES), 0), iota((LANES, LANES), 1)
    offset = query - key
    seen = ((key >> 2) == (query >> 2)) & (offset >= 0)
    for head in range(HEADS):
        lanes = slice((head % 2) * LANES, (head % 2 + 1) * LANES)
        table = jnp.full((LANES, LANES), -1e30, f32)
        for b in range(LEVELS):
            table = jnp.where(seen & (offset == b), bias_ref[BUCKETS + b, head], table)
        dbias_s[head // 2, :, lanes] = table

    def gain(g, width):
        column = gain_s[g]
        return column if width == LANES else jnp.concatenate([column] * (width // LANES), 1)

    def encode(c, carry):
        hot = onehot(ids_ref[c], CODES + n)
        both = mul(ext_s[...], hot)
        x0 = both[:D] + both[D:]
        x0_s[c] = x0
        h = norm_low(x0, inverse_rms(x0), gain(0, wide))
        for j in range(3):
            qkv_s[c, j * WIDTH : (j + 1) * WIDTH, :] = mul(
                wt_s[0, j * WIDTH : (j + 1) * WIDTH, :], h
            ).astype(bf16)
        for i in range(2):
            lanes = slice(i * LANES, (i + 1) * LANES)
            natural = mul_t(eye, h[:, lanes]).astype(bf16)[:KEYS]
            keys = mul(natural, wn_s[0, :, WIDTH : 2 * WIDTH]).astype(bf16)
            for j in range(PAIRS):
                part = slice(j * LANES, (j + 1) * LANES)
                chance, mixed = attend(
                    keys[:, part],
                    qkv_s[c, part, lanes],
                    qkv_s[c, 2 * WIDTH + j * LANES : 2 * WIDTH + (j + 1) * LANES, lanes],
                    ebias_s[j],
                )
                p_s[2 * c + i, j] = chance
                o_s[c, part, lanes] = mixed
        x1 = x0 + mul(wn_s[0, :, 3 * WIDTH : 4 * WIDTH], o_s[c])
        x1_s[c] = x1
        h = norm_low(x1, inverse_rms(x1), gain(1, wide))
        for j in range(2):
            part = slice(j * FF // 2, (j + 1) * FF // 2)
            lifted = mul(wt_s[0, MIXW + j * FF // 2 : MIXW + (j + 1) * FF // 2, :], h)
            r_s[c, part, :] = jnp.maximum(lifted, 0.0).astype(bf16)
        x2 = x1 + mul(wn_s[0, :, MIXW + FF :], r_s[c])
        x2_s[c] = x2
        e = norm_low(x2, inverse_rms(x2), gain(2, wide))
        for j in range(2):
            part = slice(j * WIDTH, (j + 1) * WIDTH)
            mem_s[c, part, :] = mul(
                wt_s[0, 4 * WIDTH + j * WIDTH : 4 * WIDTH + (j + 1) * WIDTH, :], e
            ).astype(bf16)
        return carry

    lax.fori_loop(0, chunks, encode, 0)

    start = onehot(start_ref[...], CODES)
    both = mul(ext_s[:, :CODES], start)
    y0 = both[:D] + both[D:]
    inverse0 = inverse_rms(y0)
    h0 = norm_low(y0, inverse0, gain(3, LANES))
    dz_s[:, :LANES] = mul(wt_s[1, : 3 * WIDTH, :], h0).astype(bf16)
    both = mul(mul_t(eye, h0).astype(bf16), wn_s[1, :, WIDTH : 3 * WIDTH]).astype(bf16)
    self_chance = []
    mixed_parts = []
    for j in range(PAIRS):
        part = slice(j * LANES, (j + 1) * LANES)
        chance, mixed = attend(
            both[:, part],
            dz_s[part, :LANES],
            dz_s[2 * WIDTH + j * LANES : 2 * WIDTH + (j + 1) * LANES, :LANES],
            dbias_s[j],
        )
        self_chance.append(chance)
        mixed_parts.append(mixed)
    self_values = both[:, WIDTH:]
    self_mixed = jnp.concatenate(mixed_parts, 0)
    y1 = y0 + mul(wn_s[1, :, 3 * WIDTH : 4 * WIDTH], self_mixed)
    inverse1 = inverse_rms(y1)
    h1 = norm_low(y1, inverse1, gain(4, LANES))
    cross_query = mul(wt_s[1, 4 * WIDTH : 5 * WIDTH, :], h1).astype(bf16)

    def spread_rows(table, ref, ref_t):
        for g in range(groups):
            shape = (LANES, LANES)
            row, token = g * LANES + iota(shape, 0), iota(shape, 1)
            rep = jnp.where(token == 4 * (row >> 5) + (row & 3), 1.0, 0.0).astype(bf16)
            rows = mul_t(rep, table)
            mask = (iota(rows.shape, 1) >> 6) == ((iota(rows.shape, 0) & 31) >> 2)
            ref[g] = jnp.where(mask, rows, 0.0).astype(bf16)
            token, row = iota(shape, 0), g * LANES + iota(shape, 1)
            rep = jnp.where(token == 4 * (row >> 5) + (row & 3), 1.0, 0.0).astype(bf16)
            rows = mul(table, rep)
            ref_t[g] = jnp.where(head_mask(rows.shape), rows, 0.0).astype(bf16)

    def head_mask(shape):
        return (iota(shape, 0) >> 6) == ((iota(shape, 1) & 31) >> 2)

    def gather_rows(ref):
        total = jnp.zeros((WIDTH, LANES), f32)
        for g in range(groups):
            row, token = g * LANES + iota((LANES, LANES), 0), iota((LANES, LANES), 1)
            rep = jnp.where(token == 4 * (row >> 5) + (row & 3), 1.0, 0.0).astype(bf16)
            total = total + mul(ref[g], rep)
        return total.astype(bf16)

    def blocks_of(table, half):
        owner = iota(table.shape, 0) >> 5
        zero = jnp.zeros_like(table)
        return jnp.concatenate(
            [
                jnp.where(owner == 2 * half, table, zero),
                jnp.where(owner == 2 * half + 1, table, zero),
            ],
            1,
        )

    spread_rows(cross_query, qbd_s, qbdt_s)

    def cross(g, carry):
        parts = []
        for j in range(4):
            parts.append(
                mul(
                    qbd_s[g, 32 * j : 32 * j + 32, :],
                    mem_s[2 * g + j // 2, :WIDTH, (j % 2) * LANES : (j % 2 + 1) * LANES],
                )
            )
        scores = jnp.concatenate(parts, 0)
        scores = jnp.where(iota(scores.shape, 1) < HIST_LEN, scores, -1e30)
        chance = jnp.exp(scores - jnp.max(scores, axis=1, keepdims=True))
        chance = chance * (1.0 / jnp.sum(chance, axis=1, keepdims=True))
        pc_s[g] = chance
        mixed = jnp.zeros((WIDTH, LANES), f32)
        for half in range(2):
            mixed = mixed + mul_t(
                mem_s[2 * g + half, WIDTH:, :], blocks_of(chance, half).astype(bf16)
            )
        oc_s[g] = jnp.where(head_mask(mixed.shape), mixed, 0.0).astype(bf16)
        return carry

    lax.fori_loop(0, groups, cross, 0)
    cross_mixed = gather_rows(oc_s)
    y2 = y1 + mul(wn_s[1, :, 5 * WIDTH : 6 * WIDTH], cross_mixed)
    inverse2 = inverse_rms(y2)
    h2 = norm_low(y2, inverse2, gain(5, LANES))
    lifted = mul(wt_s[1, MIXW : MIXW + FF, :], h2)
    active = jnp.maximum(lifted, 0.0).astype(bf16)
    y3 = y2 + mul(wn_s[1, :, MIXW + FF :], active)
    inverse3 = inverse_rms(y3)
    final = norm_low(y3, inverse3, gain(6, LANES))
    logits = mul(table_s[...], final)
    top = jnp.max(logits, axis=0, keepdims=True)
    log_total = top + jnp.log(jnp.sum(jnp.exp(logits - top), axis=0, keepdims=True))
    goal = goal_ref[...]
    match = iota(logits.shape, 0) == goal
    picked = jnp.sum(jnp.where(match, logits, 0.0), axis=0, keepdims=True)
    weight = jnp.zeros((1, LANES), f32)
    for d in range(DOMAINS):
        share = 1.0 / (DOMAINS * jnp.maximum(count_ref[d : d + 1, :], 1.0))
        weight = weight + jnp.where(domain_ref[...] == d, share, 0.0)
    loss = jnp.sum(weight * (log_total - picked), axis=1, keepdims=True)
    back_logits = (
        weight * (jnp.exp(logits - log_total) - jnp.where(match, 1.0, 0.0))
    ).astype(bf16)
    back_final = mul(ext_s[:D, :CODES], back_logits)
    table_grad = mul_t(back_logits, final)
    back, gain_grad = norm_back(y3, inverse3, gain(6, LANES), back_final)
    ggain_s[6] = gain_grad
    low = back.astype(bf16)
    put_blocks(grad_ref, 26, mul_t(low, active))
    back_lifted = jnp.where(lifted > 0, mul(wt_s[1, MIXW + FF :, :], low), 0.0).astype(bf16)
    put_blocks(grad_ref, 18, mul_t(h2, back_lifted))
    more, gain_grad = norm_back(
        y2, inverse2, gain(5, LANES), mul(wn_s[1, :, MIXW : MIXW + FF], back_lifted)
    )
    ggain_s[5] = gain_grad
    back = back + more
    low = back.astype(bf16)
    put_blocks(grad_ref, 15, mul_t(low, cross_mixed))
    spread_rows(mul(wt_s[1, 5 * WIDTH : 6 * WIDTH, :], low).astype(bf16), dobd_s, dobdt_s)

    def cross_back(g, carry):
        parts = []
        for j in range(4):
            parts.append(
                mul(
                    dobd_s[g, 32 * j : 32 * j + 32, :],
                    mem_s[2 * g + j // 2, WIDTH:, (j % 2) * LANES : (j % 2 + 1) * LANES],
                )
            )
        back_chance = jnp.concatenate(parts, 0)
        chance = pc_s[g]
        inner = jnp.sum(back_chance * chance, axis=1, keepdims=True)
        back_scores = chance * (back_chance - inner)
        total = jnp.zeros((WIDTH, LANES), f32)
        for half in range(2):
            spread = blocks_of(back_scores, half).astype(bf16)
            total = total + mul_t(mem_s[2 * g + half, :WIDTH, :], spread)
            mem_s[2 * g + half, :WIDTH, :] = mul(qbdt_s[g], spread).astype(bf16)
            spread = blocks_of(chance, half).astype(bf16)
            mem_s[2 * g + half, WIDTH:, :] = mul(dobdt_s[g], spread).astype(bf16)
        oc_s[g] = jnp.where(head_mask(total.shape), total, 0.0).astype(bf16)
        return carry

    lax.fori_loop(0, groups, cross_back, 0)
    back_query = gather_rows(oc_s)
    put_blocks(grad_ref, 12, mul_t(h1, back_query) * HEAD_DIM**-0.5)
    more, gain_grad = norm_back(
        y1, inverse1, gain(4, LANES), mul(wn_s[1, :, 4 * WIDTH : 5 * WIDTH], back_query)
    )
    ggain_s[4] = gain_grad
    back = back + more
    low = back.astype(bf16)
    put_blocks(grad_ref, 9, mul_t(low, self_mixed))
    back_mixed = mul(wt_s[1, 3 * WIDTH : 4 * WIDTH, :], low).astype(bf16)
    self_scores = []
    for j in range(PAIRS):
        part = slice(j * LANES, (j + 1) * LANES)
        keys = slice(WIDTH + j * LANES, WIDTH + (j + 1) * LANES)
        values = slice(2 * WIDTH + j * LANES, 2 * WIDTH + (j + 1) * LANES)
        one, two, three, scores = attend_back(
            dz_s[keys, :LANES],
            dz_s[part, :LANES],
            self_values[:, part],
            back_mixed[part],
            self_chance[j],
        )
        dz_s[part, LANES:] = one
        dz_s[keys, LANES:] = two
        dz_s[values, LANES:] = three
        self_scores.append(scores)
    put_blocks(grad_ref, 0, mul_t(h0, dz_s[:WIDTH, LANES:]) * HEAD_DIM**-0.5)
    put_blocks(grad_ref, 3, mul_t(h0, dz_s[WIDTH:, LANES:]))
    more, gain_grad = norm_back(
        y0, inverse0, gain(3, LANES), mul(wn_s[1, :, : 3 * WIDTH], dz_s[:, LANES:])
    )
    ggain_s[3] = gain_grad
    back = back + more
    spread = mul_t(onehot(start_ref[...], CODES), split_low(back))
    ge_s[:CODES, :] = table_grad + spread[:, :D] + spread[:, D:]
    ge_s[CODES:, :] = jnp.zeros((n, D), f32)

    g0_s[...] = jnp.zeros_like(g0_s)
    gbias_s[...] = jnp.zeros_like(gbias_s)
    for g in range(3):
        ggain_s[g] = jnp.zeros((D, LANES), f32)

    def fold(x):
        return x[:, :LANES] + x[:, LANES:]

    def encode_back(c, carry):
        x2 = x2_s[c]
        inverse = inverse_rms(x2)
        back_memory = mem_s[c]
        add_blocks(g0_s, 12, mul_t(norm_low(x2, inverse, gain(2, wide)), back_memory))
        back, gain_grad = norm_back(
            x2, inverse, gain(2, wide), mul(wn_s[0, :, 4 * WIDTH : 6 * WIDTH], back_memory)
        )
        ggain_s[2] += fold(gain_grad)
        low = back.astype(bf16)
        active = r_s[c]
        add_blocks(g0_s, 26, mul_t(low, active))
        back_active = mul(wt_s[0, MIXW + FF :, :], low)
        back_lifted = jnp.where(active.astype(f32) > 0, back_active, 0.0).astype(bf16)
        x1 = x1_s[c]
        inverse = inverse_rms(x1)
        add_blocks(g0_s, 18, mul_t(norm_low(x1, inverse, gain(1, wide)), back_lifted))
        more, gain_grad = norm_back(
            x1, inverse, gain(1, wide), mul(wn_s[0, :, MIXW : MIXW + FF], back_lifted)
        )
        ggain_s[1] += fold(gain_grad)
        back = back + more
        low = back.astype(bf16)
        add_blocks(g0_s, 9, mul_t(low, o_s[c]))
        back_mixed = mul(wt_s[0, 3 * WIDTH : 4 * WIDTH, :], low).astype(bf16)
        for i in range(2):
            lanes = slice(i * LANES, (i + 1) * LANES)
            for j in range(PAIRS):
                part = slice(j * LANES, (j + 1) * LANES)
                keys = slice(WIDTH + j * LANES, WIDTH + (j + 1) * LANES)
                values = slice(2 * WIDTH + j * LANES, 2 * WIDTH + (j + 1) * LANES)
                one, two, three, scores = attend_back(
                    qkv_s[c, keys, lanes],
                    qkv_s[c, part, lanes],
                    mul_t(eye, qkv_s[c, values, lanes]).astype(bf16)[:KEYS],
                    back_mixed[part, lanes],
                    p_s[2 * c + i, j],
                )
                dz_s[part, lanes] = one
                dz_s[keys, lanes] = two
                dz_s[values, lanes] = three
                gbias_s[j] += scores
        x0 = x0_s[c]
        inverse = inverse_rms(x0)
        add_blocks(g0_s, 0, mul_t(norm_low(x0, inverse, gain(0, wide)), dz_s[...]))
        more, gain_grad = norm_back(
            x0, inverse, gain(0, wide), mul(wn_s[0, :, : 3 * WIDTH], dz_s[...])
        )
        ggain_s[0] += fold(gain_grad)
        spread = mul_t(onehot(ids_ref[c], CODES + n), split_low(back + more))
        ge_s[...] += spread[:, :D] + spread[:, D:]
        return carry

    lax.fori_loop(0, chunks, encode_back, 0)

    for block in range(BLOCKS):
        value = g0_s[block]
        if block < 3:
            value = value * HEAD_DIM**-0.5
        grad_ref[0, block * D : (block + 1) * D, :] = value.astype(bf16)
    grad_embed_ref[...] = ge_s[:CODES, :].astype(bf16)
    grad_user_ref[...] = ge_s[CODES:, :].astype(bf16)

    ones = jnp.ones((8, LANES), f32)
    for g in range(7):
        small_ref[g : g + 1, :] = mul_exact(ones, ggain_s[g].T)[:1]
    small_ref[7:8, :] = jnp.broadcast_to(loss, (1, LANES))

    rows_s[...] = jnp.zeros_like(rows_s)

    def bucket_sums(b, carry):
        for head in range(HEADS):
            lanes = slice((head % 2) * LANES, (head % 2 + 1) * LANES)
            hit = jnp.where(buckets == b, gbias_s[head // 2, :, lanes], 0.0)
            rows_s[head, pl.ds(b, 1), :] = jnp.sum(hit, axis=0, keepdims=True)
        return carry

    lax.fori_loop(0, BUCKETS, bucket_sums, 0)
    for head in range(HEADS):
        lanes = slice((head % 2) * LANES, (head % 2 + 1) * LANES)
        for b in range(LEVELS):
            hit = jnp.where(offset == b, self_scores[head // 2][:, lanes], 0.0)
            rows_s[head, BUCKETS + b : BUCKETS + b + 1, :] = jnp.sum(hit, axis=0, keepdims=True)
    total = jnp.zeros((2 * BUCKETS, LANES), f32)
    for head in range(HEADS):
        pick = jnp.where(iota((LANES, LANES), 1) == head, 1.0, 0.0)
        total = total + mul_exact(rows_s[head], pick)
    small_ref[8:, :] = total


def compute(users, bias, ids, start, goal, domain, count, gains, embedding, weights):
    n = users.shape[0]
    chunks, groups = n // 2, n // 4
    wide = 2 * LANES
    vmem = pl.BlockSpec(memory_space=pltpu.VMEM)
    smem = pl.BlockSpec(memory_space=pltpu.SMEM)
    return pl.pallas_call(
        functools.partial(compute_kernel, n),
        out_shape=(
            jax.ShapeDtypeStruct((2, COLS, D), bf16),
            jax.ShapeDtypeStruct((CODES, D), bf16),
            jax.ShapeDtypeStruct((n, D), bf16),
            jax.ShapeDtypeStruct((8 + 2 * BUCKETS, LANES), f32),
        ),
        in_specs=[smem, smem] + [vmem] * 8,
        out_specs=(vmem,) * 4,
        scratch_shapes=[
            pltpu.VMEM((chunks, D, wide), f32),
            pltpu.VMEM((chunks, D, wide), f32),
            pltpu.VMEM((chunks, D, wide), f32),
            pltpu.VMEM((chunks, 3 * WIDTH, wide), bf16),
            pltpu.VMEM((n, PAIRS, KEYS, wide), bf16),
            pltpu.VMEM((chunks, WIDTH, wide), bf16),
            pltpu.VMEM((chunks, FF, wide), bf16),
            pltpu.VMEM((chunks, 2 * WIDTH, wide), bf16),
            pltpu.VMEM((3 * WIDTH, wide), bf16),
            pltpu.VMEM((2, COLS, D), bf16),
            pltpu.VMEM((2 * D, CODES + n), bf16),
            pltpu.VMEM((CODES, D), bf16),
            pltpu.VMEM((7, D, LANES), f32),
            pltpu.VMEM((PAIRS, KEYS, wide), f32),
            pltpu.VMEM((PAIRS, LANES, wide), f32),
            pltpu.VMEM((BLOCKS, D, LANES), f32),
            pltpu.VMEM((CODES + n, D), f32),
            pltpu.VMEM((PAIRS, KEYS, wide), f32),
            pltpu.VMEM((7, D, LANES), f32),
            pltpu.VMEM((HEADS, 2 * BUCKETS, LANES), f32),
            pltpu.VMEM((n, D), f32),
            pltpu.VMEM((groups, LANES, WIDTH), bf16),
            pltpu.VMEM((groups, WIDTH, LANES), bf16),
            pltpu.VMEM((groups, LANES, WIDTH), bf16),
            pltpu.VMEM((groups, WIDTH, LANES), bf16),
            pltpu.VMEM((groups, LANES, LANES), f32),
            pltpu.VMEM((groups, WIDTH, LANES), bf16),
        ],
        compiler_params=pltpu.CompilerParams(vmem_limit_bytes=62 * 2**20),
        name="gradients",
    )(users, bias, ids, start, goal, domain, count, gains, embedding, weights)


MESH = pl.DeviceIdType.MESH


def stages(dp):
    order = [("dp", 1), ("pipe", 1)]
    bit = 2
    while bit < dp:
        order.append(("dp", bit))
        bit *= 2
    return order


def side_of(axis, bit):
    return lax.rem(lax.div(lax.axis_index(axis), bit), 2)


def partner_of(axis, bit):
    place = lax.axis_index(axis)
    return {axis: place + bit * (1 - 2 * side_of(axis, bit))}


def greet(order):
    barrier = pltpu.get_barrier_semaphore()
    for axis, bit in order:
        pl.semaphore_signal(barrier, inc=1, device_id=partner_of(axis, bit), device_id_type=MESH)
    pl.semaphore_wait(barrier, len(order))


def remote(source, target, sends, recvs, index, stage):
    return pltpu.make_async_remote_copy(
        src_ref=source,
        dst_ref=target,
        send_sem=sends.at[index],
        recv_sem=recvs.at[index],
        device_id=partner_of(*stage),
        device_id_type=MESH,
    )


def begin_kernel(
    dp, mixer_ref, feed_ref, domain_ref, goal_ref, w_ref, stat_ref, stat_s, land_s, sends, recvs
):
    order = stages(dp)
    section = lax.axis_index("pipe")
    core = side_of("dp", 1)
    half = D // 2
    greet(order)

    scale = HEAD_DIM**-0.5
    cross = jnp.where(section == 1, scale, 1.0).astype(f32)
    own = w_ref.at[section]
    for start, width, ref, factor in (
        (0, WIDTH, mixer_ref, scale),
        (WIDTH, 3 * WIDTH, mixer_ref, None),
        (4 * WIDTH, WIDTH, mixer_ref, cross),
        (5 * WIDTH, WIDTH, mixer_ref, None),
        (MIXW, 2 * FF, feed_ref, None),
    ):
        first = start if ref is mixer_ref else 0
        value = ref[0, :, first : first + width]
        if factor is not None:
            value = value * factor
        own[:, start : start + width] = value.astype(bf16)
    rows = pl.ds(pl.multiple_of(core * half, half), half)
    across = remote(
        w_ref.at[section, rows], w_ref.at[section, rows], sends, recvs, 0, ("pipe", 1)
    )
    across.start()

    counts = [
        jnp.sum(jnp.where(domain_ref[...] == d, 1.0, 0.0), axis=1, keepdims=True)
        for d in range(DOMAINS)
    ]
    counts += [jnp.zeros((1, 1), f32)] * (8 - DOMAINS)
    stat_s[0, :, CODES:] = jnp.broadcast_to(jnp.concatenate(counts, 0), (8, LANES))
    stat_s[0, :, :CODES] = mul_t(jnp.ones((8, LANES), bf16), onehot(goal_ref[...], CODES))
    for k, stage in enumerate(order):
        copy = remote(stat_s.at[k], land_s.at[k], sends, recvs, 2 + k, stage)
        copy.start()
        copy.wait()
        stat_s[k + 1] = stat_s[k] + land_s[k]
    stat_ref[...] = stat_s[len(order)]

    across.wait()
    other = w_ref.at[1 - section, rows]
    share = remote(other, other, sends, recvs, 1, ("dp", 1))
    share.start()
    share.wait()


def begin(dp, mixer, feed, domain, goal):
    count = len(stages(dp))
    vmem = pl.BlockSpec(memory_space=pltpu.VMEM)
    stat = (8, CODES + LANES)
    return pl.pallas_call(
        functools.partial(begin_kernel, dp),
        out_shape=(
            jax.ShapeDtypeStruct((2, D, COLS), bf16),
            jax.ShapeDtypeStruct(stat, f32),
        ),
        in_specs=[vmem] * 4,
        out_specs=(vmem,) * 2,
        scratch_shapes=[
            pltpu.VMEM((count + 1,) + stat, f32),
            pltpu.VMEM((count,) + stat, f32),
            pltpu.SemaphoreType.DMA((2 + count,)),
            pltpu.SemaphoreType.DMA((2 + count,)),
        ],
        compiler_params=pltpu.CompilerParams(
            collective_id=0, has_side_effects=True, vmem_limit_bytes=32 * 2**20
        ),
        name="begin",
    )(mixer, feed, domain, goal)


def plan(dp):
    section_rows, code_rows = COLS, CODES
    steps = []
    for axis, bit in stages(dp):
        halve_section = axis == "dp" and section_rows % 32 == 0
        halve_codes = code_rows % 32 == 0
        steps.append((axis, bit, halve_section, halve_codes, section_rows, code_rows))
        section_rows = section_rows // 2 if halve_section else section_rows
        code_rows = code_rows // 2 if halve_codes else code_rows
    return steps, section_rows, code_rows


def reduce_kernel(
    dp,
    n,
    grad_ref,
    embed_ref,
    user_ref,
    small_ref,
    ids_ref,
    out_ref,
    out_embed_ref,
    out_user_ref,
    out_small_ref,
    out_ids_ref,
    out_square_ref,
    *scratch,
):
    steps, section_rows, code_rows = plan(dp)
    count = len(steps)
    land, land_embed = scratch[:count], scratch[count : 2 * count]
    sums, sums_embed = scratch[2 * count : 3 * count], scratch[3 * count : 4 * count]
    small_s, land_small, sends, recvs = scratch[4 * count :]
    pipe = lax.axis_index("pipe")
    greet([(step[0], step[1]) for step in steps])

    rising, falling = 0, 0
    for k, step in enumerate(steps):
        side = side_of(step[0], step[1])
        rising = rising + side * 2**k
        falling = falling + side * 2 ** (count - 1 - k)
    out_user_ref[pl.ds(pl.multiple_of(rising * n, n), n), :] = user_ref[...]
    fit = LANES // n
    owner = iota((8, LANES), 1) // n
    out_ids_ref[rising] = jnp.where(owner == lax.rem(rising, fit), ids_ref[...], 0)
    small_s[0] = small_ref[...]

    current, current_embed = grad_ref, embed_ref
    offset, offset_embed = 0, 0
    for k, (axis, bit, halve, halve_codes, rows, codes) in enumerate(steps):
        side = side_of(axis, bit)
        stage = (axis, bit)
        copies = []

        def send(source, target, index):
            copy = remote(source, target, sends, recvs, 5 * k + index, stage)
            copy.start()
            copies.append(copy)

        if axis == "pipe":
            keep = current.at[pipe]
            send(current.at[1 - pipe], land[k], 0)
        elif k == 0:
            part = rows // 2
            keep = current.at[:, pl.ds(pl.multiple_of(side * part, part), part)]
            send(current.at[:, pl.ds(pl.multiple_of((1 - side) * part, part), part)], land[k], 0)
        elif halve:
            part = rows // 2
            keep = current.at[pl.ds(pl.multiple_of(side * part, part), part)]
            send(current.at[pl.ds(pl.multiple_of((1 - side) * part, part), part)], land[k], 0)
        else:
            keep = current
            send(current, land[k], 0)
        if halve:
            offset = offset + side * (rows // 2)
        if halve_codes:
            part = codes // 2
            keep_embed = current_embed.at[pl.ds(pl.multiple_of(side * part, part), part)]
            source = current_embed.at[pl.ds(pl.multiple_of((1 - side) * part, part), part)]
            offset_embed = offset_embed + side * part
        else:
            keep_embed = source = current_embed
        send(source, land_embed[k], 1)
        slots = 2**k
        first = (rising // slots) * slots
        span = pl.ds(pl.multiple_of(first * n, n), slots * n)
        send(out_user_ref.at[span], out_user_ref.at[span], 2)
        span = pl.ds(first, slots)
        send(out_ids_ref.at[span], out_ids_ref.at[span], 3)
        send(small_s.at[k], land_small.at[k], 4)
        for copy in copies:
            copy.wait()
        sums[k][...] = (keep[...].astype(f32) + land[k][...].astype(f32)).astype(bf16)
        sums_embed[k][...] = (
            keep_embed[...].astype(f32) + land_embed[k][...].astype(f32)
        ).astype(bf16)
        small_s[k + 1] = small_s[k] + land_small[k]
        current, current_embed = sums[k], sums_embed[k]
    out_small_ref[...] = small_s[count]

    mine = pl.ds(pl.multiple_of(offset, section_rows), section_rows)
    mine_embed = pl.ds(pl.multiple_of(offset_embed, code_rows), code_rows)
    value = current[...]
    out_ref[mine, :] = value
    value = value.astype(f32)
    code_value = current_embed[...]
    out_embed_ref[mine_embed, :] = code_value
    code_value = code_value.astype(f32)
    copies_held = (2 ** (count - 1)) * section_rows // COLS
    code_copies_held = (2**count) * code_rows // CODES
    squares = jnp.sum(value * value, axis=0, keepdims=True) / copies_held
    code_squares = jnp.sum(code_value * code_value, axis=0, keepdims=True) / code_copies_held
    out_square_ref[falling] = jnp.concatenate(
        [squares, code_squares, jnp.zeros((6, LANES), f32)], 0
    )

    rows, codes = section_rows, code_rows
    for j, (axis, bit, halve, halve_codes, _, _) in enumerate(reversed(steps)):
        side = side_of(axis, bit)
        stage = (axis, bit)
        base = 5 * count + 3 * j
        copies = []
        if halve:
            span = pl.ds(pl.multiple_of(offset, section_rows), rows)
            copies.append(remote(out_ref.at[span], out_ref.at[span], sends, recvs, base, stage))
            offset = offset - side * rows
            rows = rows * 2
        if halve_codes:
            span = pl.ds(pl.multiple_of(offset_embed, code_rows), codes)
            copies.append(
                remote(out_embed_ref.at[span], out_embed_ref.at[span], sends, recvs, base + 1, stage)
            )
            offset_embed = offset_embed - side * codes
            codes = codes * 2
        slots = 2**j
        span = pl.ds((falling // slots) * slots, slots)
        copies.append(
            remote(
                out_square_ref.at[span], out_square_ref.at[span], sends, recvs, base + 2, stage
            )
        )
        for copy in copies:
            copy.start()
        for copy in copies:
            copy.wait()


def reduce(dp, grads, embed, user, small, ids):
    steps, section_rows, code_rows = plan(dp)
    count = len(steps)
    n = user.shape[0]
    devices = 2 * dp
    vmem = pl.BlockSpec(memory_space=pltpu.VMEM)
    buffers, embed_buffers = [], []
    for k, (axis, bit, halve, halve_codes, rows, codes) in enumerate(steps):
        rows = rows // 2 if halve else rows
        buffers.append(pltpu.VMEM((2, rows, D) if k == 0 else (rows, D), bf16))
        embed_buffers.append(pltpu.VMEM((codes // 2 if halve_codes else codes, D), bf16))
    return pl.pallas_call(
        functools.partial(reduce_kernel, dp, n),
        out_shape=(
            jax.ShapeDtypeStruct((COLS, D), bf16),
            jax.ShapeDtypeStruct((CODES, D), bf16),
            jax.ShapeDtypeStruct((devices * n, D), bf16),
            jax.ShapeDtypeStruct(small.shape, f32),
            jax.ShapeDtypeStruct((devices, 8, LANES), jnp.int32),
            jax.ShapeDtypeStruct((devices, 8, LANES), f32),
        ),
        in_specs=[vmem] * 5,
        out_specs=(vmem,) * 6,
        scratch_shapes=buffers
        + embed_buffers
        + buffers
        + embed_buffers
        + [
            pltpu.VMEM((count + 1,) + small.shape, f32),
            pltpu.VMEM((count,) + small.shape, f32),
            pltpu.SemaphoreType.DMA((8 * count,)),
            pltpu.SemaphoreType.DMA((8 * count,)),
        ],
        compiler_params=pltpu.CompilerParams(
            collective_id=1, has_side_effects=True, vmem_limit_bytes=48 * 2**20
        ),
        name="reduce",
    )(grads, embed, user, small, ids)


def adam(weight, moment, square, slope, rate, decay):
    moment = beta_one * moment + (1 - beta_one) * slope
    square = beta_two * square + (1 - beta_two) * slope * slope
    unbiased_moment = moment * (1 / (1 - beta_one**STEP))
    unbiased_square = square * (1 / (1 - beta_two**STEP))
    step = unbiased_moment / (jnp.sqrt(unbiased_square) + adam_eps) + decay * weight
    return weight - rate * step, moment, square


USER_ROWS = 400


def update_kernel(
    grad_ref,
    code_ref,
    user_ref,
    ids_ref,
    square_ref,
    small_ref,
    stat_ref,
    *refs,
):
    big_in, small_in, refs = refs[:9], refs[9:15], refs[15:]
    loss_ref, norm_ref, section_ref, hist_ref = refs[:4]
    big_out, small_out, low_out, refs = refs[4:13], refs[13:19], refs[19:22], refs[22:]
    hold, low_hold, user_grad, in_sems, out_sems = refs[:9], refs[9:12], *refs[12:]
    loads = [pltpu.make_async_copy(big_in[i], hold[i], in_sems.at[i]) for i in range(9)]
    for load in loads:
        load.start()

    users = user_grad.shape[0]
    span = min(1024, user_ref.shape[0])
    slots = span // LANES * (ids_ref.shape[0] * LANES // user_ref.shape[0])
    fit = ids_ref.shape[0] * LANES // user_ref.shape[0]
    user_grad[...] = jnp.zeros_like(user_grad)

    def scatter(part, carry):
        rows = user_ref[pl.ds(pl.multiple_of(part * span, span), span), :]
        lanes = []
        for group in range(span // LANES):
            total = ids_ref[part * slots + group * fit, :1, :]
            for other in range(1, fit):
                total = total + ids_ref[part * slots + group * fit + other, :1, :]
            lanes.append(total)
        ids = jnp.concatenate(lanes, 1)
        for block in range(users // USER_ROWS):
            place = slice(block * USER_ROWS, (block + 1) * USER_ROWS)
            hit = iota((USER_ROWS, span), 0) + block * USER_ROWS == ids
            user_grad[place, :] += mul(jnp.where(hit, 1.0, 0.0).astype(bf16), rows)
        return carry

    lax.fori_loop(0, user_ref.shape[0] // span, scatter, 0)

    def total(x):
        return jnp.sum(jnp.sum(x, axis=0, keepdims=True), axis=1, keepdims=True)

    devices = square_ref.shape[0]
    slot = iota((devices, 8, LANES), 0)
    row = iota((devices, 8, LANES), 1)
    squares = square_ref[...]
    side = lax.rem(lax.div(slot, devices // 4), 2)
    section_squares = [
        total(jnp.sum(jnp.where((row == 0) & (side == s), squares, 0.0), axis=0)) for s in range(2)
    ]
    rest = total(jnp.sum(jnp.where(row == 1, squares, 0.0), axis=0))
    user_values = user_grad[...]
    rest = rest + total(user_values * user_values)
    small = small_ref[...]
    lane, line = iota(small.shape, 1), iota(small.shape, 0)
    counted = (line < 7) | ((line > 7) & (lane < HEADS))
    small_kept = jnp.where(counted, small, 0.0)
    rest = rest + total(small_kept * small_kept)
    norm = jnp.sqrt(section_squares[0] + section_squares[1] + rest)
    factor = jnp.minimum(1.0, clip_norm / (norm + 1e-06))
    loss_ref[0] = small[7, 0]
    norm_ref[0] = norm[0, 0]
    for s in range(2):
        section_ref[s] = jnp.sqrt(section_squares[s])[0, 0]
    for level in range(LEVELS):
        hist_ref[level : level + 1, :] = stat_ref[
            :1, level * CODEBOOK : (level + 1) * CODEBOOK
        ]

    outs = adam(
        small_in[0][...], small_in[1][...], small_in[2][...], factor * small[:7], rate_gain, 0.0
    )
    for ref, value in zip(small_out[:3], outs):
        ref[...] = value
    for s in range(2):
        slope = factor * small[8 + s * BUCKETS : 8 + (s + 1) * BUCKETS, :HEADS]
        outs = adam(
            small_in[3][s], small_in[4][s], small_in[5][s], slope, rate_small, 0.0
        )
        for ref, value in zip(small_out[3:], outs):
            ref[s] = value

    stores = []

    def store(kind, place):
        first = 3 * kind
        pieces = [(hold[first + i], big_out[first + i]) for i in range(3)]
        pieces.append((low_hold[kind], low_out[kind]))
        for source, target in pieces:
            copy = pltpu.make_async_copy(
                source.at[place], target.at[place], out_sems.at[len(stores)]
            )
            copy.start()
            stores.append(copy)

    def step(kind, place, slope):
        first = 3 * kind
        outs = adam(
            hold[first][place],
            hold[first + 1][place],
            hold[first + 2][place],
            factor * slope,
            rate_matrix,
            decay_matrix,
        )
        for i in range(3):
            hold[first + i][place] = outs[i]
        low_hold[kind][place] = outs[0].astype(bf16)

    for i in range(3):
        loads[i].wait()
    for part in range(6):
        for block in range(3 * part, 3 * part + 3):
            lanes = slice(block * LANES, (block + 1) * LANES)
            step(0, (0, slice(None), lanes), grad_ref[lanes, :].astype(f32))
        store(0, (0, slice(None), slice(3 * part * LANES, 3 * (part + 1) * LANES)))
    for i in range(3, 6):
        loads[i].wait()
    for part in range(4):
        for block in range(4 * part, 4 * part + 4):
            lanes = slice(block * LANES, (block + 1) * LANES)
            rows = slice(MIXW + block * LANES, MIXW + (block + 1) * LANES)
            step(1, (0, slice(None), lanes), grad_ref[rows, :].astype(f32))
        store(1, (0, slice(None), slice(4 * part * LANES, 4 * (part + 1) * LANES)))
    for i in range(6, 9):
        loads[i].wait()
    for part in range(4):
        rows = slice(part * CODEBOOK, (part + 1) * CODEBOOK)
        step(2, (rows, slice(None)), code_ref[rows, :].astype(f32))
        store(2, (rows, slice(None)))
    for part in range(users // USER_ROWS):
        rows = slice(part * USER_ROWS, (part + 1) * USER_ROWS)
        place = (slice(CODES + part * USER_ROWS, CODES + (part + 1) * USER_ROWS), slice(None))
        step(2, place, user_grad[rows, :])
        store(2, place)
    for copy in stores:
        copy.wait()


def update(reduced, stat, mixers, feeds, embeds, gains, biases):
    vmem = pl.BlockSpec(memory_space=pltpu.VMEM)
    smem = pl.BlockSpec(memory_space=pltpu.SMEM)
    hbm = pl.BlockSpec(memory_space=pl.ANY)
    big = [*mixers, *feeds, *embeds]
    small = [*gains, *biases]
    low = [jax.ShapeDtypeStruct(x[0].shape, bf16) for x in (mixers, feeds, embeds)]
    users = embeds[0].shape[0] - CODES
    pieces = 4 * (6 + 4 + 4 + users // USER_ROWS)
    return pl.pallas_call(
        update_kernel,
        out_shape=[
            jax.ShapeDtypeStruct((1,), f32),
            jax.ShapeDtypeStruct((1,), f32),
            jax.ShapeDtypeStruct((2,), f32),
            jax.ShapeDtypeStruct((LEVELS, CODEBOOK), f32),
        ]
        + [jax.ShapeDtypeStruct(x.shape, f32) for x in big + small]
        + low,
        in_specs=[vmem] * 7 + [hbm] * 9 + [vmem] * 6,
        out_specs=[smem] * 3 + [vmem] + [hbm] * 9 + [vmem] * 6 + [hbm] * 3,
        scratch_shapes=[pltpu.VMEM(x.shape, f32) for x in big]
        + [pltpu.VMEM(x.shape, bf16) for x in low]
        + [
            pltpu.VMEM((users, D), f32),
            pltpu.SemaphoreType.DMA((9,)),
            pltpu.SemaphoreType.DMA((pieces,)),
        ],
        compiler_params=pltpu.CompilerParams(vmem_limit_bytes=40 * 2**20),
        name="update",
    )(*reduced, stat, *big, *small)


def shards(
    history_codes,
    user_ids,
    targets,
    domains,
    mixer,
    mixer_moment,
    mixer_square,
    feed,
    feed_moment,
    feed_square,
    embedding,
    embedding_moment,
    embedding_square,
    gains,
    gains_moment,
    gains_square,
    position_bias,
    bias_moment,
    bias_square,
):
    dp = lax.axis_size("dp")
    n = history_codes.shape[0] // 2
    first = lax.axis_index("pipe") * n

    def own(table):
        return lax.dynamic_slice_in_dim(table, first, n)

    codes, users, goal = own(history_codes), own(user_ids), own(targets)
    level = jnp.arange(codes.shape[1]) % LEVELS
    ids = jnp.concatenate(
        [
            CODES + jnp.arange(n, dtype=jnp.int32)[:, None],
            level[None, :] * CODEBOOK + codes,
            jnp.full((n, LANES - HIST_LEN), -1, jnp.int32),
        ],
        1,
    ).reshape(n // 2, 1, 2 * LANES)
    goal = jnp.arange(LEVELS)[None, :] * CODEBOOK + goal
    start = jnp.concatenate([jnp.zeros((n, 1), jnp.int32), goal[:, :-1]], 1).reshape(1, -1)
    goal = goal.reshape(1, -1)
    domain = jnp.broadcast_to(own(domains)[:, None], (n, LEVELS)).reshape(1, -1)
    weights, stat = begin(dp, mixer, feed, domain, goal)
    grads, embed, user, small = compute(
        users,
        position_bias.reshape(2 * BUCKETS, HEADS),
        ids,
        start,
        goal,
        domain,
        stat[:, CODES:],
        gains,
        embedding,
        weights,
    )
    spread = jnp.broadcast_to(jnp.tile(users, LANES // n)[None, :], (8, LANES))
    out, out_embed, out_user, out_small, out_ids, out_square = reduce(
        dp, grads, embed, user, small, spread
    )
    outs = update(
        (out, out_embed, out_user, out_ids, out_square, out_small),
        stat,
        (mixer, mixer_moment, mixer_square),
        (feed, feed_moment, feed_square),
        (embedding, embedding_moment, embedding_square),
        (gains, gains_moment, gains_square),
        (position_bias, bias_moment, bias_square),
    )
    loss, norm, sections, histograms = outs[:4]
    return (loss.reshape(()), norm.reshape(()), sections, histograms, *outs[4:])


def solution(mesh):
    by_dp, by_pipe, copied = P("dp"), P("pipe"), P()
    return jax.shard_map(
        shards,
        mesh=mesh,
        in_specs=(by_dp,) * 4 + (by_pipe,) * 6 + (copied,) * 9,
        out_specs=(copied,) * 4 + (by_pipe,) * 6 + (copied,) * 9 + (by_pipe,) * 2 + (copied,),
        check_vma=False,
    )
```

time: 1080 us -> 288 us (0.27); the launches traced: 1070 us -> 288 us
  local copies, waits for them, and re-layouts: 337 us -> 25.4 us
  Pallas kernels: 0 us -> 259 us
  matrix products: 234 us -> 0 us
  waiting for transfers between devices: 204 us -> 0 us
  other arithmetic: 151 us -> 2.17 us
  blocking collectives: 78 us -> 0 us
  loops' own time: 26.7 us -> 0 us
  between operations: 20.7 us -> 0.85 us
  starting transfers between devices: 15.6 us -> 0 us
    pallas_call x0 -> x4, Pallas kernels: none -> 259 us  [the longest x1 143 us: compute(): pl.pallas_call(functools.partial(compute_kernel, n), out_shape=(jax.Shape...]
    dot_general x94 -> x0, matrix products: 234 us -> none  [the longest x20 50.3 us: product(): return jnp.dot(left, right, preferred_element_type=jnp.float32)]
    psum x2 -> x0, waiting for transfers between devices: 175 us -> none  [the longest x1 98.3 us: shards(): mixer_grad, feed_grad = lax.psum((mixer_grad, feed_grad), 'dp')]
    reshape x48 -> x3, local copies, waits for them, and re-layouts: 157 us -> 0.83 us  [the longest x1 0.62 us: shards(): jnp.concatenate([jnp.zeros((n, 1), jnp.int32), goal[:, :-1]], 1)]
    psum x2 -> x0, blocking collectives: 73 us -> none  [the longest x1 37.1 us: shards(): lax.psum((embed_grad, gain_grad, bias_grad, loss_part), ('pipe', 'dp'))]
    cond x200 -> x0, local copies, waits for them, and re-layouts: 55.2 us -> none  [the longest x8 19.6 us: shards(): encoded_grads = lax.cond(section == 0, encode_back, blank)]
    scatter-add x4 -> x0, other arithmetic: 44.7 us -> none  [encoder_backward(): embed_grad = jax.ops.segment_sum(back_start, token_ids, VOCAB)]
    slice x18 -> x1, local copies, waits for them, and re-layouts: 35.7 us -> 0.59 us  [shards(): stat[:, CODES:]]
  transfers between devices with their start and end apart: 10 -> 0, of which waited for: 4 -> 0; matrix products, arithmetic and copies ran while one was open for 50% -> 0% of each run, Pallas kernels for 0% -> 0%
where the time goes in v1:
time: 288 us
  Pallas kernels  259 us (90%)
  local copies, waits for them, and re-layouts  25.4 us (9%)
    pallas_call x1, Pallas kernels, compute(): pl.pallas_call(functools.partial(compute_kernel, n), out_shape=(jax.Shape...  143 us
    pallas_call x1, Pallas kernels, reduce(): pl.pallas_call(functools.partial(reduce_kernel, dp, n), out_shape=(jax.Sh...  76.4 us
    pallas_call x1, Pallas kernels, begin(): pl.pallas_call(functools.partial(begin_kernel, dp), out_shape=(jax.ShapeD...  30.4 us
    unnamed x53, local copies, waits for them, and re-layouts  22.1 us
    pallas_call x1, Pallas kernels, update(): pl.pallas_call(update_kernel, out_shape=[jax.ShapeDtypeStruct((1,), f32),...  9.79 us

profile of v1, /device:TPU:0, one launch (start us, length us, event | category | flops | bytes accessed | tf_op | source)
XLA Modules:
  0.0 287.6 jit_solution(7235008860067483956)
XLA Ops:
  0.7 0.7 dynamic_slice.12.users_ref
  1.4 0.7 dynamic_slice.15
  2.2 0.8 dynamic-slice_add_fusion.1
  3.1 0.7 dynamic-slice_add_fusion
  5.7 1.4 copy.50.refs_12_
  7.1 0.8 copy.54.refs_13_
  7.8 0.8 copy.55.refs_14_
  8.6 1.3 copy-done.1
  9.9 1.2 copy-done.3
  11.1 30.4 %begin.1 = (bf16[2,128,4352]{2,1,0:T(8,128)(2,1)S(1)}, f32[8,1152]{1,0:T(8,128)S(1)}) custom-call(f32[1,128,2304]{2,1,0:T(8,128)S(1)} %copy-done.1, f32[1,128,2048]{2,1,0:T(8,128)S(1)} %copy-done.3, s32[1,128]{1,0:T(1,128)S(1)} %reshape.96.domain_ref, s32[1,128]{1,0:T(1,128)S(1)} %reshape.95.goal_ref), custom_call_target="tpu_custom_call" | custom-call | tf_op jit(solution)/shard_map/begin/pallas_call | solution.py:713
  41.5 1.4 copy-done.6
  43.5 142.7 %gradients.1 = (bf16[2,4352,128]{2,1,0:T(8,128)(2,1)}, bf16[1024,128]{1,0:T(8,128)(2,1)}, bf16[32,128]{1,0:T(8,128)(2,1)}, f32[72,128]{1,0:T(8,128)}) custom-call(s32[32]{0:T(128)} %copy-done.22, f32[64,6]{1,0:T(8,128)} %bitcast.5, s32[16,1,256]{2,1,0:T(1,128)} %bitcast.6, s32[1,128]{1,0:T(1,128)} %reshape.94.start_ref, s32[1,128]{1,0:T(1,128)} %copy-done.19, ...), custom_call_target="tpu_custom_call" | custom-call | tf_op jit(solution)/shard_map/gradients/pallas_call | solution.py:575
  186.2 1.7 copy-done.5
  188.0 0.9 copy-done.14
  188.9 0.8 copy-done.15
  190.4 76.4 %reduce.1 = (bf16[4352,128]{1,0:T(8,128)(2,1)S(1)}, bf16[1024,128]{1,0:T(8,128)(2,1)S(1)}, bf16[1024,128]{1,0:T(8,128)(2,1)S(1)}, f32[72,128]{1,0:T(8,128)S(1)},...) custom-call(bf16[2,4352,128]{2,1,0:T(8,128)(2,1)S(1)} %copy-done.5, bf16[1024,128]{1,0:T(8,128)(2,1)S(1)} %copy-done.14, ...), custom_call_target="tpu_custom_call" | custom-call | tf_op jit(solution)/shard_map/reduce/pallas_call | solution.py:892
  266.8 1.2 copy-done.4
  268.0 1.4 copy-done.7
  269.4 1.4 copy-done.8
  270.8 1.3 copy-done.9
  272.1 1.3 copy-done.10
  273.4 1.2 copy-done.11
  274.6 1.2 copy-done.12
  275.8 9.8 %update.1 = (f32[1]{0:T(128)}, f32[1]{0:T(128)}, f32[2]{0:T(128)}, f32[4,256]{1,0:T(4,128)}, f32[1,128,2304]{2,1,0:T(8,128)}, /*index=5*/f32[1,128,2304]{2,1,0:T...) custom-call(bf16[4352,128]{1,0:T(8,128)(2,1)S(1)} %get-tuple-element, ...), custom_call_target="tpu_custom_call" | custom-call | tf_op jit(solution)/shard_map/update/pallas_call | solution.py:1083
  (53 shorter events, 5.4 us)
Async XLA Ops:
  1.4 42.1 %copy-start.22 = (s32[32]{0:T(128)}, s32[32]{0:T(128)S(1)}, u32[]{:S(2)}) copy-start(s32[32]{0:T(128)S(1)} %dynamic_slice.12.users_ref) | copy-start | bytes 388
  4.0 39.5 %copy-start.18 = (s32[1,128]{1,0:T(1,128)}, s32[1,128]{1,0:T(1,128)S(1)}, u32[]{:S(2)}) copy-start(s32[1,128]{1,0:T(1,128)S(1)} %reshape.96.domain_ref) | copy-start | bytes 1540
  5.0 38.5 %copy-start.19 = (s32[1,128]{1,0:T(1,128)}, s32[1,128]{1,0:T(1,128)S(1)}, u32[]{:S(2)}) copy-start(s32[1,128]{1,0:T(1,128)S(1)} %reshape.95.goal_ref) | copy-start | bytes 1540
  8.6 1.3 copy-start.1
  9.9 1.2 copy-start.3
  41.5 1.4 copy-start.6
  43.5 223.3 %copy-start.2 = (f32[1,128,2304]{2,1,0:T(8,128)S(1)}, f32[1,128,2304]{2,1,0:T(8,128)}, u32[]{:S(2)}) copy-start(f32[1,128,2304]{2,1,0:T(8,128)} %refs_0_.1) | copy-start | bytes 3538948
  43.5 223.3 %copy-start.13 = (f32[2,32,6]{2,1,0:T(8,128)S(1)}, f32[2,32,6]{2,1,0:T(8,128)}, u32[]{:S(2)}) copy-start(f32[2,32,6]{2,1,0:T(8,128)} %copy.50.refs_12_) | copy-start | bytes 4612
  43.5 223.3 %copy-start.16 = (f32[7,128]{1,0:T(8,128)S(1)}, f32[7,128]{1,0:T(8,128)}, u32[]{:S(2)}) copy-start(f32[7,128]{1,0:T(8,128)} %refs_9_.1) | copy-start | bytes 10756
  43.5 223.3 %copy-start.20 = (f32[7,128]{1,0:T(8,128)S(1)}, f32[7,128]{1,0:T(8,128)}, u32[]{:S(2)}) copy-start(f32[7,128]{1,0:T(8,128)} %refs_10_.1) | copy-start | bytes 10756
  43.5 223.3 %copy-start.21 = (f32[7,128]{1,0:T(8,128)S(1)}, f32[7,128]{1,0:T(8,128)}, u32[]{:S(2)}) copy-start(f32[7,128]{1,0:T(8,128)} %refs_11_.1) | copy-start | bytes 10756
  186.2 80.6 %copy-start = (f32[3024,128]{1,0:T(8,128)S(1)}, f32[3024,128]{1,0:T(8,128)}, u32[]{:S(2)}) copy-start(f32[3024,128]{1,0:T(8,128)} %refs_6_.1) | copy-start | bytes 4644868
  186.2 1.7 copy-start.5
  188.0 0.9 copy-start.14
  188.9 0.8 copy-start.15
  189.7 0.7 copy-start.17
  266.8 1.2 copy-start.4
  268.0 1.4 copy-start.7
  269.4 1.4 copy-start.8
  270.8 1.3 copy-start.9
  272.1 1.3 copy-start.10
  273.4 1.2 copy-start.11
  274.6 1.2 copy-start.12

commit v2 on v1

--- a/solution.py
+++ b/solution.py
@@ -24,6 +24,8 @@
 COLS = MIXW + 2 * FF
 BLOCKS = COLS // LANES
 KEYS = 96
+GROUP = 4
+WIDE = GROUP * LANES
 PAIRS = HEADS // 2
 ROWS = 32
 
@@ -170,16 +172,12 @@
     ggain_s,
     rows_s,
     user_s,
-    qbd_s,
-    qbdt_s,
-    dobd_s,
-    dobdt_s,
+    cross_s,
+    cross_back_s,
     pc_s,
     oc_s,
 ):
-    chunks = n // 2
-    groups = n // 4
-    wide = 2 * LANES
+    chunks = n // GROUP
     eye = jnp.where(iota((LANES, LANES), 0) == iota((LANES, LANES), 1), 1.0, 0.0).astype(bf16)
 
     for section in range(2):
@@ -243,12 +241,12 @@
         both = mul(ext_s[...], hot)
         x0 = both[:D] + both[D:]
         x0_s[c] = x0
-        h = norm_low(x0, inverse_rms(x0), gain(0, wide))
+        h = norm_low(x0, inverse_rms(x0), gain(0, WIDE))
         for j in range(3):
             qkv_s[c, j * WIDTH : (j + 1) * WIDTH, :] = mul(
                 wt_s[0, j * WIDTH : (j + 1) * WIDTH, :], h
             ).astype(bf16)
-        for i in range(2):
+        for i in range(GROUP):
             lanes = slice(i * LANES, (i + 1) * LANES)
             natural = mul_t(eye, h[:, lanes]).astype(bf16)[:KEYS]
             keys = mul(natural, wn_s[0, :, WIDTH : 2 * WIDTH]).astype(bf16)
@@ -260,18 +258,18 @@
                     qkv_s[c, 2 * WIDTH + j * LANES : 2 * WIDTH + (j + 1) * LANES, lanes],
                     ebias_s[j],
                 )
-                p_s[2 * c + i, j] = chance
+                p_s[GROUP * c + i, j] = chance
                 o_s[c, part, lanes] = mixed
         x1 = x0 + mul(wn_s[0, :, 3 * WIDTH : 4 * WIDTH], o_s[c])
         x1_s[c] = x1
-        h = norm_low(x1, inverse_rms(x1), gain(1, wide))
+        h = norm_low(x1, inverse_rms(x1), gain(1, WIDE))
         for j in range(2):
             part = slice(j * FF // 2, (j + 1) * FF // 2)
             lifted = mul(wt_s[0, MIXW + j * FF // 2 : MIXW + (j + 1) * FF // 2, :], h)
             r_s[c, part, :] = jnp.maximum(lifted, 0.0).astype(bf16)
         x2 = x1 + mul(wn_s[0, :, MIXW + FF :], r_s[c])
         x2_s[c] = x2
-        e = norm_low(x2, inverse_rms(x2), gain(2, wide))
+        e = norm_low(x2, inverse_rms(x2), gain(2, WIDE))
         for j in range(2):
             part = slice(j * WIDTH, (j + 1) * WIDTH)
             mem_s[c, part, :] = mul(
@@ -305,52 +303,47 @@
     y1 = y0 + mul(wn_s[1, :, 3 * WIDTH : 4 * WIDTH], self_mixed)
     inverse1 = inverse_rms(y1)
     h1 = norm_low(y1, inverse1, gain(4, LANES))
-    cross_query = mul(wt_s[1, 4 * WIDTH : 5 * WIDTH, :], h1).astype(bf16)
-
-    def spread_rows(table, ref, ref_t):
-        for g in range(groups):
-            shape = (LANES, LANES)
-            row, token = g * LANES + iota(shape, 0), iota(shape, 1)
-            rep = jnp.where(token == 4 * (row >> 5) + (row & 3), 1.0, 0.0).astype(bf16)
-            rows = mul_t(rep, table)
-            mask = (iota(rows.shape, 1) >> 6) == ((iota(rows.shape, 0) & 31) >> 2)
-            ref[g] = jnp.where(mask, rows, 0.0).astype(bf16)
-            token, row = iota(shape, 0), g * LANES + iota(shape, 1)
-            rep = jnp.where(token == 4 * (row >> 5) + (row & 3), 1.0, 0.0).astype(bf16)
-            rows = mul(table, rep)
-            ref_t[g] = jnp.where(head_mask(rows.shape), rows, 0.0).astype(bf16)
+    cross_s[...] = mul(wt_s[1, 4 * WIDTH : 5 * WIDTH, :], h1).astype(bf16)
+
+    def rows_of(g, table):
+        row, token = iota((LANES, LANES), 0), iota((LANES, LANES), 1)
+        rep = jnp.where(token == 16 * g + 4 * (row >> 5) + (row & 3), 1.0, 0.0).astype(bf16)
+        rows = mul_t(rep, table)
+        mask = (iota(rows.shape, 1) >> 6) == ((iota(rows.shape, 0) & 31) >> 2)
+        return jnp.where(mask, rows, 0.0).astype(bf16)
+
+    def rows_t_of(g, table):
+        token, row = iota((LANES, LANES), 0), iota((LANES, LANES), 1)
+        rep = jnp.where(token == 16 * g + 4 * (row >> 5) + (row & 3), 1.0, 0.0).astype(bf16)
+        rows = mul(table, rep)
+        return jnp.where(head_mask(rows.shape), rows, 0.0).astype(bf16)
 
     def head_mask(shape):
         return (iota(shape, 0) >> 6) == ((iota(shape, 1) & 31) >> 2)
 
     def gather_rows(ref):
         total = jnp.zeros((WIDTH, LANES), f32)
-        for g in range(groups):
-            row, token = g * LANES + iota((LANES, LANES), 0), iota((LANES, LANES), 1)
-            rep = jnp.where(token == 4 * (row >> 5) + (row & 3), 1.0, 0.0).astype(bf16)
+        for g in range(chunks):
+            row, token = iota((LANES, LANES), 0), iota((LANES, LANES), 1)
+            rep = jnp.where(token == 16 * g + 4 * (row >> 5) + (row & 3), 1.0, 0.0).astype(bf16)
             total = total + mul(ref[g], rep)
         return total.astype(bf16)
 
-    def blocks_of(table, half):
+    def blocks_of(table):
         owner = iota(table.shape, 0) >> 5
         zero = jnp.zeros_like(table)
         return jnp.concatenate(
-            [
-                jnp.where(owner == 2 * half, table, zero),
-                jnp.where(owner == 2 * half + 1, table, zero),
-            ],
-            1,
-        )
-
-    spread_rows(cross_query, qbd_s, qbdt_s)
+            [jnp.where(owner == j, table, zero) for j in range(GROUP)], 1
+        ).astype(bf16)
 
     def cross(g, carry):
+        queries = rows_of(g, cross_s[...])
         parts = []
-        for j in range(4):
+        for j in range(GROUP):
             parts.append(
                 mul(
-                    qbd_s[g, 32 * j : 32 * j + 32, :],
-                    mem_s[2 * g + j // 2, :WIDTH, (j % 2) * LANES : (j % 2 + 1) * LANES],
+                    queries[32 * j : 32 * j + 32],
+                    mem_s[g, :WIDTH, j * LANES : (j + 1) * LANES],
                 )
             )
         scores = jnp.concatenate(parts, 0)
@@ -358,15 +351,11 @@
         chance = jnp.exp(scores - jnp.max(scores, axis=1, keepdims=True))
         chance = chance * (1.0 / jnp.sum(chance, axis=1, keepdims=True))
         pc_s[g] = chance
-        mixed = jnp.zeros((WIDTH, LANES), f32)
-        for half in range(2):
-            mixed = mixed + mul_t(
-                mem_s[2 * g + half, WIDTH:, :], blocks_of(chance, half).astype(bf16)
-            )
+        mixed = mul_t(mem_s[g, WIDTH:, :], blocks_of(chance))
         oc_s[g] = jnp.where(head_mask(mixed.shape), mixed, 0.0).astype(bf16)
         return carry
 
-    lax.fori_loop(0, groups, cross, 0)
+    lax.fori_loop(0, chunks, cross, 0)
     cross_mixed = gather_rows(oc_s)
     y2 = y1 + mul(wn_s[1, :, 5 * WIDTH : 6 * WIDTH], cross_mixed)
     inverse2 = inverse_rms(y2)
@@ -405,32 +394,29 @@
     back = back + more
     low = back.astype(bf16)
     put_blocks(grad_ref, 15, mul_t(low, cross_mixed))
-    spread_rows(mul(wt_s[1, 5 * WIDTH : 6 * WIDTH, :], low).astype(bf16), dobd_s, dobdt_s)
+    cross_back_s[...] = mul(wt_s[1, 5 * WIDTH : 6 * WIDTH, :], low).astype(bf16)
 
     def cross_back(g, carry):
+        mixed_rows = rows_of(g, cross_back_s[...])
         parts = []
-        for j in range(4):
+        for j in range(GROUP):
             parts.append(
                 mul(
-                    dobd_s[g, 32 * j : 32 * j + 32, :],
-                    mem_s[2 * g + j // 2, WIDTH:, (j % 2) * LANES : (j % 2 + 1) * LANES],
+                    mixed_rows[32 * j : 32 * j + 32],
+                    mem_s[g, WIDTH:, j * LANES : (j + 1) * LANES],
                 )
             )
         back_chance = jnp.concatenate(parts, 0)
         chance = pc_s[g]
         inner = jnp.sum(back_chance * chance, axis=1, keepdims=True)
-        back_scores = chance * (back_chance - inner)
-        total = jnp.zeros((WIDTH, LANES), f32)
-        for half in range(2):
-            spread = blocks_of(back_scores, half).astype(bf16)
-            total = total + mul_t(mem_s[2 * g + half, :WIDTH, :], spread)
-            mem_s[2 * g + half, :WIDTH, :] = mul(qbdt_s[g], spread).astype(bf16)
-            spread = blocks_of(chance, half).astype(bf16)
-            mem_s[2 * g + half, WIDTH:, :] = mul(dobdt_s[g], spread).astype(bf16)
+        spread = blocks_of(chance * (back_chance - inner))
+        total = mul_t(mem_s[g, :WIDTH, :], spread)
+        mem_s[g, :WIDTH, :] = mul(rows_t_of(g, cross_s[...]), spread).astype(bf16)
+        mem_s[g, WIDTH:, :] = mul(rows_t_of(g, cross_back_s[...]), blocks_of(chance)).astype(bf16)
         oc_s[g] = jnp.where(head_mask(total.shape), total, 0.0).astype(bf16)
         return carry
 
-    lax.fori_loop(0, groups, cross_back, 0)
+    lax.fori_loop(0, chunks, cross_back, 0)
     back_query = gather_rows(oc_s)
     put_blocks(grad_ref, 12, mul_t(h1, back_query) * HEAD_DIM**-0.5)
     more, gain_grad = norm_back(
@@ -453,14 +439,14 @@
             back_mixed[part],
             self_chance[j],
         )
-        dz_s[part, LANES:] = one
-        dz_s[keys, LANES:] = two
-        dz_s[values, LANES:] = three
+        dz_s[part, LANES : 2 * LANES] = one
+        dz_s[keys, LANES : 2 * LANES] = two
+        dz_s[values, LANES : 2 * LANES] = three
         self_scores.append(scores)
-    put_blocks(grad_ref, 0, mul_t(h0, dz_s[:WIDTH, LANES:]) * HEAD_DIM**-0.5)
-    put_blocks(grad_ref, 3, mul_t(h0, dz_s[WIDTH:, LANES:]))
+    put_blocks(grad_ref, 0, mul_t(h0, dz_s[:WIDTH, LANES : 2 * LANES]) * HEAD_DIM**-0.5)
+    put_blocks(grad_ref, 3, mul_t(h0, dz_s[WIDTH:, LANES : 2 * LANES]))
     more, gain_grad = norm_back(
-        y0, inverse0, gain(3, LANES), mul(wn_s[1, :, : 3 * WIDTH], dz_s[:, LANES:])
+        y0, inverse0, gain(3, LANES), mul(wn_s[1, :, : 3 * WIDTH], dz_s[:, LANES : 2 * LANES])
     )
     ggain_s[3] = gain_grad
     back = back + more
@@ -474,15 +460,15 @@
         ggain_s[g] = jnp.zeros((D, LANES), f32)
 
     def fold(x):
-        return x[:, :LANES] + x[:, LANES:]
+        return sum(x[:, i * LANES : (i + 1) * LANES] for i in range(GROUP))
 
     def encode_back(c, carry):
         x2 = x2_s[c]
         inverse = inverse_rms(x2)
         back_memory = mem_s[c]
-        add_blocks(g0_s, 12, mul_t(norm_low(x2, inverse, gain(2, wide)), back_memory))
+        add_blocks(g0_s, 12, mul_t(norm_low(x2, inverse, gain(2, WIDE)), back_memory))
         back, gain_grad = norm_back(
-            x2, inverse, gain(2, wide), mul(wn_s[0, :, 4 * WIDTH : 6 * WIDTH], back_memory)
+            x2, inverse, gain(2, WIDE), mul(wn_s[0, :, 4 * WIDTH : 6 * WIDTH], back_memory)
         )
         ggain_s[2] += fold(gain_grad)
         low = back.astype(bf16)
@@ -492,16 +478,16 @@
         back_lifted = jnp.where(active.astype(f32) > 0, back_active, 0.0).astype(bf16)
         x1 = x1_s[c]
         inverse = inverse_rms(x1)
-        add_blocks(g0_s, 18, mul_t(norm_low(x1, inverse, gain(1, wide)), back_lifted))
+        add_blocks(g0_s, 18, mul_t(norm_low(x1, inverse, gain(1, WIDE)), back_lifted))
         more, gain_grad = norm_back(
-            x1, inverse, gain(1, wide), mul(wn_s[0, :, MIXW : MIXW + FF], back_lifted)
+            x1, inverse, gain(1, WIDE), mul(wn_s[0, :, MIXW : MIXW + FF], back_lifted)
         )
         ggain_s[1] += fold(gain_grad)
         back = back + more
         low = back.astype(bf16)
         add_blocks(g0_s, 9, mul_t(low, o_s[c]))
         back_mixed = mul(wt_s[0, 3 * WIDTH : 4 * WIDTH, :], low).astype(bf16)
-        for i in range(2):
+        for i in range(GROUP):
             lanes = slice(i * LANES, (i + 1) * LANES)
             for j in range(PAIRS):
                 part = slice(j * LANES, (j + 1) * LANES)
@@ -512,7 +498,7 @@
                     qkv_s[c, part, lanes],
                     mul_t(eye, qkv_s[c, values, lanes]).astype(bf16)[:KEYS],
                     back_mixed[part, lanes],
-                    p_s[2 * c + i, j],
+                    p_s[GROUP * c + i, j],
                 )
                 dz_s[part, lanes] = one
                 dz_s[keys, lanes] = two
@@ -520,9 +506,9 @@
                 gbias_s[j] += scores
         x0 = x0_s[c]
         inverse = inverse_rms(x0)
-        add_blocks(g0_s, 0, mul_t(norm_low(x0, inverse, gain(0, wide)), dz_s[...]))
+        add_blocks(g0_s, 0, mul_t(norm_low(x0, inverse, gain(0, WIDE)), dz_s[...]))
         more, gain_grad = norm_back(
-            x0, inverse, gain(0, wide), mul(wn_s[0, :, : 3 * WIDTH], dz_s[...])
+            x0, inverse, gain(0, WIDE), mul(wn_s[0, :, : 3 * WIDTH], dz_s[...])
         )
         ggain_s[0] += fold(gain_grad)
         spread = mul_t(onehot(ids_ref[c], CODES + n), split_low(back + more))
@@ -568,8 +554,7 @@
 
 def compute(users, bias, ids, start, goal, domain, count, gains, embedding, weights):
     n = users.shape[0]
-    chunks, groups = n // 2, n // 4
-    wide = 2 * LANES
+    chunks = n // GROUP
     vmem = pl.BlockSpec(memory_space=pltpu.VMEM)
     smem = pl.BlockSpec(memory_space=pltpu.SMEM)
     return pl.pallas_call(
@@ -583,33 +568,31 @@
         in_specs=[smem, smem] + [vmem] * 8,
         out_specs=(vmem,) * 4,
         scratch_shapes=[
-            pltpu.VMEM((chunks, D, wide), f32),
-            pltpu.VMEM((chunks, D, wide), f32),
-            pltpu.VMEM((chunks, D, wide), f32),
-            pltpu.VMEM((chunks, 3 * WIDTH, wide), bf16),
-            pltpu.VMEM((n, PAIRS, KEYS, wide), bf16),
-            pltpu.VMEM((chunks, WIDTH, wide), bf16),
-            pltpu.VMEM((chunks, FF, wide), bf16),
-            pltpu.VMEM((chunks, 2 * WIDTH, wide), bf16),
-            pltpu.VMEM((3 * WIDTH, wide), bf16),
+            pltpu.VMEM((chunks, D, WIDE), f32),
+            pltpu.VMEM((chunks, D, WIDE), f32),
+            pltpu.VMEM((chunks, D, WIDE), f32),
+            pltpu.VMEM((chunks, 3 * WIDTH, WIDE), bf16),
+            pltpu.VMEM((n, PAIRS, KEYS, 2 * LANES), bf16),
+            pltpu.VMEM((chunks, WIDTH, WIDE), bf16),
+            pltpu.VMEM((chunks, FF, WIDE), bf16),
+            pltpu.VMEM((chunks, 2 * WIDTH, WIDE), bf16),
+            pltpu.VMEM((3 * WIDTH, WIDE), bf16),
             pltpu.VMEM((2, COLS, D), bf16),
             pltpu.VMEM((2 * D, CODES + n), bf16),
             pltpu.VMEM((CODES, D), bf16),
             pltpu.VMEM((7, D, LANES), f32),
-            pltpu.VMEM((PAIRS, KEYS, wide), f32),
-            pltpu.VMEM((PAIRS, LANES, wide), f32),
+            pltpu.VMEM((PAIRS, KEYS, 2 * LANES), f32),
+            pltpu.VMEM((PAIRS, LANES, 2 * LANES), f32),
             pltpu.VMEM((BLOCKS, D, LANES), f32),
             pltpu.VMEM((CODES + n, D), f32),
-            pltpu.VMEM((PAIRS, KEYS, wide), f32),
+            pltpu.VMEM((PAIRS, KEYS, 2 * LANES), f32),
             pltpu.VMEM((7, D, LANES), f32),
             pltpu.VMEM((HEADS, 2 * BUCKETS, LANES), f32),
             pltpu.VMEM((n, D), f32),
-            pltpu.VMEM((groups, LANES, WIDTH), bf16),
-            pltpu.VMEM((groups, WIDTH, LANES), bf16),
-            pltpu.VMEM((groups, LANES, WIDTH), bf16),
-            pltpu.VMEM((groups, WIDTH, LANES), bf16),
-            pltpu.VMEM((groups, LANES, LANES), f32),
-            pltpu.VMEM((groups, WIDTH, LANES), bf16),
+            pltpu.VMEM((WIDTH, LANES), bf16),
+            pltpu.VMEM((WIDTH, LANES), bf16),
+            pltpu.VMEM((chunks, LANES, LANES), f32),
+            pltpu.VMEM((chunks, WIDTH, LANES), bf16),
         ],
         compiler_params=pltpu.CompilerParams(vmem_limit_bytes=62 * 2**20),
         name="gradients",
@@ -930,23 +913,19 @@
 USER_ROWS = 400
 
 
-def update_kernel(
-    grad_ref,
-    code_ref,
-    user_ref,
-    ids_ref,
-    square_ref,
-    small_ref,
-    stat_ref,
-    *refs,
-):
-    big_in, small_in, refs = refs[:9], refs[9:15], refs[15:]
+def update_kernel(*refs):
+    parts_in, big_in, small_in, refs = refs[:7], refs[7:16], refs[16:22], refs[22:]
     loss_ref, norm_ref, section_ref, hist_ref = refs[:4]
     big_out, small_out, low_out, refs = refs[4:13], refs[13:19], refs[19:22], refs[22:]
-    hold, low_hold, user_grad, in_sems, out_sems = refs[:9], refs[9:12], *refs[12:]
+    parts, hold, low_hold = refs[:7], refs[7:16], refs[16:19]
+    user_grad, part_sems, in_sems, out_sems = refs[19:]
+    grad_ref, code_ref, user_ref, ids_ref, square_ref, small_ref, stat_ref = parts
+    arrivals = [pltpu.make_async_copy(parts_in[i], parts[i], part_sems.at[i]) for i in range(7)]
     loads = [pltpu.make_async_copy(big_in[i], hold[i], in_sems.at[i]) for i in range(9)]
-    for load in loads:
+    for load in arrivals[1:] + arrivals[:1] + loads:
         load.start()
+    for arrival in arrivals:
+        arrival.wait()
 
     users = user_grad.shape[0]
     span = min(1024, user_ref.shape[0])
@@ -1090,12 +1069,14 @@
         ]
         + [jax.ShapeDtypeStruct(x.shape, f32) for x in big + small]
         + low,
-        in_specs=[vmem] * 7 + [hbm] * 9 + [vmem] * 6,
+        in_specs=[hbm] * 16 + [vmem] * 6,
         out_specs=[smem] * 3 + [vmem] + [hbm] * 9 + [vmem] * 6 + [hbm] * 3,
-        scratch_shapes=[pltpu.VMEM(x.shape, f32) for x in big]
+        scratch_shapes=[pltpu.VMEM(x.shape, x.dtype) for x in (*reduced, stat)]
+        + [pltpu.VMEM(x.shape, f32) for x in big]
         + [pltpu.VMEM(x.shape, bf16) for x in low]
         + [
             pltpu.VMEM((users, D), f32),
+            pltpu.SemaphoreType.DMA((7,)),
             pltpu.SemaphoreType.DMA((9,)),
             pltpu.SemaphoreType.DMA((pieces,)),
         ],
@@ -1141,7 +1122,7 @@
             jnp.full((n, LANES - HIST_LEN), -1, jnp.int32),
         ],
         1,
-    ).reshape(n // 2, 1, 2 * LANES)
+    ).reshape(n // GROUP, 1, WIDE)
     goal = jnp.arange(LEVELS)[None, :] * CODEBOOK + goal
     start = jnp.concatenate([jnp.zeros((n, 1), jnp.int32), goal[:, :-1]], 1).reshape(1, -1)
     goal = goal.reshape(1, -1)

time: 288 us -> 265 us (0.920)
  Pallas kernels: 259 us -> 236 us
    pallas_call x1, Pallas kernels: 143 us -> 119 us  [compute(): pl.pallas_call(functools.partial(compute_kernel, n), out_shape=(jax.Shape...]
where the time goes in v2:
time: 265 us
  Pallas kernels  236 us (89%)
  local copies, waits for them, and re-layouts  25.4 us (10%)
    pallas_call x1, Pallas kernels, compute(): pl.pallas_call(functools.partial(compute_kernel, n), out_shape=(jax.Shape...  119 us
    pallas_call x1, Pallas kernels, reduce(): pl.pallas_call(functools.partial(reduce_kernel, dp, n), out_shape=(jax.Sh...  76.4 us
    pallas_call x1, Pallas kernels, begin(): pl.pallas_call(functools.partial(begin_kernel, dp), out_shape=(jax.ShapeD...  30.4 us
    unnamed x53, local copies, waits for them, and re-layouts  22.1 us
    pallas_call x1, Pallas kernels, update(): pl.pallas_call(update_kernel, out_shape=[jax.ShapeDtypeStruct((1,), f32),...  10.6 us

profile of v2, /device:TPU:0, one launch (start us, length us, event | category | flops | bytes accessed | tf_op | source)
XLA Modules:
  0.0 264.7 jit_solution(12895606211921794029)
XLA Ops:
  0.7 0.7 dynamic_slice.12.users_ref
  1.4 0.7 dynamic_slice.15
  2.2 0.8 dynamic-slice_add_fusion.1
  3.1 0.7 dynamic-slice_add_fusion
  5.7 1.4 copy.50.refs_19_
  7.1 0.8 copy.54.refs_20_
  7.8 0.8 copy.55.refs_21_
  8.6 1.3 copy-done.1
  9.9 1.2 copy-done.3
  11.1 30.4 %begin.1 = (bf16[2,128,4352]{2,1,0:T(8,128)(2,1)S(1)}, f32[8,1152]{1,0:T(8,128)S(1)}) custom-call(f32[1,128,2304]{2,1,0:T(8,128)S(1)} %copy-done.1, f32[1,128,2048]{2,1,0:T(8,128)S(1)} %copy-done.3, s32[1,128]{1,0:T(1,128)S(1)} %reshape.96.domain_ref, s32[1,128]{1,0:T(1,128)S(1)} %reshape.95.goal_ref), custom_call_target="tpu_custom_call" | custom-call | tf_op jit(solution)/shard_map/begin/pallas_call | solution.py:696
  41.5 1.4 copy-done.6
  43.5 118.9 %gradients.1 = (bf16[2,4352,128]{2,1,0:T(8,128)(2,1)}, bf16[1024,128]{1,0:T(8,128)(2,1)}, bf16[32,128]{1,0:T(8,128)(2,1)}, f32[72,128]{1,0:T(8,128)}) custom-call(s32[32]{0:T(128)} %copy-done.22, f32[64,6]{1,0:T(8,128)} %bitcast.5, s32[8,1,512]{2,1,0:T(1,128)} %bitcast.6, s32[1,128]{1,0:T(1,128)} %reshape.94.start_ref, s32[1,128]{1,0:T(1,128)} %copy-done.19, ...), custom_call_target="tpu_custom_call" | custom-call | tf_op jit(solution)/shard_map/gradients/pallas_call | solution.py:560
  162.4 1.7 copy-done.5
  164.2 0.9 copy-done.14
  165.1 0.8 copy-done.15
  166.6 76.4 %reduce.1 = (bf16[4352,128]{1,0:T(8,128)(2,1)S(1)}, bf16[1024,128]{1,0:T(8,128)(2,1)S(1)}, bf16[1024,128]{1,0:T(8,128)(2,1)S(1)}, f32[72,128]{1,0:T(8,128)S(1)},...) custom-call(bf16[2,4352,128]{2,1,0:T(8,128)(2,1)S(1)} %copy-done.5, bf16[1024,128]{1,0:T(8,128)(2,1)S(1)} %copy-done.14, ...), custom_call_target="tpu_custom_call" | custom-call | tf_op jit(solution)/shard_map/reduce/pallas_call | solution.py:875
  243.0 1.2 copy-done.4
  244.2 1.4 copy-done.7
  245.6 1.4 copy-done.8
  247.0 1.3 copy-done.9
  248.3 1.3 copy-done.10
  249.6 1.2 copy-done.11
  250.8 1.2 copy-done.12
  252.0 10.6 %update.1 = (f32[1]{0:T(128)}, f32[1]{0:T(128)}, f32[2]{0:T(128)}, f32[4,256]{1,0:T(4,128)}, f32[1,128,2304]{2,1,0:T(8,128)}, /*index=5*/f32[1,128,2304]{2,1,0:T...) custom-call(bf16[4352,128]{1,0:T(8,128)(2,1)S(1)} %get-tuple-element, ...), custom_call_target="tpu_custom_call" | custom-call | tf_op jit(solution)/shard_map/update/pallas_call | solution.py:1062
  (53 shorter events, 5.4 us)
Async XLA Ops:
  1.4 42.1 %copy-start.22 = (s32[32]{0:T(128)}, s32[32]{0:T(128)S(1)}, u32[]{:S(2)}) copy-start(s32[32]{0:T(128)S(1)} %dynamic_slice.12.users_ref) | copy-start | bytes 388
  4.0 39.5 %copy-start.18 = (s32[1,128]{1,0:T(1,128)}, s32[1,128]{1,0:T(1,128)S(1)}, u32[]{:S(2)}) copy-start(s32[1,128]{1,0:T(1,128)S(1)} %reshape.96.domain_ref) | copy-start | bytes 1540
  5.0 38.5 %copy-start.19 = (s32[1,128]{1,0:T(1,128)}, s32[1,128]{1,0:T(1,128)S(1)}, u32[]{:S(2)}) copy-start(s32[1,128]{1,0:T(1,128)S(1)} %reshape.95.goal_ref) | copy-start | bytes 1540
  8.6 1.3 copy-start.1
  9.9 1.2 copy-start.3
  41.5 1.4 copy-start.6
  43.5 199.5 %copy-start.2 = (f32[1,128,2304]{2,1,0:T(8,128)S(1)}, f32[1,128,2304]{2,1,0:T(8,128)}, u32[]{:S(2)}) copy-start(f32[1,128,2304]{2,1,0:T(8,128)} %refs_7_.1) | copy-start | bytes 3538948
  43.5 199.5 %copy-start.13 = (f32[2,32,6]{2,1,0:T(8,128)S(1)}, f32[2,32,6]{2,1,0:T(8,128)}, u32[]{:S(2)}) copy-start(f32[2,32,6]{2,1,0:T(8,128)} %copy.50.refs_19_) | copy-start | bytes 4612
  43.5 199.5 %copy-start.16 = (f32[7,128]{1,0:T(8,128)S(1)}, f32[7,128]{1,0:T(8,128)}, u32[]{:S(2)}) copy-start(f32[7,128]{1,0:T(8,128)} %refs_16_.1) | copy-start | bytes 10756
  43.5 199.5 %copy-start.20 = (f32[7,128]{1,0:T(8,128)S(1)}, f32[7,128]{1,0:T(8,128)}, u32[]{:S(2)}) copy-start(f32[7,128]{1,0:T(8,128)} %refs_17_.1) | copy-start | bytes 10756
  43.5 199.5 %copy-start.21 = (f32[7,128]{1,0:T(8,128)S(1)}, f32[7,128]{1,0:T(8,128)}, u32[]{:S(2)}) copy-start(f32[7,128]{1,0:T(8,128)} %refs_18_.1) | copy-start | bytes 10756
  162.4 80.6 %copy-start = (f32[3024,128]{1,0:T(8,128)S(1)}, f32[3024,128]{1,0:T(8,128)}, u32[]{:S(2)}) copy-start(f32[3024,128]{1,0:T(8,128)} %refs_13_.1) | copy-start | bytes 4644868
  162.4 1.7 copy-start.5
  164.2 0.9 copy-start.14
  165.1 0.8 copy-start.15
  165.9 0.7 copy-start.17
  243.0 1.2 copy-start.4
  244.2 1.4 copy-start.7
  245.6 1.4 copy-start.8
  247.0 1.3 copy-start.9
  248.3 1.3 copy-start.10
  249.6 1.2 copy-start.11
  250.8 1.2 copy-start.12

commit v3 on v2

v3 whole, which is shorter than its diff:
```python
import functools

import jax
import jax.numpy as jnp
from jax import lax
from jax.experimental import pallas as pl
from jax.experimental.pallas import tpu as pltpu
from jax.sharding import PartitionSpec as P

D = 128
HEADS = 6
HEAD_DIM = 64
FF = 1024
CODEBOOK = 256
LEVELS = 4
BUCKETS = 32
DOMAINS = 3
HIST_LEN = 81
STEP = 5
CODES = 1024
LANES = 128
WIDTH = HEADS * HEAD_DIM
MIXW = 6 * WIDTH
COLS = MIXW + 2 * FF
BLOCKS = COLS // LANES
KEYS = 96
GROUP = 4
WIDE = GROUP * LANES
PAIRS = HEADS // 2
FIRST = 4 * WIDTH
REST = COLS - FIRST
USER_ROWS = 400
MESH = pl.DeviceIdType.MESH

norm_eps = 1e-06
beta_one = 0.9
beta_two = 0.999
adam_eps = 1e-08
clip_norm = 0.5
rate_matrix = 0.04
rate_gain = 0.8
rate_small = 0.3
decay_matrix = 0.01

f32 = jnp.float32
bf16 = jnp.bfloat16


def iota(shape, axis):
    return lax.broadcasted_iota(jnp.int32, shape, axis)


def mul(left, right):
    return jnp.dot(left, right, preferred_element_type=f32)


def mul_t(left, right):
    return lax.dot_general(left, right, (((1,), (1,)), ((), ())), preferred_element_type=f32)


def mul_exact(left, right):
    return jnp.dot(left, right, preferred_element_type=f32, precision=lax.Precision.HIGHEST)


def onehot(ids, rows):
    return jnp.where(iota((rows, ids.shape[1]), 0) == ids, 1.0, 0.0).astype(bf16)


def inverse_rms(x):
    return lax.rsqrt(jnp.mean(x * x, axis=0, keepdims=True) + norm_eps)


def norm_low(x, inverse, gain):
    return (x * inverse * gain).astype(bf16)


def norm_back(x, inverse, gain, upstream):
    scaled = x * inverse
    inner = upstream * gain
    back = inverse * (inner - scaled * jnp.mean(inner * scaled, axis=0, keepdims=True))
    return back, upstream * scaled


def block_diag(pair):
    zero = jnp.zeros((HEAD_DIM, LANES), pair.dtype)
    left = jnp.concatenate([pair[:HEAD_DIM], zero], 0)
    right = jnp.concatenate([zero, pair[HEAD_DIM:]], 0)
    return jnp.concatenate([left, right], 1)


def diagonal(both):
    return jnp.concatenate([both[:HEAD_DIM, :LANES], both[HEAD_DIM:, LANES:]], 0)


def pad_keys(table):
    if table.shape[0] == LANES:
        return table
    zero = jnp.zeros((LANES - table.shape[0], table.shape[1]), table.dtype)
    return jnp.concatenate([table, zero], 0)


def attend(keys, query, values, bias):
    scores = mul(keys, block_diag(query)) + bias
    top = jnp.max(scores, axis=0, keepdims=True)
    chance = jnp.exp(scores - top)
    total = jnp.sum(chance, axis=0, keepdims=True)
    chance = (chance * (1.0 / total)).astype(bf16)
    mixed = diagonal(mul(values, pad_keys(chance))).astype(bf16)
    return chance, mixed


def attend_back(keys_t, query, values, back_mixed, chance):
    exact = chance.astype(f32)
    spread = block_diag(back_mixed)
    back_chance = mul(values, spread)
    inner = jnp.sum(back_chance * exact, axis=0, keepdims=True)
    back_scores = exact * (back_chance - inner)
    low = pad_keys(back_scores.astype(bf16))
    back_query = diagonal(mul(keys_t, low)).astype(bf16)
    back_keys = mul_t(block_diag(query), low).astype(bf16)
    back_values = mul_t(spread, pad_keys(chance)).astype(bf16)
    return back_query, back_keys, back_values, back_scores


def split_low(x):
    high = x.astype(bf16)
    return jnp.concatenate([high, (x - high.astype(f32)).astype(bf16)], 0)


def stages(dp):
    order = []
    bit = 1
    while bit < dp:
        order.append(("dp", bit))
        bit *= 2
    return order + [("pipe", 1)]


def side_of(stage):
    axis, bit = stage
    return lax.rem(lax.div(lax.axis_index(axis), bit), 2)


def partner_of(stage):
    axis, bit = stage
    return {axis: lax.axis_index(axis) + bit * (1 - 2 * side_of(stage))}


def shares(order, rows):
    held = [rows]
    for stage in order:
        held.append(held[-1] // 2 if held[-1] % 32 == 0 else held[-1])
    return held


def span(start, size):
    return pl.ds(pl.multiple_of(start, 16), size)


def step_kernel(n, dp, *refs):
    codes_ref, users_ref, user_row_ref, targets_ref, domains_ref, bias_ref, gains_ref = refs[:7]
    mixer_ref, feed_ref, embed_ref = refs[7:10]
    out_ref, out_user_ref, out_ids_ref, out_square_ref, out_small_ref, out_stat_ref = refs[10:16]
    x0_s, x1_s, x2_s, qkv_s, p_s, o_s, r_s, mem_s, dz_s, wn_s, wt_s, ext_s, table_s = refs[16:29]
    gain_s, ebias_s, dbias_s, g0_s, ge_s, gbias_s, ggain_s, rows_s, user_s, ids_s = refs[29:39]
    cross_s, cross_back_s, pc_s, oc_s, rest_s, first_s, codes_s, slot_s, user_low_s = refs[39:48]
    stat_s, stat_land, small_s, small_land, local_sems, sends, recvs = refs[48:55]
    lands = refs[55:]
    order = stages(dp)
    across = order[-1]
    depth = len(order)
    chunks = n // GROUP
    section = lax.axis_index("pipe")
    used = [0]

    def remote(source, target, stage):
        index = used[0]
        used[0] += 1
        return pltpu.make_async_remote_copy(
            src_ref=source,
            dst_ref=target,
            send_sem=sends.at[index],
            recv_sem=recvs.at[index],
            device_id=partner_of(stage),
            device_id_type=MESH,
        )

    locals_in = []
    for block in range(BLOCKS):
        lanes = slice(block * LANES, (block + 1) * LANES)
        if block < MIXW // LANES:
            source = mixer_ref.at[0, :, lanes]
        else:
            source = feed_ref.at[0, :, slice(lanes.start - MIXW, lanes.stop - MIXW)]
        locals_in.append(pltpu.make_async_copy(source, g0_s.at[block], local_sems.at[block]))
    vocabulary = embed_ref.shape[0]
    flat = x2_s.at[pl.ds(0, vocabulary)]
    load_embed = pltpu.make_async_copy(embed_ref, flat, local_sems.at[BLOCKS])
    for copy in locals_in:
        copy.start()
    load_embed.start()

    barrier = pltpu.get_barrier_semaphore()
    for stage in order:
        pl.semaphore_signal(barrier, inc=1, device_id=partner_of(stage), device_id_type=MESH)
    pl.semaphore_wait(barrier, depth)

    scale = HEAD_DIM**-0.5
    cross_scale = jnp.where(section == 1, scale, 1.0).astype(f32)
    for copy in locals_in:
        copy.wait()
    for block in range(BLOCKS):
        value = g0_s[block]
        if block < 3:
            value = value * scale
        elif 12 <= block < 15:
            value = value * cross_scale
        wn_s[section, :, block * LANES : (block + 1) * LANES] = value.astype(bf16)
    half = D // 2
    mine = span(side_of(order[0]) * half, half)
    over = remote(wn_s.at[section, mine], wn_s.at[section, mine], across)
    over.start()

    ids_s[:, : HIST_LEN - 1] = codes_ref[pl.ds(pl.multiple_of(section * n, 8), n), :]
    lane, row = iota((n, LANES), 1), iota((n, LANES), 0)
    ids = ids_s[...] + ((lane & 3) << 8)
    ids = jnp.where(lane < HIST_LEN - 1, ids, jnp.where(lane == HIST_LEN - 1, CODES + row, -1))
    ids_s[...] = ids
    count = targets_ref.shape[1]
    history, token = iota((count, LANES), 0), iota((count, LANES), 1)
    pick = jnp.where((token >> 2) + section * n == history, 1.0, 0.0)
    level, place = iota((LEVELS, LANES), 0), iota((LEVELS, LANES), 1) & 3
    target = mul(targets_ref[...].astype(f32), pick) + (level * CODEBOOK).astype(f32)
    goal = jnp.sum(jnp.where(level == place, target, 0.0), axis=0, keepdims=True).astype(jnp.int32)
    start_ids = jnp.sum(
        jnp.where(level == place - 1, target, 0.0), axis=0, keepdims=True
    ).astype(jnp.int32)
    domain = mul(domains_ref[...].astype(f32), pick)
    pick = jnp.where(lax.rem(token, n) + section * n == history, 1.0, 0.0)
    own_users = mul_exact(user_row_ref[...].astype(f32), pick)

    counts = [
        jnp.sum(jnp.where(domain == d, 1.0, 0.0), axis=1, keepdims=True) for d in range(DOMAINS)
    ]
    counts += [jnp.zeros((1, 1), f32)] * (8 - DOMAINS)
    stat_s[0, :, CODES:] = jnp.broadcast_to(jnp.concatenate(counts, 0), (8, LANES))
    stat_s[0, :, :CODES] = mul_t(jnp.ones((8, LANES), bf16), onehot(goal, CODES))
    slot = 0
    for k, stage in enumerate(order):
        slot = slot + side_of(stage) * 2 ** (depth - 1 - k)
    owner = iota((8, LANES), 1) // n
    own_users = jnp.broadcast_to(own_users, (8, LANES)).astype(jnp.int32)
    slot_s[...] = jnp.where(owner == lax.rem(slot, LANES // n), own_users, 0)
    store_ids = pltpu.make_async_copy(slot_s, out_ids_ref.at[slot], local_sems.at[BLOCKS + 1])
    store_ids.start()
    store_ids.wait()

    def slots_of(j):
        return pl.ds(lax.div(slot, 2**j) * 2**j, 2**j)

    early = []
    for j, stage in enumerate(reversed(order)):
        held = out_ids_ref.at[slots_of(j)]
        early.append(
            (
                remote(stat_s.at[j], stat_land.at[j], stage),
                remote(held, held, stage),
            )
        )

    def early_step(j):
        if j > 0:
            for copy in early[j - 1]:
                copy.wait()
            stat_s[j] = stat_s[j - 1] + stat_land[j - 1]
        if j < depth:
            for copy in early[j]:
                copy.start()

    eye = jnp.where(iota((LANES, LANES), 0) == iota((LANES, LANES), 1), 1.0, 0.0).astype(bf16)
    load_embed.wait()

    def fetch(i, carry):
        user_s[pl.ds(i, 1), :] = x2_s[pl.ds(CODES + users_ref[section * n + i], 1), :]
        return carry

    lax.fori_loop(0, n, fetch, 0)
    for block in range(CODES // LANES + 1):
        if block < CODES // LANES:
            rows = x2_s[block * LANES : (block + 1) * LANES, :]
            table_s[block * LANES : (block + 1) * LANES, :] = rows.astype(bf16)
            width = LANES
        else:
            rows = user_s[...]
            width = n
        high = rows.astype(bf16)
        low = (rows - high.astype(f32)).astype(bf16)
        lanes = slice(block * LANES, block * LANES + width)
        ext_s[:D, lanes] = mul_t(eye, high).astype(bf16)
        ext_s[D:, lanes] = mul_t(eye, low).astype(bf16)

    def lookup(c, carry):
        ids = jnp.concatenate([ids_s[pl.ds(GROUP * c + i, 1), :] for i in range(GROUP)], 1)
        both = mul(ext_s[...], onehot(ids, CODES + n))
        x0_s[c] = both[:D] + both[D:]
        return carry

    lax.fori_loop(0, chunks, lookup, 0)

    for g in range(7):
        gain_s[g] = jnp.broadcast_to(gains_ref[g : g + 1, :], (LANES, LANES)).T

    def positions(axis):
        index = iota((KEYS, LANES), axis)
        return jnp.where(index == HIST_LEN - 1, 0, index + 1)

    key, query = positions(0), positions(1)
    distance = jnp.abs(query - key)
    remoteness = jnp.zeros_like(distance)
    for edge in (12, 16, 23, 32, 46, 64, 91):
        remoteness = remoteness + (distance >= edge).astype(jnp.int32)
    nearby = jnp.minimum(jnp.where(distance < 8, distance, 8 + remoteness), 15)
    buckets = nearby + jnp.where(key > query, 16, 0)
    real = iota((KEYS, LANES), 0) < HIST_LEN
    for head in range(HEADS):
        lanes = slice((head % 2) * LANES, (head % 2 + 1) * LANES)

        def choose(b, table):
            return jnp.where(buckets == b, bias_ref[head, 0, b], table)

        table = lax.fori_loop(0, BUCKETS, choose, jnp.zeros((KEYS, LANES), f32))
        ebias_s[head // 2, :, lanes] = jnp.where(real, table, -1e30)
    key, query = iota((LANES, LANES), 0), iota((LANES, LANES), 1)
    offset = query - key
    seen = ((key >> 2) == (query >> 2)) & (offset >= 0)
    for head in range(HEADS):
        lanes = slice((head % 2) * LANES, (head % 2 + 1) * LANES)
        table = jnp.full((LANES, LANES), -1e30, f32)
        for b in range(LEVELS):
            table = jnp.where(seen & (offset == b), bias_ref[head, 1, b], table)
        dbias_s[head // 2, :, lanes] = table

    def transpose_weights(which):
        for block in range(BLOCKS):
            place = slice(block * LANES, (block + 1) * LANES)
            wt_s[which, place, :] = mul_t(eye, wn_s[which, :, place]).astype(bf16)

    transpose_weights(section)
    over.wait()
    came = wn_s.at[1 - section, mine]
    beside = remote(came, came, order[0])
    beside.start()
    beside.wait()
    transpose_weights(1 - section)

    def gain(g, width):
        column = gain_s[g]
        return column if width == LANES else jnp.concatenate([column] * (width // LANES), 1)

    def encode(c, carry):
        for j in range(depth + 1):
            pl.when(c == j)(functools.partial(early_step, j))
        x0 = x0_s[c]
        h = norm_low(x0, inverse_rms(x0), gain(0, WIDE))
        for j in range(3):
            part = slice(j * WIDTH, (j + 1) * WIDTH)
            qkv_s[c, part, :] = mul(wt_s[0, part, :], h).astype(bf16)
        for i in range(GROUP):
            lanes = slice(i * LANES, (i + 1) * LANES)
            natural = mul_t(eye, h[:, lanes]).astype(bf16)[:KEYS]
            keys = mul(natural, wn_s[0, :, WIDTH : 2 * WIDTH]).astype(bf16)
            for j in range(PAIRS):
                part = slice(j * LANES, (j + 1) * LANES)
                chance, mixed = attend(
                    keys[:, part],
                    qkv_s[c, part, lanes],
                    qkv_s[c, 2 * WIDTH + j * LANES : 2 * WIDTH + (j + 1) * LANES, lanes],
                    ebias_s[j],
                )
                p_s[GROUP * c + i, j] = chance
                o_s[c, part, lanes] = mixed
        x1 = x0 + mul(wn_s[0, :, 3 * WIDTH : 4 * WIDTH], o_s[c])
        x1_s[c] = x1
        h = norm_low(x1, inverse_rms(x1), gain(1, WIDE))
        for j in range(2):
            part = slice(j * FF // 2, (j + 1) * FF // 2)
            lifted = mul(wt_s[0, MIXW + j * FF // 2 : MIXW + (j + 1) * FF // 2, :], h)
            r_s[c, part, :] = jnp.maximum(lifted, 0.0).astype(bf16)
        x2 = x1 + mul(wn_s[0, :, MIXW + FF :], r_s[c])
        put_wide(x2_s, c, x2)
        e = norm_low(x2, inverse_rms(x2), gain(2, WIDE))
        for j in range(2):
            part = slice(j * WIDTH, (j + 1) * WIDTH)
            mem_s[c, part, :] = mul(
                wt_s[0, 4 * WIDTH + j * WIDTH : 4 * WIDTH + (j + 1) * WIDTH, :], e
            ).astype(bf16)
        return carry

    def put_wide(ref, c, value):
        for i in range(GROUP):
            ref[pl.ds(pl.multiple_of((GROUP * c + i) * D, D), D), :] = value[
                :, i * LANES : (i + 1) * LANES
            ]

    def get_wide(ref, c):
        return jnp.concatenate(
            [ref[pl.ds(pl.multiple_of((GROUP * c + i) * D, D), D), :] for i in range(GROUP)], 1
        )

    lax.fori_loop(0, chunks, encode, 0)
    for j in range(chunks, depth + 1):
        early_step(j)
    out_stat_ref[...] = stat_s[depth, :1, :CODES]

    def put_blocks(first, value):
        for index in range(value.shape[1] // LANES):
            block = first + index
            part = value[:, index * LANES : (index + 1) * LANES].astype(bf16)
            if block < FIRST // LANES:
                first_s[1, block * D : (block + 1) * D, :] = part
            else:
                block -= FIRST // LANES
                rest_s[1, block * D : (block + 1) * D, :] = part

    def add_blocks(first, value):
        for index in range(value.shape[1] // LANES):
            g0_s[first + index] += value[:, index * LANES : (index + 1) * LANES]

    start = onehot(start_ids, CODES)
    both = mul(ext_s[:, :CODES], start)
    y0 = both[:D] + both[D:]
    inverse0 = inverse_rms(y0)
    h0 = norm_low(y0, inverse0, gain(3, LANES))
    dz_s[:, :LANES] = mul(wt_s[1, : 3 * WIDTH, :], h0).astype(bf16)
    both = mul(mul_t(eye, h0).astype(bf16), wn_s[1, :, WIDTH : 3 * WIDTH]).astype(bf16)
    self_chance = []
    mixed_parts = []
    for j in range(PAIRS):
        part = slice(j * LANES, (j + 1) * LANES)
        chance, mixed = attend(
            both[:, part],
            dz_s[part, :LANES],
            dz_s[2 * WIDTH + j * LANES : 2 * WIDTH + (j + 1) * LANES, :LANES],
            dbias_s[j],
        )
        self_chance.append(chance)
        mixed_parts.append(mixed)
    self_values = both[:, WIDTH:]
    self_mixed = jnp.concatenate(mixed_parts, 0)
    y1 = y0 + mul(wn_s[1, :, 3 * WIDTH : 4 * WIDTH], self_mixed)
    inverse1 = inverse_rms(y1)
    h1 = norm_low(y1, inverse1, gain(4, LANES))
    cross_s[...] = mul(wt_s[1, 4 * WIDTH : 5 * WIDTH, :], h1).astype(bf16)

    def rows_of(g, table):
        row, token = iota((LANES, LANES), 0), iota((LANES, LANES), 1)
        rep = jnp.where(token == 16 * g + 4 * (row >> 5) + (row & 3), 1.0, 0.0).astype(bf16)
        rows = mul_t(rep, table)
        mask = (iota(rows.shape, 1) >> 6) == ((iota(rows.shape, 0) & 31) >> 2)
        return jnp.where(mask, rows, 0.0).astype(bf16)

    def head_mask(shape):
        return (iota(shape, 0) >> 6) == ((iota(shape, 1) & 31) >> 2)

    def rows_t_of(g, table):
        token, row = iota((LANES, LANES), 0), iota((LANES, LANES), 1)
        rep = jnp.where(token == 16 * g + 4 * (row >> 5) + (row & 3), 1.0, 0.0).astype(bf16)
        rows = mul(table, rep)
        return jnp.where(head_mask(rows.shape), rows, 0.0).astype(bf16)

    def gather_rows(ref):
        total = jnp.zeros((WIDTH, LANES), f32)
        for g in range(chunks):
            row, token = iota((LANES, LANES), 0), iota((LANES, LANES), 1)
            rep = jnp.where(token == 16 * g + 4 * (row >> 5) + (row & 3), 1.0, 0.0).astype(bf16)
            total = total + mul(ref[g], rep)
        return total.astype(bf16)

    def blocks_of(table):
        owner = iota(table.shape, 0) >> 5
        zero = jnp.zeros_like(table)
        return jnp.concatenate(
            [jnp.where(owner == j, table, zero) for j in range(GROUP)], 1
        ).astype(bf16)

    def cross(g, carry):
        queries = rows_of(g, cross_s[...])
        parts = []
        for j in range(GROUP):
            parts.append(
                mul(
                    queries[32 * j : 32 * j + 32],
                    mem_s[g, :WIDTH, j * LANES : (j + 1) * LANES],
                )
            )
        scores = jnp.concatenate(parts, 0)
        scores = jnp.where(iota(scores.shape, 1) < HIST_LEN, scores, -1e30)
        chance = jnp.exp(scores - jnp.max(scores, axis=1, keepdims=True))
        chance = chance * (1.0 / jnp.sum(chance, axis=1, keepdims=True))
        pc_s[g] = chance
        mixed = mul_t(mem_s[g, WIDTH:, :], blocks_of(chance))
        oc_s[g] = jnp.where(head_mask(mixed.shape), mixed, 0.0).astype(bf16)
        return carry

    lax.fori_loop(0, chunks, cross, 0)
    cross_mixed = gather_rows(oc_s)
    y2 = y1 + mul(wn_s[1, :, 5 * WIDTH : 6 * WIDTH], cross_mixed)
    inverse2 = inverse_rms(y2)
    h2 = norm_low(y2, inverse2, gain(5, LANES))
    lifted = mul(wt_s[1, MIXW : MIXW + FF, :], h2)
    active = jnp.maximum(lifted, 0.0).astype(bf16)
    y3 = y2 + mul(wn_s[1, :, MIXW + FF :], active)
    inverse3 = inverse_rms(y3)
    final = norm_low(y3, inverse3, gain(6, LANES))
    logits = mul(table_s[...], final)
    top = jnp.max(logits, axis=0, keepdims=True)
    log_total = top + jnp.log(jnp.sum(jnp.exp(logits - top), axis=0, keepdims=True))
    match = iota(logits.shape, 0) == goal
    picked = jnp.sum(jnp.where(match, logits, 0.0), axis=0, keepdims=True)
    weight = jnp.zeros((1, LANES), f32)
    for d in range(DOMAINS):
        share = 1.0 / (DOMAINS * jnp.maximum(stat_s[depth, d : d + 1, CODES:], 1.0))
        weight = weight + jnp.where(domain == d, share, 0.0)
    loss = jnp.sum(weight * (log_total - picked), axis=1, keepdims=True)
    back_logits = (
        weight * (jnp.exp(logits - log_total) - jnp.where(match, 1.0, 0.0))
    ).astype(bf16)
    back_final = mul(ext_s[:D, :CODES], back_logits)
    table_grad = mul_t(back_logits, final)
    back, gain_grad = norm_back(y3, inverse3, gain(6, LANES), back_final)
    ggain_s[6] = gain_grad
    low = back.astype(bf16)
    put_blocks(26, mul_t(low, active))
    back_lifted = jnp.where(lifted > 0, mul(wt_s[1, MIXW + FF :, :], low), 0.0).astype(bf16)
    put_blocks(18, mul_t(h2, back_lifted))
    more, gain_grad = norm_back(
        y2, inverse2, gain(5, LANES), mul(wn_s[1, :, MIXW : MIXW + FF], back_lifted)
    )
    ggain_s[5] = gain_grad
    back = back + more
    low = back.astype(bf16)
    put_blocks(15, mul_t(low, cross_mixed))
    cross_back_s[...] = mul(wt_s[1, 5 * WIDTH : 6 * WIDTH, :], low).astype(bf16)

    def cross_back(g, carry):
        mixed_rows = rows_of(g, cross_back_s[...])
        parts = []
        for j in range(GROUP):
            parts.append(
                mul(
                    mixed_rows[32 * j : 32 * j + 32],
                    mem_s[g, WIDTH:, j * LANES : (j + 1) * LANES],
                )
            )
        back_chance = jnp.concatenate(parts, 0)
        chance = pc_s[g]
        inner = jnp.sum(back_chance * chance, axis=1, keepdims=True)
        spread = blocks_of(chance * (back_chance - inner))
        total = mul_t(mem_s[g, :WIDTH, :], spread)
        mem_s[g, :WIDTH, :] = mul(rows_t_of(g, cross_s[...]), spread).astype(bf16)
        mem_s[g, WIDTH:, :] = mul(rows_t_of(g, cross_back_s[...]), blocks_of(chance)).astype(bf16)
        oc_s[g] = jnp.where(head_mask(total.shape), total, 0.0).astype(bf16)
        return carry

    lax.fori_loop(0, chunks, cross_back, 0)
    back_query = gather_rows(oc_s)
    put_blocks(12, mul_t(h1, back_query) * HEAD_DIM**-0.5)
    more, gain_grad = norm_back(
        y1, inverse1, gain(4, LANES), mul(wn_s[1, :, 4 * WIDTH : 5 * WIDTH], back_query)
    )
    ggain_s[4] = gain_grad
    back = back + more
    low = back.astype(bf16)
    put_blocks(9, mul_t(low, self_mixed))
    back_mixed = mul(wt_s[1, 3 * WIDTH : 4 * WIDTH, :], low).astype(bf16)
    self_scores = []
    for j in range(PAIRS):
        part = slice(j * LANES, (j + 1) * LANES)
        keys = slice(WIDTH + j * LANES, WIDTH + (j + 1) * LANES)
        values = slice(2 * WIDTH + j * LANES, 2 * WIDTH + (j + 1) * LANES)
        one, two, three, scores = attend_back(
            dz_s[keys, :LANES],
            dz_s[part, :LANES],
            self_values[:, part],
            back_mixed[part],
            self_chance[j],
        )
        dz_s[part, LANES : 2 * LANES] = one
        dz_s[keys, LANES : 2 * LANES] = two
        dz_s[values, LANES : 2 * LANES] = three
        self_scores.append(scores)
    put_blocks(0, mul_t(h0, dz_s[:WIDTH, LANES : 2 * LANES]) * HEAD_DIM**-0.5)
    put_blocks(3, mul_t(h0, dz_s[WIDTH:, LANES : 2 * LANES]))
    more, gain_grad = norm_back(
        y0, inverse0, gain(3, LANES), mul(wn_s[1, :, : 3 * WIDTH], dz_s[:, LANES : 2 * LANES])
    )
    ggain_s[3] = gain_grad
    back = back + more
    spread = mul_t(start, split_low(back))
    ge_s[:CODES, :] = table_grad + spread[:, :D] + spread[:, D:]
    ge_s[CODES:, :] = jnp.zeros((n, D), f32)
    rows_s[...] = jnp.zeros_like(rows_s)
    for head in range(HEADS):
        lanes = slice((head % 2) * LANES, (head % 2 + 1) * LANES)
        for b in range(LEVELS):
            hit = jnp.where(offset == b, self_scores[head // 2][:, lanes], 0.0)
            rows_s[head, BUCKETS + b : BUCKETS + b + 1, :] = jnp.sum(hit, axis=0, keepdims=True)

    def reducing(buffer, kept):
        steps, at = [], 0
        held = shares(order[:-1], buffer.shape[0])
        for k, stage in enumerate(order[:-1]):
            rows, left = held[k], held[k + 1]
            side = side_of(stage)
            if left < rows:
                source = buffer.at[span(at + (1 - side) * left, left)]
                at = at + side * left
            else:
                source = buffer.at[span(at, rows)]
            steps.append((remote(source, kept[k], stage), at, left))
        return steps, at, held

    def begin(steps, k):
        steps[k][0].start()

    def finish(steps, buffer, kept, k):
        copy, at, left = steps[k]
        copy.wait()
        place = span(at, left)
        total = buffer[place, :].astype(f32) + kept[k][...].astype(f32)
        buffer[place, :] = total.astype(bf16)

    flat_depth = depth - 1
    land = {}
    for index, name in enumerate(("rest0", "rest1", "first0", "first1", "codes")):
        land[name] = lands[index * flat_depth : (index + 1) * flat_depth]
    land_rest, land_first, land_codes = lands[5 * flat_depth :]
    rest1 = reducing(rest_s.at[1], land["rest1"])
    first1 = reducing(first_s.at[1], land["first1"])
    rest0 = reducing(rest_s.at[0], land["rest0"])
    first0 = reducing(first_s.at[0], land["first0"])
    codes = reducing(codes_s, land["codes"])

    def step1(k):
        if k > 0:
            finish(rest1[0], rest_s.at[1], land["rest1"], k - 1)
            finish(first1[0], first_s.at[1], land["first1"], k - 1)
        if k < flat_depth:
            begin(rest1[0], k)
            begin(first1[0], k)

    def crossing(buffer, target, at, rows):
        source = buffer.at[1 - section, span(at, rows)]
        return remote(source, target, across)

    cross_rest = crossing(rest_s, land_rest, rest1[1], rest1[2][-1])
    cross_first = crossing(first_s, land_first, first1[1], first1[2][-1])

    def settle(copy, buffer, landed, at, rows, base):
        copy.wait()
        value = (buffer[section, span(at, rows), :].astype(f32) + landed[...].astype(f32)).astype(
            bf16
        )
        out_ref[span(base + at, rows), :] = value
        value = value.astype(f32)
        return jnp.sum(value * value, axis=0, keepdims=True)

    def gathering(base, at, held):
        steps = []
        for k in reversed(range(flat_depth)):
            rows, left = held[k], held[k + 1]
            if left < rows:
                place = out_ref.at[span(base + at, left)]
                steps.append(remote(place, place, order[k]))
                at = at - side_of(order[k]) * left
            else:
                steps.append(None)
        return steps

    gather_rest = gathering(0, rest1[1], rest1[2])
    gather_first = gathering(REST, first1[1], first1[2])

    def step0(k):
        if k > 0 and k <= flat_depth:
            finish(rest0[0], rest_s.at[0], land["rest0"], k - 1)
        if k < flat_depth:
            begin(rest0[0], k)
        if k == flat_depth:
            cross_rest.start()
        if k == flat_depth + 1:
            squares = settle(cross_rest, rest_s, land_rest, rest1[1], rest1[2][-1], 0)
            out_square_ref[slot, 0:1, :] = squares / (dp * rest1[2][-1] // REST)
        if k > flat_depth + 1 and gather_rest[k - flat_depth - 2] is not None:
            gather_rest[k - flat_depth - 2].wait()
        if flat_depth < k < 2 * flat_depth + 1 and gather_rest[k - flat_depth - 1] is not None:
            gather_rest[k - flat_depth - 1].start()

    g0_s[...] = jnp.zeros_like(g0_s)
    gbias_s[...] = jnp.zeros_like(gbias_s)
    for g in range(3):
        ggain_s[g] = jnp.zeros((D, LANES), f32)

    def fold(x):
        return sum(x[:, i * LANES : (i + 1) * LANES] for i in range(GROUP))

    def back_rest(c, carry):
        for j in range(flat_depth + 1):
            pl.when(c == j)(functools.partial(step1, j))
        x2 = get_wide(x2_s, c)
        inverse = inverse_rms(x2)
        back_memory = mem_s[c]
        add_blocks(12, mul_t(norm_low(x2, inverse, gain(2, WIDE)), back_memory))
        back, gain_grad = norm_back(
            x2, inverse, gain(2, WIDE), mul(wn_s[0, :, 4 * WIDTH : 6 * WIDTH], back_memory)
        )
        ggain_s[2] += fold(gain_grad)
        low = back.astype(bf16)
        active = r_s[c]
        add_blocks(26, mul_t(low, active))
        back_active = mul(wt_s[0, MIXW + FF :, :], low)
        back_lifted = jnp.where(active.astype(f32) > 0, back_active, 0.0).astype(bf16)
        x1 = x1_s[c]
        inverse = inverse_rms(x1)
        add_blocks(18, mul_t(norm_low(x1, inverse, gain(1, WIDE)), back_lifted))
        more, gain_grad = norm_back(
            x1, inverse, gain(1, WIDE), mul(wn_s[0, :, MIXW : MIXW + FF], back_lifted)
        )
        ggain_s[1] += fold(gain_grad)
        put_wide(x2_s, c, back + more)
        return carry

    lax.fori_loop(0, chunks, back_rest, 0)
    for j in range(chunks, flat_depth + 1):
        step1(j)
    for block in range(REST // D):
        rest_s[0, block * D : (block + 1) * D, :] = g0_s[FIRST // D + block].astype(bf16)

    def back_first(c, carry):
        for j in range(min(chunks, 2 * flat_depth + 2)):
            pl.when(c == j)(functools.partial(step0, j))
        back = get_wide(x2_s, c)
        low = back.astype(bf16)
        add_blocks(9, mul_t(low, o_s[c]))
        back_mixed = mul(wt_s[0, 3 * WIDTH : 4 * WIDTH, :], low).astype(bf16)
        for i in range(GROUP):
            lanes = slice(i * LANES, (i + 1) * LANES)
            for j in range(PAIRS):
                part = slice(j * LANES, (j + 1) * LANES)
                keys = slice(WIDTH + j * LANES, WIDTH + (j + 1) * LANES)
                values = slice(2 * WIDTH + j * LANES, 2 * WIDTH + (j + 1) * LANES)
                one, two, three, scores = attend_back(
                    qkv_s[c, keys, lanes],
                    qkv_s[c, part, lanes],
                    mul_t(eye, qkv_s[c, values, lanes]).astype(bf16)[:KEYS],
                    back_mixed[part, lanes],
                    p_s[GROUP * c + i, j],
                )
                mem_s[c, part, lanes] = one
                mem_s[c, keys, lanes] = two
                r_s[c, part, lanes] = three
                gbias_s[j] += scores
        x0 = x0_s[c]
        inverse = inverse_rms(x0)
        h = norm_low(x0, inverse, gain(0, WIDE))
        add_blocks(0, mul_t(h, mem_s[c]))
        add_blocks(6, mul_t(h, r_s[c, :WIDTH, :]))
        back_normed = mul(wn_s[0, :, : 2 * WIDTH], mem_s[c])
        back_normed = back_normed + mul(wn_s[0, :, 2 * WIDTH : 3 * WIDTH], r_s[c, :WIDTH, :])
        more, gain_grad = norm_back(x0, inverse, gain(0, WIDE), back_normed)
        ggain_s[0] += fold(gain_grad)
        ids = jnp.concatenate([ids_s[pl.ds(GROUP * c + i, 1), :] for i in range(GROUP)], 1)
        spread = mul_t(onehot(ids, CODES + n), split_low(back + more))
        ge_s[...] += spread[:, :D] + spread[:, D:]
        return carry

    lax.fori_loop(0, chunks, back_first, 0)

    for block in range(FIRST // D):
        value = g0_s[block]
        if block < 3:
            value = value * HEAD_DIM**-0.5
        first_s[0, block * D : (block + 1) * D, :] = value.astype(bf16)
    codes_s[...] = ge_s[:CODES, :].astype(bf16)
    begin(first0[0], 0)
    begin(codes[0], 0)
    user_low_s[...] = ge_s[CODES:, :].astype(bf16)
    store_users = pltpu.make_async_copy(
        user_low_s, out_user_ref.at[span(slot * n, n)], local_sems.at[BLOCKS + 2]
    )
    store_users.start()

    ones = jnp.ones((8, LANES), f32)
    for g in range(7):
        small_s[0, g : g + 1, :] = mul_exact(ones, ggain_s[g].T)[:1]
    small_s[0, 7:8, :] = jnp.broadcast_to(loss, (1, LANES))

    def bucket_sums(b, carry):
        for head in range(HEADS):
            lanes = slice((head % 2) * LANES, (head % 2 + 1) * LANES)
            hit = jnp.where(buckets == b, gbias_s[head // 2, :, lanes], 0.0)
            rows_s[head, pl.ds(b, 1), :] = jnp.sum(hit, axis=0, keepdims=True)
        return carry

    lax.fori_loop(0, BUCKETS, bucket_sums, 0)
    for head in range(HEADS):
        small_s[0, 8 + head : 9 + head, :] = mul_exact(ones, rows_s[head].T)[:1]
    small_s[0, 8 + HEADS :, :] = jnp.zeros((8 - HEADS, LANES), f32)

    small_steps = [remote(small_s.at[k], small_land.at[k], stage) for k, stage in enumerate(order)]
    small_steps[0].start()
    done = min(chunks, 2 * flat_depth + 2)
    for k in range(flat_depth):
        finish(first0[0], first_s.at[0], land["first0"], k)
        finish(codes[0], codes_s, land["codes"], k)
        small_steps[k].wait()
        small_s[k + 1] = small_s[k] + small_land[k]
        small_steps[k + 1].start()
        if k + 1 < flat_depth:
            begin(first0[0], k + 1)
            begin(codes[0], k + 1)
        if done < 2 * flat_depth + 2:
            step0(done)
            done += 1
    while done < 2 * flat_depth + 2:
        step0(done)
        done += 1
    at, rows = codes[1], codes[2][-1]
    left = rows // 2 if rows % 32 == 0 else rows
    side = side_of(across)
    cross_first.start()
    if left < rows:
        source = codes_s.at[span(at + (1 - side) * left, left)]
        at = at + side * left
    else:
        source = codes_s.at[span(at, rows)]
    cross_codes = remote(source, land_codes, across)
    cross_codes.start()
    squares = settle(cross_first, first_s, land_first, first1[1], first1[2][-1], REST)
    out_square_ref[slot, 1:2, :] = squares / (dp * first1[2][-1] // FIRST)
    cross_codes.wait()
    value = codes_s[span(at, left), :].astype(f32) + land_codes[...].astype(f32)
    value = value.astype(bf16)
    out_ref[span(COLS + at, left), :] = value
    value = value.astype(f32)
    squares = jnp.sum(value * value, axis=0, keepdims=True)
    out_square_ref[slot, 2:3, :] = squares / (2 * dp * left // CODES)
    out_square_ref[slot, 3:, :] = jnp.zeros((5, LANES), f32)
    small_steps[depth - 1].wait()
    out_small_ref[...] = small_s[depth - 1] + small_land[depth - 1]

    store_users.wait()
    for j, stage in enumerate(reversed(order)):
        copies = []
        if j == 0:
            if left < rows:
                place = out_ref.at[span(COLS + at, left)]
                copies.append(remote(place, place, stage))
                at = at - side * left
        else:
            k = flat_depth - j
            rows, left = codes[2][k], codes[2][k + 1]
            if left < rows:
                place = out_ref.at[span(COLS + at, left)]
                copies.append(remote(place, place, stage))
                at = at - side_of(stage) * left
            if gather_first[j - 1] is not None:
                copies.append(gather_first[j - 1])
        held = out_square_ref.at[slots_of(j)]
        copies.append(remote(held, held, stage))
        start_row = lax.div(slot, 2**j) * 2**j * n
        held = out_user_ref.at[span(start_row, 2**j * n)]
        copies.append(remote(held, held, stage))
        for copy in copies:
            copy.start()
        for copy in copies:
            copy.wait()


def gradients(codes, users, targets, domains, bias, gains, mixer, feed, embedding, dp):
    n = users.shape[0] // 2
    chunks = n // GROUP
    order = stages(dp)
    depth = len(order)
    devices = 2 * dp
    vmem = pl.BlockSpec(memory_space=pltpu.VMEM)
    smem = pl.BlockSpec(memory_space=pltpu.SMEM)
    hbm = pl.BlockSpec(memory_space=pl.ANY)
    stat = (8, CODES + LANES)
    lands = []
    for rows in (REST, REST, FIRST, FIRST, CODES):
        held = shares(order[:-1], rows)
        lands += [pltpu.VMEM((left, D), bf16) for left in held[1:]]
    last = [shares(order[:-1], rows)[-1] for rows in (REST, FIRST)]
    last.append(shares(order, CODES)[-1])
    lands += [pltpu.VMEM((left, D), bf16) for left in last]
    copies = 16 * depth + 16
    return pl.pallas_call(
        functools.partial(step_kernel, n, dp),
        out_shape=(
            jax.ShapeDtypeStruct((COLS + CODES, D), bf16),
            jax.ShapeDtypeStruct((devices * n, D), bf16),
            jax.ShapeDtypeStruct((devices, 8, LANES), jnp.int32),
            jax.ShapeDtypeStruct((devices, 8, LANES), f32),
            jax.ShapeDtypeStruct((16, LANES), f32),
            jax.ShapeDtypeStruct((1, CODES), f32),
        ),
        in_specs=[vmem, smem, vmem, vmem, vmem, smem, vmem, hbm, hbm, hbm],
        out_specs=(vmem, hbm, hbm, vmem, vmem, vmem),
        scratch_shapes=[
            pltpu.VMEM((chunks, D, WIDE), f32),
            pltpu.VMEM((chunks, D, WIDE), f32),
            pltpu.VMEM((n * D, LANES), f32),
            pltpu.VMEM((chunks, 3 * WIDTH, WIDE), bf16),
            pltpu.VMEM((n, PAIRS, KEYS, 2 * LANES), bf16),
            pltpu.VMEM((chunks, WIDTH, WIDE), bf16),
            pltpu.VMEM((chunks, FF, WIDE), bf16),
            pltpu.VMEM((chunks, 2 * WIDTH, WIDE), bf16),
            pltpu.VMEM((3 * WIDTH, 2 * LANES), bf16),
            pltpu.VMEM((2, D, COLS), bf16),
            pltpu.VMEM((2, COLS, D), bf16),
            pltpu.VMEM((2 * D, CODES + n), bf16),
            pltpu.VMEM((CODES, D), bf16),
            pltpu.VMEM((7, D, LANES), f32),
            pltpu.VMEM((PAIRS, KEYS, 2 * LANES), f32),
            pltpu.VMEM((PAIRS, LANES, 2 * LANES), f32),
            pltpu.VMEM((BLOCKS, D, LANES), f32),
            pltpu.VMEM((CODES + n, D), f32),
            pltpu.VMEM((PAIRS, KEYS, 2 * LANES), f32),
            pltpu.VMEM((7, D, LANES), f32),
            pltpu.VMEM((HEADS, LANES, LANES), f32),
            pltpu.VMEM((n, D), f32),
            pltpu.VMEM((n, LANES), jnp.int32),
            pltpu.VMEM((WIDTH, LANES), bf16),
            pltpu.VMEM((WIDTH, LANES), bf16),
            pltpu.VMEM((chunks, LANES, LANES), f32),
            pltpu.VMEM((chunks, WIDTH, LANES), bf16),
            pltpu.VMEM((2, REST, D), bf16),
            pltpu.VMEM((2, FIRST, D), bf16),
            pltpu.VMEM((CODES, D), bf16),
            pltpu.VMEM((8, LANES), jnp.int32),
            pltpu.VMEM((n, D), bf16),
            pltpu.VMEM((depth + 1,) + stat, f32),
            pltpu.VMEM((depth,) + stat, f32),
            pltpu.VMEM((depth, 16, LANES), f32),
            pltpu.VMEM((depth, 16, LANES), f32),
            pltpu.SemaphoreType.DMA((BLOCKS + 3,)),
            pltpu.SemaphoreType.DMA((copies,)),
            pltpu.SemaphoreType.DMA((copies,)),
        ]
        + lands,
        compiler_params=pltpu.CompilerParams(
            collective_id=0, has_side_effects=True, vmem_limit_bytes=63 * 2**20
        ),
        name="gradients",
    )(codes, users, users.reshape(1, -1), targets, domains, bias, gains, mixer, feed, embedding)


def adam(weight, moment, square, slope, rate, decay):
    moment = beta_one * moment + (1 - beta_one) * slope
    square = beta_two * square + (1 - beta_two) * slope * slope
    unbiased_moment = moment * (1 / (1 - beta_one**STEP))
    unbiased_square = square * (1 / (1 - beta_two**STEP))
    step = unbiased_moment / (jnp.sqrt(unbiased_square) + adam_eps) + decay * weight
    return weight - rate * step, moment, square


def update_kernel(*refs):
    parts_in, big_in, small_in, refs = refs[:6], refs[6:15], refs[15:21], refs[21:]
    loss_ref, norm_ref, section_ref, hist_ref = refs[:4]
    big_out, small_out, low_out, refs = refs[4:13], refs[13:19], refs[19:22], refs[22:]
    parts, hold, low_hold = refs[:6], refs[6:15], refs[15:18]
    user_grad, part_sems, in_sems, out_sems = refs[18:]
    grad_ref, user_ref, ids_ref, square_ref, small_ref, stat_ref = parts
    arrivals = [pltpu.make_async_copy(parts_in[i], parts[i], part_sems.at[i]) for i in range(6)]
    loads = [pltpu.make_async_copy(big_in[i], hold[i], in_sems.at[i]) for i in range(9)]
    for load in arrivals[1:] + arrivals[:1] + loads:
        load.start()
    for arrival in arrivals:
        arrival.wait()

    users = user_grad.shape[0]
    span = min(1024, user_ref.shape[0])
    slots = span // LANES * (ids_ref.shape[0] * LANES // user_ref.shape[0])
    fit = ids_ref.shape[0] * LANES // user_ref.shape[0]
    user_grad[...] = jnp.zeros_like(user_grad)

    def scatter(part, carry):
        rows = user_ref[pl.ds(pl.multiple_of(part * span, span), span), :]
        lanes = []
        for group in range(span // LANES):
            total = ids_ref[part * slots + group * fit, :1, :]
            for other in range(1, fit):
                total = total + ids_ref[part * slots + group * fit + other, :1, :]
            lanes.append(total)
        ids = jnp.concatenate(lanes, 1)
        for block in range(users // USER_ROWS):
            place = slice(block * USER_ROWS, (block + 1) * USER_ROWS)
            hit = iota((USER_ROWS, span), 0) + block * USER_ROWS == ids
            user_grad[place, :] += mul(jnp.where(hit, 1.0, 0.0).astype(bf16), rows)
        return carry

    lax.fori_loop(0, user_ref.shape[0] // span, scatter, 0)

    def total(x):
        return jnp.sum(jnp.sum(x, axis=0, keepdims=True), axis=1, keepdims=True)

    devices = square_ref.shape[0]
    slot = iota((devices, 8, LANES), 0)
    row = iota((devices, 8, LANES), 1)
    squares = square_ref[...]
    side = lax.rem(slot, 2)
    section_squares = [
        total(jnp.sum(jnp.where((row < 2) & (side == s), squares, 0.0), axis=0)) for s in range(2)
    ]
    rest = total(jnp.sum(jnp.where(row == 2, squares, 0.0), axis=0))
    user_values = user_grad[...]
    rest = rest + total(user_values * user_values)
    small = small_ref[...]
    lane, line = iota(small.shape, 1), iota(small.shape, 0)
    counted = (line < 7) | ((line > 7) & (lane < 2 * BUCKETS))
    small_kept = jnp.where(counted, small, 0.0)
    rest = rest + total(small_kept * small_kept)
    norm = jnp.sqrt(section_squares[0] + section_squares[1] + rest)
    factor = jnp.minimum(1.0, clip_norm / (norm + 1e-06))
    loss_ref[0] = small[7, 0]
    norm_ref[0] = norm[0, 0]
    for s in range(2):
        section_ref[s] = jnp.sqrt(section_squares[s])[0, 0]
    for level in range(LEVELS):
        hist_ref[level : level + 1, :] = stat_ref[
            :1, level * CODEBOOK : (level + 1) * CODEBOOK
        ]

    outs = adam(
        small_in[0][...], small_in[1][...], small_in[2][...], factor * small[:7], rate_gain, 0.0
    )
    for ref, value in zip(small_out[:3], outs):
        ref[...] = value
    for head in range(HEADS):
        for s in range(2):
            slope = factor * small[8 + head : 9 + head, s * BUCKETS : (s + 1) * BUCKETS]
            one = slice(s, s + 1)
            outs = adam(
                small_in[3][head, one, :],
                small_in[4][head, one, :],
                small_in[5][head, one, :],
                slope,
                rate_small,
                0.0,
            )
            for ref, value in zip(small_out[3:], outs):
                ref[head, one, :] = value

    stores = []

    def store(kind, place):
        first = 3 * kind
        pieces = [(hold[first + i], big_out[first + i]) for i in range(3)]
        pieces.append((low_hold[kind], low_out[kind]))
        for source, target in pieces:
            copy = pltpu.make_async_copy(
                source.at[place], target.at[place], out_sems.at[len(stores)]
            )
            copy.start()
            stores.append(copy)

    def step(kind, place, slope):
        first = 3 * kind
        outs = adam(
            hold[first][place],
            hold[first + 1][place],
            hold[first + 2][place],
            factor * slope,
            rate_matrix,
            decay_matrix,
        )
        for i in range(3):
            hold[first + i][place] = outs[i]
        low_hold[kind][place] = outs[0].astype(bf16)

    def block_of(block):
        first = FIRST // D
        place = block - first if block >= first else REST // D + block
        return grad_ref[place * D : (place + 1) * D, :].astype(f32)

    for i in range(3):
        loads[i].wait()
    for part in range(6):
        for block in range(3 * part, 3 * part + 3):
            lanes = slice(block * LANES, (block + 1) * LANES)
            step(0, (0, slice(None), lanes), block_of(block))
        store(0, (0, slice(None), slice(3 * part * LANES, 3 * (part + 1) * LANES)))
    for i in range(3, 6):
        loads[i].wait()
    for part in range(4):
        for block in range(4 * part, 4 * part + 4):
            lanes = slice(block * LANES, (block + 1) * LANES)
            step(1, (0, slice(None), lanes), block_of(MIXW // LANES + block))
        store(1, (0, slice(None), slice(4 * part * LANES, 4 * (part + 1) * LANES)))
    for i in range(6, 9):
        loads[i].wait()
    for part in range(4):
        rows = slice(part * CODEBOOK, (part + 1) * CODEBOOK)
        step(2, (rows, slice(None)), grad_ref[COLS + rows.start : COLS + rows.stop, :].astype(f32))
        store(2, (rows, slice(None)))
    for part in range(users // USER_ROWS):
        rows = slice(part * USER_ROWS, (part + 1) * USER_ROWS)
        place = (slice(CODES + part * USER_ROWS, CODES + (part + 1) * USER_ROWS), slice(None))
        step(2, place, user_grad[rows, :])
        store(2, place)
    for copy in stores:
        copy.wait()


def update(reduced, mixers, feeds, embeds, gains, biases):
    vmem = pl.BlockSpec(memory_space=pltpu.VMEM)
    smem = pl.BlockSpec(memory_space=pltpu.SMEM)
    hbm = pl.BlockSpec(memory_space=pl.ANY)
    big = [*mixers, *feeds, *embeds]
    small = [*gains, *biases]
    low = [jax.ShapeDtypeStruct(x[0].shape, bf16) for x in (mixers, feeds, embeds)]
    users = embeds[0].shape[0] - CODES
    pieces = 4 * (6 + 4 + 4 + users // USER_ROWS)
    return pl.pallas_call(
        update_kernel,
        out_shape=[
            jax.ShapeDtypeStruct((1,), f32),
            jax.ShapeDtypeStruct((1,), f32),
            jax.ShapeDtypeStruct((2,), f32),
            jax.ShapeDtypeStruct((LEVELS, CODEBOOK), f32),
        ]
        + [jax.ShapeDtypeStruct(x.shape, f32) for x in big + small]
        + low,
        in_specs=[hbm] * 15 + [vmem] * 6,
        out_specs=[smem] * 3 + [vmem] + [hbm] * 9 + [vmem] * 6 + [hbm] * 3,
        scratch_shapes=[pltpu.VMEM(x.shape, x.dtype) for x in reduced]
        + [pltpu.VMEM(x.shape, f32) for x in big]
        + [pltpu.VMEM(x.shape, bf16) for x in low]
        + [
            pltpu.VMEM((users, D), f32),
            pltpu.SemaphoreType.DMA((6,)),
            pltpu.SemaphoreType.DMA((9,)),
            pltpu.SemaphoreType.DMA((pieces,)),
        ],
        compiler_params=pltpu.CompilerParams(vmem_limit_bytes=62 * 2**20),
        name="update",
    )(*reduced, *big, *small)


def shards(
    history_codes,
    user_ids,
    targets,
    domains,
    mixer,
    mixer_moment,
    mixer_square,
    feed,
    feed_moment,
    feed_square,
    embedding,
    embedding_moment,
    embedding_square,
    gains,
    gains_moment,
    gains_square,
    position_bias,
    bias_moment,
    bias_square,
):
    def turned(table):
        return jnp.transpose(table, (2, 0, 1))

    biases = [turned(x) for x in (position_bias, bias_moment, bias_square)]
    reduced = gradients(
        history_codes,
        user_ids,
        targets.T,
        domains.reshape(1, -1),
        biases[0],
        gains,
        mixer,
        feed,
        embedding,
        lax.axis_size("dp"),
    )
    outs = update(
        reduced,
        (mixer, mixer_moment, mixer_square),
        (feed, feed_moment, feed_square),
        (embedding, embedding_moment, embedding_square),
        (gains, gains_moment, gains_square),
        biases,
    )
    loss, norm, sections, histograms = outs[:4]
    back = [jnp.transpose(x, (1, 2, 0)) for x in outs[16:19]]
    return (
        loss.reshape(()),
        norm.reshape(()),
        sections,
        histograms,
        *outs[4:16],
        *back,
        *outs[19:],
    )


def solution(mesh):
    by_dp, by_pipe, copied = P("dp"), P("pipe"), P()
    return jax.shard_map(
        shards,
        mesh=mesh,
        in_specs=(by_dp,) * 4 + (by_pipe,) * 6 + (copied,) * 9,
        out_specs=(copied,) * 4 + (by_pipe,) * 6 + (copied,) * 9 + (by_pipe,) * 2 + (copied,),
        check_vma=False,
    )
```

time: 265 us -> 197 us (0.74)
  Pallas kernels: 236 us -> 196 us
  local copies, waits for them, and re-layouts: 25.4 us -> 0 us
    pallas_call x3 -> x1, Pallas kernels: 226 us -> 183 us  [gradients(): pl.pallas_call(functools.partial(step_kernel, n, dp), out_shape=(jax.Shap...]
    unnamed x53 -> x0, local copies, waits for them, and re-layouts: 22.1 us -> none
where the time goes in v3:
time: 197 us
  Pallas kernels  196 us (99%)
    pallas_call x1, Pallas kernels, gradients(): pl.pallas_call(functools.partial(step_kernel, n, dp), out_shape=(jax.Shap...  183 us
    pallas_call x1, Pallas kernels, update(): pl.pallas_call(update_kernel, out_shape=[jax.ShapeDtypeStruct((1,), f32),...  13.1 us

profile of v3, /device:TPU:0, one launch (start us, length us, event | category | flops | bytes accessed | tf_op | source)
XLA Modules:
  0.0 196.8 jit_solution(11821233451286255183)
XLA Ops:
  0.7 182.9 %gradients.1 = (bf16[5376,128]{1,0:T(8,128)(2,1)}, bf16[1024,128]{1,0:T(8,128)(2,1)}, s32[32,8,128]{2,1,0:T(8,128)}, f32[32,8,128]{2,1,0:T(8,128)}, f32[16,128]{1,0:T(8,128)}, /*index=5*/f32[1,1024]{1,0:T(1,128)}) custom-call(s32[64,80]{1,0:T(8,128)} %refs_0_.1, s32[64]{0:T(128)} %refs_1_.1, s32[1,64]{1,0:T(1,128)} %bitcast.16, s32[4,64]{1,0:T(4,128)} %bitcast.15, ...), custom_call_target="tpu_custom_call" | custom-call | tf_op jit(solution)/shard_map/gradients/pallas_call | solution.py:897
  183.6 13.1 %update.1 = (f32[1]{0:T(128)}, f32[1]{0:T(128)}, f32[2]{0:T(128)}, f32[4,256]{1,0:T(4,128)}, f32[1,128,2304]{2,1,0:T(8,128)}, /*index=5*/f32[1,128,2304]{2,1,0:T...) custom-call(bf16[5376,128]{1,0:T(8,128)(2,1)} %get-tuple-element.50., ...), custom_call_target="tpu_custom_call" | custom-call | tf_op jit(solution)/shard_map/update/pallas_call | solution.py:1124

commit v4 on v3

--- a/solution.py
+++ b/solution.py
@@ -423,8 +423,8 @@
                 rest_s[1, block * D : (block + 1) * D, :] = part
 
     def add_blocks(first, value):
-        for index in range(value.shape[1] // LANES):
-            g0_s[first + index] += value[:, index * LANES : (index + 1) * LANES]
+        for index in range(value.shape[0] // LANES):
+            g0_s[first + index] += value[index * LANES : (index + 1) * LANES, :]
 
     start = onehot(start_ids, CODES)
     both = mul(ext_s[:, :CODES], start)
@@ -709,19 +709,19 @@
         x2 = get_wide(x2_s, c)
         inverse = inverse_rms(x2)
         back_memory = mem_s[c]
-        add_blocks(12, mul_t(norm_low(x2, inverse, gain(2, WIDE)), back_memory))
+        add_blocks(12, mul_t(back_memory, norm_low(x2, inverse, gain(2, WIDE))))
         back, gain_grad = norm_back(
             x2, inverse, gain(2, WIDE), mul(wn_s[0, :, 4 * WIDTH : 6 * WIDTH], back_memory)
         )
         ggain_s[2] += fold(gain_grad)
         low = back.astype(bf16)
         active = r_s[c]
-        add_blocks(26, mul_t(low, active))
+        add_blocks(26, mul_t(active, low))
         back_active = mul(wt_s[0, MIXW + FF :, :], low)
         back_lifted = jnp.where(active.astype(f32) > 0, back_active, 0.0).astype(bf16)
         x1 = x1_s[c]
         inverse = inverse_rms(x1)
-        add_blocks(18, mul_t(norm_low(x1, inverse, gain(1, WIDE)), back_lifted))
+        add_blocks(18, mul_t(back_lifted, norm_low(x1, inverse, gain(1, WIDE))))
         more, gain_grad = norm_back(
             x1, inverse, gain(1, WIDE), mul(wn_s[0, :, MIXW : MIXW + FF], back_lifted)
         )
@@ -733,14 +733,15 @@
     for j in range(chunks, flat_depth + 1):
         step1(j)
     for block in range(REST // D):
-        rest_s[0, block * D : (block + 1) * D, :] = g0_s[FIRST // D + block].astype(bf16)
+        turned = mul_t(eye, g0_s[FIRST // D + block].astype(bf16)).astype(bf16)
+        rest_s[0, block * D : (block + 1) * D, :] = turned
 
     def back_first(c, carry):
         for j in range(min(chunks, 2 * flat_depth + 2)):
             pl.when(c == j)(functools.partial(step0, j))
         back = get_wide(x2_s, c)
         low = back.astype(bf16)
-        add_blocks(9, mul_t(low, o_s[c]))
+        add_blocks(9, mul_t(o_s[c], low))
         back_mixed = mul(wt_s[0, 3 * WIDTH : 4 * WIDTH, :], low).astype(bf16)
         for i in range(GROUP):
             lanes = slice(i * LANES, (i + 1) * LANES)
@@ -762,8 +763,8 @@
         x0 = x0_s[c]
         inverse = inverse_rms(x0)
         h = norm_low(x0, inverse, gain(0, WIDE))
-        add_blocks(0, mul_t(h, mem_s[c]))
-        add_blocks(6, mul_t(h, r_s[c, :WIDTH, :]))
+        add_blocks(0, mul_t(mem_s[c], h))
+        add_blocks(6, mul_t(r_s[c, :WIDTH, :], h))
         back_normed = mul(wn_s[0, :, : 2 * WIDTH], mem_s[c])
         back_normed = back_normed + mul(wn_s[0, :, 2 * WIDTH : 3 * WIDTH], r_s[c, :WIDTH, :])
         more, gain_grad = norm_back(x0, inverse, gain(0, WIDE), back_normed)
@@ -779,7 +780,8 @@
         value = g0_s[block]
         if block < 3:
             value = value * HEAD_DIM**-0.5
-        first_s[0, block * D : (block + 1) * D, :] = value.astype(bf16)
+        turned = mul_t(eye, value.astype(bf16)).astype(bf16)
+        first_s[0, block * D : (block + 1) * D, :] = turned
     codes_s[...] = ge_s[:CODES, :].astype(bf16)
     begin(first0[0], 0)
     begin(codes[0], 0)
@@ -960,7 +962,8 @@
     square = beta_two * square + (1 - beta_two) * slope * slope
     unbiased_moment = moment * (1 / (1 - beta_one**STEP))
     unbiased_square = square * (1 / (1 - beta_two**STEP))
-    step = unbiased_moment / (jnp.sqrt(unbiased_square) + adam_eps) + decay * weight
+    root = unbiased_square * lax.rsqrt(unbiased_square)
+    step = unbiased_moment / (root + adam_eps) + decay * weight
     return weight - rate * step, moment, square
 
 

time: 197 us -> 198 us (level)
  no operation moved by 1% of the time
where the time goes in v4:
time: 198 us
  Pallas kernels  197 us (99%)
    pallas_call x1, Pallas kernels, gradients(): pl.pallas_call(functools.partial(step_kernel, n, dp), out_shape=(jax.Shap...  184 us
    pallas_call x1, Pallas kernels, update(): pl.pallas_call(update_kernel, out_shape=[jax.ShapeDtypeStruct((1,), f32),...  13 us

profile of v4, /device:TPU:0, one launch (start us, length us, event | category | flops | bytes accessed | tf_op | source)
XLA Modules:
  0.0 197.8 jit_solution(18166515535570224959)
XLA Ops:
  0.7 184.0 %gradients.1 = (bf16[5376,128]{1,0:T(8,128)(2,1)}, bf16[1024,128]{1,0:T(8,128)(2,1)}, s32[32,8,128]{2,1,0:T(8,128)}, f32[32,8,128]{2,1,0:T(8,128)}, f32[16,128]{1,0:T(8,128)}, /*index=5*/f32[1,1024]{1,0:T(1,128)}) custom-call(s32[64,80]{1,0:T(8,128)} %refs_0_.1, s32[64]{0:T(128)} %refs_1_.1, s32[1,64]{1,0:T(1,128)} %bitcast.16, s32[4,64]{1,0:T(4,128)} %bitcast.15, ...), custom_call_target="tpu_custom_call" | custom-call | tf_op jit(solution)/shard_map/gradients/pallas_call | solution.py:899
  184.6 13.0 %update.1 = (f32[1]{0:T(128)}, f32[1]{0:T(128)}, f32[2]{0:T(128)}, f32[4,256]{1,0:T(4,128)}, f32[1,128,2304]{2,1,0:T(8,128)}, /*index=5*/f32[1,128,2304]{2,1,0:T...) custom-call(bf16[5376,128]{1,0:T(8,128)(2,1)} %get-tuple-element.50., ...), custom_call_target="tpu_custom_call" | custom-call | tf_op jit(solution)/shard_map/update/pallas_call | solution.py:1127

commit v5 on v3

--- a/solution.py
+++ b/solution.py
@@ -92,6 +92,10 @@
     return jnp.concatenate([both[:HEAD_DIM, :LANES], both[HEAD_DIM:, LANES:]], 0)
 
 
+def stack(both):
+    return jnp.concatenate([both[:, :LANES], both[:, LANES:]], 0)
+
+
 def pad_keys(table):
     if table.shape[0] == LANES:
         return table
@@ -117,8 +121,8 @@
     back_scores = exact * (back_chance - inner)
     low = pad_keys(back_scores.astype(bf16))
     back_query = diagonal(mul(keys_t, low)).astype(bf16)
-    back_keys = mul_t(block_diag(query), low).astype(bf16)
-    back_values = mul_t(spread, pad_keys(chance)).astype(bf16)
+    back_keys = diagonal(mul_t(query, stack(low))).astype(bf16)
+    back_values = diagonal(mul_t(back_mixed, stack(pad_keys(chance)))).astype(bf16)
     return back_query, back_keys, back_values, back_scores
 
 
@@ -218,8 +222,13 @@
         wn_s[section, :, block * LANES : (block + 1) * LANES] = value.astype(bf16)
     half = D // 2
     mine = span(side_of(order[0]) * half, half)
-    over = remote(wn_s.at[section, mine], wn_s.at[section, mine], across)
-    over.start()
+    pieces = (slice(0, FIRST), slice(FIRST, COLS))
+    over = [
+        remote(wn_s.at[section, mine, piece], wn_s.at[section, mine, piece], across)
+        for piece in pieces
+    ]
+    for copy in over:
+        copy.start()
 
     ids_s[:, : HIST_LEN - 1] = codes_ref[pl.ds(pl.multiple_of(section * n, 8), n), :]
     lane, row = iota((n, LANES), 1), iota((n, LANES), 0)
@@ -340,18 +349,26 @@
             table = jnp.where(seen & (offset == b), bias_ref[head, 1, b], table)
         dbias_s[head // 2, :, lanes] = table
 
-    def transpose_weights(which):
-        for block in range(BLOCKS):
+    def transpose_weights(which, first, last):
+        for block in range(first, last):
             place = slice(block * LANES, (block + 1) * LANES)
-            wt_s[which, place, :] = mul_t(eye, wn_s[which, :, place]).astype(bf16)
-
-    transpose_weights(section)
-    over.wait()
-    came = wn_s.at[1 - section, mine]
-    beside = remote(came, came, order[0])
-    beside.start()
-    beside.wait()
-    transpose_weights(1 - section)
+            wt_s[which, place, :] = wn_s[which, :, place].T
+
+    beside = []
+    for piece in pieces:
+        came = wn_s.at[1 - section, mine, piece]
+        beside.append(remote(came, came, order[0]))
+    over[0].wait()
+    beside[0].start()
+    transpose_weights(section, 0, BLOCKS)
+    beside[0].wait()
+    transpose_weights(1 - section, 0, FIRST // LANES)
+
+    def rest_arrives():
+        over[1].wait()
+        beside[1].start()
+        beside[1].wait()
+        transpose_weights(1 - section, FIRST // LANES, BLOCKS)
 
     def gain(g, width):
         column = gain_s[g]
@@ -367,12 +384,11 @@
             qkv_s[c, part, :] = mul(wt_s[0, part, :], h).astype(bf16)
         for i in range(GROUP):
             lanes = slice(i * LANES, (i + 1) * LANES)
-            natural = mul_t(eye, h[:, lanes]).astype(bf16)[:KEYS]
-            keys = mul(natural, wn_s[0, :, WIDTH : 2 * WIDTH]).astype(bf16)
             for j in range(PAIRS):
                 part = slice(j * LANES, (j + 1) * LANES)
+                keys = slice(WIDTH + j * LANES, WIDTH + (j + 1) * LANES)
                 chance, mixed = attend(
-                    keys[:, part],
+                    qkv_s[c, keys, lanes].T[:KEYS],
                     qkv_s[c, part, lanes],
                     qkv_s[c, 2 * WIDTH + j * LANES : 2 * WIDTH + (j + 1) * LANES, lanes],
                     ebias_s[j],
@@ -381,6 +397,7 @@
                 o_s[c, part, lanes] = mixed
         x1 = x0 + mul(wn_s[0, :, 3 * WIDTH : 4 * WIDTH], o_s[c])
         x1_s[c] = x1
+        pl.when(c == 0)(rest_arrives)
         h = norm_low(x1, inverse_rms(x1), gain(1, WIDE))
         for j in range(2):
             part = slice(j * FF // 2, (j + 1) * FF // 2)
@@ -483,17 +500,17 @@
             [jnp.where(owner == j, table, zero) for j in range(GROUP)], 1
         ).astype(bf16)
 
+    def row_products(rows, ref, g, first):
+        parts = []
+        for j in range(0, GROUP, 2):
+            pair = slice(j * LANES, (j + 2) * LANES)
+            both = mul(rows[32 * j : 32 * j + 64], ref[g, first : first + WIDTH, pair])
+            parts += [both[:32, :LANES], both[32:, LANES:]]
+        return jnp.concatenate(parts, 0)
+
     def cross(g, carry):
         queries = rows_of(g, cross_s[...])
-        parts = []
-        for j in range(GROUP):
-            parts.append(
-                mul(
-                    queries[32 * j : 32 * j + 32],
-                    mem_s[g, :WIDTH, j * LANES : (j + 1) * LANES],
-                )
-            )
-        scores = jnp.concatenate(parts, 0)
+        scores = row_products(queries, mem_s, g, 0)
         scores = jnp.where(iota(scores.shape, 1) < HIST_LEN, scores, -1e30)
         chance = jnp.exp(scores - jnp.max(scores, axis=1, keepdims=True))
         chance = chance * (1.0 / jnp.sum(chance, axis=1, keepdims=True))
@@ -544,15 +561,7 @@
 
     def cross_back(g, carry):
         mixed_rows = rows_of(g, cross_back_s[...])
-        parts = []
-        for j in range(GROUP):
-            parts.append(
-                mul(
-                    mixed_rows[32 * j : 32 * j + 32],
-                    mem_s[g, WIDTH:, j * LANES : (j + 1) * LANES],
-                )
-            )
-        back_chance = jnp.concatenate(parts, 0)
+        back_chance = row_products(mixed_rows, mem_s, g, WIDTH)
         chance = pc_s[g]
         inner = jnp.sum(back_chance * chance, axis=1, keepdims=True)
         spread = blocks_of(chance * (back_chance - inner))
@@ -751,7 +760,7 @@
                 one, two, three, scores = attend_back(
                     qkv_s[c, keys, lanes],
                     qkv_s[c, part, lanes],
-                    mul_t(eye, qkv_s[c, values, lanes]).astype(bf16)[:KEYS],
+                    qkv_s[c, values, lanes].T[:KEYS],
                     back_mixed[part, lanes],
                     p_s[GROUP * c + i, j],
                 )
@@ -960,7 +969,8 @@
     square = beta_two * square + (1 - beta_two) * slope * slope
     unbiased_moment = moment * (1 / (1 - beta_one**STEP))
     unbiased_square = square * (1 / (1 - beta_two**STEP))
-    step = unbiased_moment / (jnp.sqrt(unbiased_square) + adam_eps) + decay * weight
+    root = unbiased_square * lax.rsqrt(unbiased_square)
+    step = unbiased_moment / (root + adam_eps) + decay * weight
     return weight - rate * step, moment, square
 
 

time: 197 us -> 184 us (0.934)
  Pallas kernels: 196 us -> 183 us
    pallas_call x1, Pallas kernels: 183 us -> 170 us  [gradients(): pl.pallas_call(functools.partial(step_kernel, n, dp), out_shape=(jax.Shap...]
where the time goes in v5:
time: 184 us
  Pallas kernels  183 us (99%)
    pallas_call x1, Pallas kernels, gradients(): pl.pallas_call(functools.partial(step_kernel, n, dp), out_shape=(jax.Shap...  170 us
    pallas_call x1, Pallas kernels, update(): pl.pallas_call(update_kernel, out_shape=[jax.ShapeDtypeStruct((1,), f32),...  13 us

profile of v5, /device:TPU:0, one launch (start us, length us, event | category | flops | bytes accessed | tf_op | source)
XLA Modules:
  0.0 183.7 jit_solution(6529705662849134522)
XLA Ops:
  0.7 169.8 %gradients.1 = (bf16[5376,128]{1,0:T(8,128)(2,1)}, bf16[1024,128]{1,0:T(8,128)(2,1)}, s32[32,8,128]{2,1,0:T(8,128)}, f32[32,8,128]{2,1,0:T(8,128)}, f32[16,128]{1,0:T(8,128)}, /*index=5*/f32[1,1024]{1,0:T(1,128)}) custom-call(s32[64,80]{1,0:T(8,128)} %refs_0_.1, s32[64]{0:T(128)} %refs_1_.1, s32[1,64]{1,0:T(1,128)} %bitcast.16, s32[4,64]{1,0:T(4,128)} %bitcast.15, ...), custom_call_target="tpu_custom_call" | custom-call | tf_op jit(solution)/shard_map/gradients/pallas_call | solution.py:906
  170.5 13.0 %update.1 = (f32[1]{0:T(128)}, f32[1]{0:T(128)}, f32[2]{0:T(128)}, f32[4,256]{1,0:T(4,128)}, f32[1,128,2304]{2,1,0:T(8,128)}, /*index=5*/f32[1,128,2304]{2,1,0:T...) custom-call(bf16[5376,128]{1,0:T(8,128)(2,1)} %get-tuple-element.50., ...), custom_call_target="tpu_custom_call" | custom-call | tf_op jit(solution)/shard_map/update/pallas_call | solution.py:1134

commit v6 on v5

--- a/solution.py
+++ b/solution.py
@@ -62,6 +62,16 @@
     return jnp.dot(left, right, preferred_element_type=f32, precision=lax.Precision.HIGHEST)
 
 
+def mul_exact_t(left, right):
+    return lax.dot_general(
+        left,
+        right,
+        (((1,), (1,)), ((), ())),
+        preferred_element_type=f32,
+        precision=lax.Precision.HIGHEST,
+    )
+
+
 def onehot(ids, rows):
     return jnp.where(iota((rows, ids.shape[1]), 0) == ids, 1.0, 0.0).astype(bf16)
 
@@ -132,12 +142,9 @@
 
 
 def stages(dp):
-    order = []
-    bit = 1
-    while bit < dp:
-        order.append(("dp", bit))
-        bit *= 2
-    return order + [("pipe", 1)]
+    bits = [2**k for k in range(dp.bit_length() - 1)]
+    near = bits[1:4]
+    return [("dp", bit) for bit in bits[:1] + bits[4:] + near] + [("pipe", 1)]
 
 
 def side_of(stage):
@@ -150,10 +157,13 @@
     return {axis: lax.axis_index(axis) + bit * (1 - 2 * side_of(stage))}
 
 
-def shares(order, rows):
+def shares(dp, rows, across=0):
     held = [rows]
-    for stage in order:
-        held.append(held[-1] // 2 if held[-1] % 32 == 0 else held[-1])
+    depth = len(stages(dp)) - 1
+    for k in range(depth + across):
+        later = min(3, depth - 1 - k) + across if k < depth else 0
+        half = held[-1] // 2
+        held.append(half if half % (16 * 2**later) == 0 else held[-1])
     return held
 
 
@@ -164,12 +174,12 @@
 def step_kernel(n, dp, *refs):
     codes_ref, users_ref, user_row_ref, targets_ref, domains_ref, bias_ref, gains_ref = refs[:7]
     mixer_ref, feed_ref, embed_ref = refs[7:10]
-    out_ref, out_user_ref, out_ids_ref, out_square_ref, out_small_ref, out_stat_ref = refs[10:16]
-    x0_s, x1_s, x2_s, qkv_s, p_s, o_s, r_s, mem_s, dz_s, wn_s, wt_s, ext_s, table_s = refs[16:29]
-    gain_s, ebias_s, dbias_s, g0_s, ge_s, gbias_s, ggain_s, rows_s, user_s, ids_s = refs[29:39]
-    cross_s, cross_back_s, pc_s, oc_s, rest_s, first_s, codes_s, slot_s, user_low_s = refs[39:48]
-    stat_s, stat_land, small_s, small_land, local_sems, sends, recvs = refs[48:55]
-    lands = refs[55:]
+    out_ref, out_user_ref, out_ids_ref, out_slot_ref, out_stat_ref = refs[10:15]
+    x0_s, x1_s, x2_s, qkv_s, p_s, o_s, r_s, mem_s, dz_s, wn_s, wt_s, ext_s = refs[15:27]
+    gain_s, ebias_s, dbias_s, g0_s, ge_s, gbias_s, ggain_s, rows_s, user_s, ids_s = refs[27:37]
+    cross_s, cross_back_s, pc_s, oc_s, rest_s, first_s, codes_s, slot_s, user_low_s, own_slot_s = refs[37:47]
+    stat_s, stat_land, near_first, near_codes, local_sems, sends, recvs = refs[47:54]
+    lands = refs[54:]
     order = stages(dp)
     across = order[-1]
     depth = len(order)
@@ -177,7 +187,7 @@
     section = lax.axis_index("pipe")
     used = [0]
 
-    def remote(source, target, stage):
+    def remote_to(source, target, device):
         index = used[0]
         used[0] += 1
         return pltpu.make_async_remote_copy(
@@ -185,9 +195,29 @@
             dst_ref=target,
             send_sem=sends.at[index],
             recv_sem=recvs.at[index],
-            device_id=partner_of(stage),
+            device_id=device,
             device_id_type=MESH,
         )
+
+    def remote(source, target, stage):
+        return remote_to(source, target, partner_of(stage))
+
+    near, far = order[-4:], order[:-4]
+    masks = range(1, 2 ** len(near))
+
+    def device_of(mask):
+        place = {"dp": lax.axis_index("dp"), "pipe": lax.axis_index("pipe")}
+        for i, (axis, bit) in enumerate(near):
+            if mask >> i & 1:
+                place[axis] = place[axis] + bit * (1 - 2 * side_of((axis, bit)))
+        return place
+
+    def shift_of(mask, lefts):
+        total = 0
+        for i, left in enumerate(lefts):
+            side = side_of(near[i])
+            total = total + (1 - side if mask >> i & 1 else side) * left
+        return total
 
     locals_in = []
     for block in range(BLOCKS):
@@ -205,9 +235,11 @@
     load_embed.start()
 
     barrier = pltpu.get_barrier_semaphore()
-    for stage in order:
+    for stage in far:
         pl.semaphore_signal(barrier, inc=1, device_id=partner_of(stage), device_id_type=MESH)
-    pl.semaphore_wait(barrier, depth)
+    for mask in masks:
+        pl.semaphore_signal(barrier, inc=1, device_id=device_of(mask), device_id_type=MESH)
+    pl.semaphore_wait(barrier, len(far) + len(masks))
 
     scale = HEAD_DIM**-0.5
     cross_scale = jnp.where(section == 1, scale, 1.0).astype(f32)
@@ -252,8 +284,10 @@
         jnp.sum(jnp.where(domain == d, 1.0, 0.0), axis=1, keepdims=True) for d in range(DOMAINS)
     ]
     counts += [jnp.zeros((1, 1), f32)] * (8 - DOMAINS)
-    stat_s[0, :, CODES:] = jnp.broadcast_to(jnp.concatenate(counts, 0), (8, LANES))
-    stat_s[0, :, :CODES] = mul_t(jnp.ones((8, LANES), bf16), onehot(goal, CODES))
+    stat_s[0, 8:, :] = jnp.broadcast_to(jnp.concatenate(counts, 0), (8, LANES))
+    histogram = mul_t(jnp.ones((8, LANES), bf16), onehot(goal, CODES))
+    for r in range(8):
+        stat_s[0, r : r + 1, :] = histogram[:1, r * LANES : (r + 1) * LANES]
     slot = 0
     for k, stage in enumerate(order):
         slot = slot + side_of(stage) * 2 ** (depth - 1 - k)
@@ -297,7 +331,7 @@
     for block in range(CODES // LANES + 1):
         if block < CODES // LANES:
             rows = x2_s[block * LANES : (block + 1) * LANES, :]
-            table_s[block * LANES : (block + 1) * LANES, :] = rows.astype(bf16)
+            codes_s[block * LANES : (block + 1) * LANES, :] = rows.astype(bf16)
             width = LANES
         else:
             rows = user_s[...]
@@ -427,7 +461,7 @@
     lax.fori_loop(0, chunks, encode, 0)
     for j in range(chunks, depth + 1):
         early_step(j)
-    out_stat_ref[...] = stat_s[depth, :1, :CODES]
+    out_stat_ref[...] = stat_s[depth, :8, :]
 
     def put_blocks(first, value):
         for index in range(value.shape[1] // LANES):
@@ -529,14 +563,14 @@
     y3 = y2 + mul(wn_s[1, :, MIXW + FF :], active)
     inverse3 = inverse_rms(y3)
     final = norm_low(y3, inverse3, gain(6, LANES))
-    logits = mul(table_s[...], final)
+    logits = mul(codes_s[...], final)
     top = jnp.max(logits, axis=0, keepdims=True)
     log_total = top + jnp.log(jnp.sum(jnp.exp(logits - top), axis=0, keepdims=True))
     match = iota(logits.shape, 0) == goal
     picked = jnp.sum(jnp.where(match, logits, 0.0), axis=0, keepdims=True)
     weight = jnp.zeros((1, LANES), f32)
     for d in range(DOMAINS):
-        share = 1.0 / (DOMAINS * jnp.maximum(stat_s[depth, d : d + 1, CODES:], 1.0))
+        share = 1.0 / (DOMAINS * jnp.maximum(stat_s[depth, 8 + d : 9 + d, :], 1.0))
         weight = weight + jnp.where(domain == d, share, 0.0)
     loss = jnp.sum(weight * (log_total - picked), axis=1, keepdims=True)
     back_logits = (
@@ -615,10 +649,9 @@
             hit = jnp.where(offset == b, self_scores[head // 2][:, lanes], 0.0)
             rows_s[head, BUCKETS + b : BUCKETS + b + 1, :] = jnp.sum(hit, axis=0, keepdims=True)
 
-    def reducing(buffer, kept):
+    def reducing(buffer, kept, held, upto):
         steps, at = [], 0
-        held = shares(order[:-1], buffer.shape[0])
-        for k, stage in enumerate(order[:-1]):
+        for k, stage in enumerate(order[:upto]):
             rows, left = held[k], held[k + 1]
             side = side_of(stage)
             if left < rows:
@@ -640,15 +673,22 @@
         buffer[place, :] = total.astype(bf16)
 
     flat_depth = depth - 1
-    land = {}
-    for index, name in enumerate(("rest0", "rest1", "first0", "first1", "codes")):
-        land[name] = lands[index * flat_depth : (index + 1) * flat_depth]
-    land_rest, land_first, land_codes = lands[5 * flat_depth :]
-    rest1 = reducing(rest_s.at[1], land["rest1"])
-    first1 = reducing(first_s.at[1], land["first1"])
-    rest0 = reducing(rest_s.at[0], land["rest0"])
-    first0 = reducing(first_s.at[0], land["first0"])
-    codes = reducing(codes_s, land["codes"])
+    held_rest, held_first, held_codes = shares(dp, REST), shares(dp, FIRST), shares(dp, CODES, 1)
+    land, rest = {}, lands
+    for name, number in (
+        ("rest0", flat_depth),
+        ("rest1", flat_depth),
+        ("first1", flat_depth),
+        ("first0", len(far)),
+        ("codes", len(far)),
+    ):
+        land[name], rest = rest[:number], rest[number:]
+    land_rest, land_first = rest
+    rest1 = reducing(rest_s.at[1], land["rest1"], held_rest, flat_depth)
+    first1 = reducing(first_s.at[1], land["first1"], held_first, flat_depth)
+    rest0 = reducing(rest_s.at[0], land["rest0"], held_rest, flat_depth)
+    first0 = reducing(first_s.at[0], land["first0"], held_first, len(far))
+    codes = reducing(codes_s, land["codes"], held_codes, len(far))
 
     def step1(k):
         if k > 0:
@@ -687,7 +727,6 @@
         return steps
 
     gather_rest = gathering(0, rest1[1], rest1[2])
-    gather_first = gathering(REST, first1[1], first1[2])
 
     def step0(k):
         if k > 0 and k <= flat_depth:
@@ -698,7 +737,7 @@
             cross_rest.start()
         if k == flat_depth + 1:
             squares = settle(cross_rest, rest_s, land_rest, rest1[1], rest1[2][-1], 0)
-            out_square_ref[slot, 0:1, :] = squares / (dp * rest1[2][-1] // REST)
+            own_slot_s[16:17, :] = squares / (dp * rest1[2][-1] // REST)
         if k > flat_depth + 1 and gather_rest[k - flat_depth - 2] is not None:
             gather_rest[k - flat_depth - 2].wait()
         if flat_depth < k < 2 * flat_depth + 1 and gather_rest[k - flat_depth - 1] is not None:
@@ -797,11 +836,15 @@
         user_low_s, out_user_ref.at[span(slot * n, n)], local_sems.at[BLOCKS + 2]
     )
     store_users.start()
+    late = list(range(min(chunks, 2 * flat_depth + 2), 2 * flat_depth + 2))
+    if late:
+        step0(late.pop(0))
 
     ones = jnp.ones((8, LANES), f32)
+    own_slot_s[8:16, :] = jnp.zeros((8, LANES), f32)
     for g in range(7):
-        small_s[0, g : g + 1, :] = mul_exact(ones, ggain_s[g].T)[:1]
-    small_s[0, 7:8, :] = jnp.broadcast_to(loss, (1, LANES))
+        own_slot_s[g : g + 1, :] = mul_exact_t(ones, ggain_s[g])[:1]
+    own_slot_s[7:8, :] = jnp.broadcast_to(loss, (1, LANES))
 
     def bucket_sums(b, carry):
         for head in range(HEADS):
@@ -812,72 +855,127 @@
 
     lax.fori_loop(0, BUCKETS, bucket_sums, 0)
     for head in range(HEADS):
-        small_s[0, 8 + head : 9 + head, :] = mul_exact(ones, rows_s[head].T)[:1]
-    small_s[0, 8 + HEADS :, :] = jnp.zeros((8 - HEADS, LANES), f32)
-
-    small_steps = [remote(small_s.at[k], small_land.at[k], stage) for k, stage in enumerate(order)]
-    small_steps[0].start()
-    done = min(chunks, 2 * flat_depth + 2)
-    for k in range(flat_depth):
+        sums = mul_exact_t(ones, rows_s[head])
+        own_slot_s[8 + head : 9 + head, : 2 * BUCKETS] = sums[:1]
+    own_slot_s[19:, :] = jnp.zeros((5, LANES), f32)
+
+    for k in range(len(far)):
         finish(first0[0], first_s.at[0], land["first0"], k)
         finish(codes[0], codes_s, land["codes"], k)
-        small_steps[k].wait()
-        small_s[k + 1] = small_s[k] + small_land[k]
-        small_steps[k + 1].start()
-        if k + 1 < flat_depth:
+        if k + 1 < len(far):
             begin(first0[0], k + 1)
             begin(codes[0], k + 1)
-        if done < 2 * flat_depth + 2:
-            step0(done)
-            done += 1
-    while done < 2 * flat_depth + 2:
-        step0(done)
-        done += 1
-    at, rows = codes[1], codes[2][-1]
-    left = rows // 2 if rows % 32 == 0 else rows
-    side = side_of(across)
-    cross_first.start()
-    if left < rows:
-        source = codes_s.at[span(at + (1 - side) * left, left)]
-        at = at + side * left
-    else:
-        source = codes_s.at[span(at, rows)]
-    cross_codes = remote(source, land_codes, across)
-    cross_codes.start()
-    squares = settle(cross_first, first_s, land_first, first1[1], first1[2][-1], REST)
-    out_square_ref[slot, 1:2, :] = squares / (dp * first1[2][-1] // FIRST)
-    cross_codes.wait()
-    value = codes_s[span(at, left), :].astype(f32) + land_codes[...].astype(f32)
+
+    first_at, first_left = first0[1], held_first[len(far) + 1 :]
+    codes_at, codes_left = codes[1], held_codes[len(far) + 1 :]
+    size, code_size = first_left[-1], codes_left[-1]
+    mine_first = first_at + shift_of(0, first_left)
+    mine_codes = codes_at + shift_of(0, codes_left)
+    inside, crossing_first, everyone = [], [], []
+    for mask in masks:
+        source = first_s.at[0, span(first_at + shift_of(mask, first_left), size)]
+        copy = remote_to(source, near_first.at[mask], device_of(mask))
+        (crossing_first if mask >> 3 else inside).append(copy)
+    for mask in masks:
+        source = codes_s.at[span(codes_at + shift_of(mask, codes_left), code_size)]
+        everyone.append(remote_to(source, near_codes.at[mask], device_of(mask)))
+    store_users.wait()
+    held = out_user_ref.at[span(slot * n, n)]
+    users_out = [remote_to(held, held, device_of(mask)) for mask in masks]
+
+    @pl.when(section == 0)
+    def _():
+        for copy in inside:
+            copy.start()
+        cross_first.start()
+
+    @pl.when(section == 1)
+    def _():
+        for copy in crossing_first:
+            copy.start()
+
+    for copy in everyone + users_out:
+        copy.start()
+    for step in late:
+        step0(step)
+
+    def keep_first(value):
+        value = value.astype(bf16)
+        out_ref[span(REST + mine_first, size), :] = value
+        value = value.astype(f32)
+        squares = jnp.sum(value * value, axis=0, keepdims=True)
+        own_slot_s[17:18, :] = squares / (dp * size // FIRST)
+
+    @pl.when(section == 0)
+    def _():
+        for copy in inside:
+            copy.wait()
+        for copy in crossing_first:
+            copy.wait_recv()
+        cross_first.wait_send()
+        value = first_s[0, span(mine_first, size), :].astype(f32)
+        for mask in masks:
+            value = value + near_first[mask].astype(f32)
+        keep_first(value)
+
+    @pl.when(section == 1)
+    def _():
+        for copy in crossing_first:
+            copy.wait_send()
+        cross_first.wait_recv()
+        value = first_s[1, span(mine_first, size), :].astype(f32)
+        keep_first(value + land_first[...].astype(f32))
+
+    for copy in everyone:
+        copy.wait()
+    value = codes_s[span(mine_codes, code_size), :].astype(f32)
+    for mask in masks:
+        value = value + near_codes[mask].astype(f32)
     value = value.astype(bf16)
-    out_ref[span(COLS + at, left), :] = value
+    out_ref[span(COLS + mine_codes, code_size), :] = value
     value = value.astype(f32)
     squares = jnp.sum(value * value, axis=0, keepdims=True)
-    out_square_ref[slot, 2:3, :] = squares / (2 * dp * left // CODES)
-    out_square_ref[slot, 3:, :] = jnp.zeros((5, LANES), f32)
-    small_steps[depth - 1].wait()
-    out_small_ref[...] = small_s[depth - 1] + small_land[depth - 1]
-
-    store_users.wait()
-    for j, stage in enumerate(reversed(order)):
+    own_slot_s[18:19, :] = squares / (2 * dp * code_size // CODES)
+
+    store_slot = pltpu.make_async_copy(
+        own_slot_s, out_slot_ref.at[slot], local_sems.at[BLOCKS + 3]
+    )
+    store_slot.start()
+
+    copies = []
+    place = out_ref.at[span(REST + mine_first, size)]
+    code_place = out_ref.at[span(COLS + mine_codes, code_size)]
+    for mask in masks:
+        device = device_of(mask)
+        if not mask >> 3:
+            copies.append(remote_to(place, place, device))
+        copies.append(remote_to(code_place, code_place, device))
+    for copy in copies:
+        copy.start()
+    store_slot.wait()
+    held = out_slot_ref.at[slot]
+    slots_out = [remote_to(held, held, device_of(mask)) for mask in masks]
+    for copy in slots_out:
+        copy.start()
+    copies += slots_out
+    for copy in copies + users_out:
+        copy.wait()
+    for j, k in enumerate(reversed(range(len(far)))):
+        stage = far[k]
         copies = []
-        if j == 0:
-            if left < rows:
-                place = out_ref.at[span(COLS + at, left)]
-                copies.append(remote(place, place, stage))
-                at = at - side * left
-        else:
-            k = flat_depth - j
-            rows, left = codes[2][k], codes[2][k + 1]
-            if left < rows:
-                place = out_ref.at[span(COLS + at, left)]
-                copies.append(remote(place, place, stage))
-                at = at - side_of(stage) * left
-            if gather_first[j - 1] is not None:
-                copies.append(gather_first[j - 1])
-        held = out_square_ref.at[slots_of(j)]
+        if held_first[k + 1] < held_first[k]:
+            place = out_ref.at[span(REST + first_at, held_first[k + 1])]
+            copies.append(remote(place, place, stage))
+            first_at = first_at - side_of(stage) * held_first[k + 1]
+        if held_codes[k + 1] < held_codes[k]:
+            place = out_ref.at[span(COLS + codes_at, held_codes[k + 1])]
+            copies.append(remote(place, place, stage))
+            codes_at = codes_at - side_of(stage) * held_codes[k + 1]
+        slots = 16 * 2**j
+        first_slot = lax.div(slot, slots) * slots
+        held = out_slot_ref.at[pl.ds(first_slot, slots)]
         copies.append(remote(held, held, stage))
-        start_row = lax.div(slot, 2**j) * 2**j * n
-        held = out_user_ref.at[span(start_row, 2**j * n)]
+        held = out_user_ref.at[span(first_slot * n, slots * n)]
         copies.append(remote(held, held, stage))
         for copy in copies:
             copy.start()
@@ -894,27 +992,24 @@
     vmem = pl.BlockSpec(memory_space=pltpu.VMEM)
     smem = pl.BlockSpec(memory_space=pltpu.SMEM)
     hbm = pl.BlockSpec(memory_space=pl.ANY)
-    stat = (8, CODES + LANES)
-    lands = []
-    for rows in (REST, REST, FIRST, FIRST, CODES):
-        held = shares(order[:-1], rows)
-        lands += [pltpu.VMEM((left, D), bf16) for left in held[1:]]
-    last = [shares(order[:-1], rows)[-1] for rows in (REST, FIRST)]
-    last.append(shares(order, CODES)[-1])
-    lands += [pltpu.VMEM((left, D), bf16) for left in last]
-    copies = 16 * depth + 16
+    stat = (16, LANES)
+    held_rest, held_first, held_codes = shares(dp, REST), shares(dp, FIRST), shares(dp, CODES, 1)
+    plane, far = depth - 1, depth - 4
+    sizes = [*held_rest[1:] * 2, *held_first[1:]]
+    sizes += [*held_first[1 : far + 1], *held_codes[1 : far + 1], held_rest[-1], held_first[-1]]
+    lands = [pltpu.VMEM((rows, D), bf16) for rows in sizes]
+    copies = 128 + 16 * depth
     return pl.pallas_call(
         functools.partial(step_kernel, n, dp),
         out_shape=(
             jax.ShapeDtypeStruct((COLS + CODES, D), bf16),
             jax.ShapeDtypeStruct((devices * n, D), bf16),
             jax.ShapeDtypeStruct((devices, 8, LANES), jnp.int32),
-            jax.ShapeDtypeStruct((devices, 8, LANES), f32),
-            jax.ShapeDtypeStruct((16, LANES), f32),
-            jax.ShapeDtypeStruct((1, CODES), f32),
+            jax.ShapeDtypeStruct((devices, 24, LANES), f32),
+            jax.ShapeDtypeStruct((8, LANES), f32),
         ),
         in_specs=[vmem, smem, vmem, vmem, vmem, smem, vmem, hbm, hbm, hbm],
-        out_specs=(vmem, hbm, hbm, vmem, vmem, vmem),
+        out_specs=(vmem, hbm, hbm, hbm, vmem),
         scratch_shapes=[
             pltpu.VMEM((chunks, D, WIDE), f32),
             pltpu.VMEM((chunks, D, WIDE), f32),
@@ -928,7 +1023,6 @@
             pltpu.VMEM((2, D, COLS), bf16),
             pltpu.VMEM((2, COLS, D), bf16),
             pltpu.VMEM((2 * D, CODES + n), bf16),
-            pltpu.VMEM((CODES, D), bf16),
             pltpu.VMEM((7, D, LANES), f32),
             pltpu.VMEM((PAIRS, KEYS, 2 * LANES), f32),
             pltpu.VMEM((PAIRS, LANES, 2 * LANES), f32),
@@ -936,7 +1030,7 @@
             pltpu.VMEM((CODES + n, D), f32),
             pltpu.VMEM((PAIRS, KEYS, 2 * LANES), f32),
             pltpu.VMEM((7, D, LANES), f32),
-            pltpu.VMEM((HEADS, LANES, LANES), f32),
+            pltpu.VMEM((HEADS, 2 * BUCKETS, LANES), f32),
             pltpu.VMEM((n, D), f32),
             pltpu.VMEM((n, LANES), jnp.int32),
             pltpu.VMEM((WIDTH, LANES), bf16),
@@ -948,11 +1042,12 @@
             pltpu.VMEM((CODES, D), bf16),
             pltpu.VMEM((8, LANES), jnp.int32),
             pltpu.VMEM((n, D), bf16),
+            pltpu.VMEM((24, LANES), f32),
             pltpu.VMEM((depth + 1,) + stat, f32),
             pltpu.VMEM((depth,) + stat, f32),
-            pltpu.VMEM((depth, 16, LANES), f32),
-            pltpu.VMEM((depth, 16, LANES), f32),
-            pltpu.SemaphoreType.DMA((BLOCKS + 3,)),
+            pltpu.VMEM((16, held_first[-1], D), bf16),
+            pltpu.VMEM((16, held_codes[-1], D), bf16),
+            pltpu.SemaphoreType.DMA((BLOCKS + 4,)),
             pltpu.SemaphoreType.DMA((copies,)),
             pltpu.SemaphoreType.DMA((copies,)),
         ]
@@ -975,13 +1070,13 @@
 
 
 def update_kernel(*refs):
-    parts_in, big_in, small_in, refs = refs[:6], refs[6:15], refs[15:21], refs[21:]
+    parts_in, big_in, small_in, refs = refs[:5], refs[5:14], refs[14:20], refs[20:]
     loss_ref, norm_ref, section_ref, hist_ref = refs[:4]
     big_out, small_out, low_out, refs = refs[4:13], refs[13:19], refs[19:22], refs[22:]
-    parts, hold, low_hold = refs[:6], refs[6:15], refs[15:18]
-    user_grad, part_sems, in_sems, out_sems = refs[18:]
-    grad_ref, user_ref, ids_ref, square_ref, small_ref, stat_ref = parts
-    arrivals = [pltpu.make_async_copy(parts_in[i], parts[i], part_sems.at[i]) for i in range(6)]
+    parts, hold, low_hold = refs[:5], refs[5:14], refs[14:17]
+    user_grad, part_sems, in_sems, out_sems = refs[17:]
+    grad_ref, user_ref, ids_ref, slot_ref, stat_ref = parts
+    arrivals = [pltpu.make_async_copy(parts_in[i], parts[i], part_sems.at[i]) for i in range(5)]
     loads = [pltpu.make_async_copy(big_in[i], hold[i], in_sems.at[i]) for i in range(9)]
     for load in arrivals[1:] + arrivals[:1] + loads:
         load.start()
@@ -1014,18 +1109,19 @@
     def total(x):
         return jnp.sum(jnp.sum(x, axis=0, keepdims=True), axis=1, keepdims=True)
 
-    devices = square_ref.shape[0]
-    slot = iota((devices, 8, LANES), 0)
-    row = iota((devices, 8, LANES), 1)
-    squares = square_ref[...]
-    side = lax.rem(slot, 2)
-    section_squares = [
-        total(jnp.sum(jnp.where((row < 2) & (side == s), squares, 0.0), axis=0)) for s in range(2)
-    ]
-    rest = total(jnp.sum(jnp.where(row == 2, squares, 0.0), axis=0))
+    def slot_sum(first):
+        def add(i, value):
+            return value + slot_ref[2 * i + first]
+
+        zero = jnp.zeros(slot_ref.shape[1:], f32)
+        return lax.fori_loop(0, slot_ref.shape[0] // 2, add, zero)
+
+    even, odd = slot_sum(0), slot_sum(1)
+    section_squares = [total(x[16:17] + x[17:18]) for x in (even, odd)]
+    small = even[:16] + odd[:16]
+    rest = total(even[18:19] + odd[18:19])
     user_values = user_grad[...]
     rest = rest + total(user_values * user_values)
-    small = small_ref[...]
     lane, line = iota(small.shape, 1), iota(small.shape, 0)
     counted = (line < 7) | ((line > 7) & (lane < 2 * BUCKETS))
     small_kept = jnp.where(counted, small, 0.0)
@@ -1036,10 +1132,9 @@
     norm_ref[0] = norm[0, 0]
     for s in range(2):
         section_ref[s] = jnp.sqrt(section_squares[s])[0, 0]
-    for level in range(LEVELS):
-        hist_ref[level : level + 1, :] = stat_ref[
-            :1, level * CODEBOOK : (level + 1) * CODEBOOK
-        ]
+    for row in range(8):
+        lanes = slice((row % 2) * LANES, (row % 2 + 1) * LANES)
+        hist_ref[row // 2 : row // 2 + 1, lanes] = stat_ref[row : row + 1, :]
 
     outs = adam(
         small_in[0][...], small_in[1][...], small_in[2][...], factor * small[:7], rate_gain, 0.0
@@ -1141,14 +1236,14 @@
         ]
         + [jax.ShapeDtypeStruct(x.shape, f32) for x in big + small]
         + low,
-        in_specs=[hbm] * 15 + [vmem] * 6,
+        in_specs=[hbm] * 14 + [vmem] * 6,
         out_specs=[smem] * 3 + [vmem] + [hbm] * 9 + [vmem] * 6 + [hbm] * 3,
         scratch_shapes=[pltpu.VMEM(x.shape, x.dtype) for x in reduced]
         + [pltpu.VMEM(x.shape, f32) for x in big]
         + [pltpu.VMEM(x.shape, bf16) for x in low]
         + [
             pltpu.VMEM((users, D), f32),
-            pltpu.SemaphoreType.DMA((6,)),
+            pltpu.SemaphoreType.DMA((5,)),
             pltpu.SemaphoreType.DMA((9,)),
             pltpu.SemaphoreType.DMA((pieces,)),
         ],

time: 184 us -> 176 us (0.957)
  Pallas kernels: 183 us -> 175 us
    pallas_call x1, Pallas kernels: 170 us -> 161 us  [gradients(): pl.pallas_call(functools.partial(step_kernel, n, dp), out_shape=(jax.Shap...]
where the time goes in v6:
time: 176 us; the launch traced here: 175 us
  Pallas kernels  175 us (99%)
    pallas_call x1, Pallas kernels, gradients(): pl.pallas_call(functools.partial(step_kernel, n, dp), out_shape=(jax.Shap...  161 us
    pallas_call x1, Pallas kernels, update(): pl.pallas_call(update_kernel, out_shape=[jax.ShapeDtypeStruct((1,), f32),...  13.6 us

profile of v6, /device:TPU:0, one launch (start us, length us, event | category | flops | bytes accessed | tf_op | source)
XLA Modules:
  0.0 175.3 jit_solution(11164968597727095641)
XLA Ops:
  0.7 160.9 %gradients.1 = (bf16[5376,128]{1,0:T(8,128)(2,1)}, bf16[1024,128]{1,0:T(8,128)(2,1)}, s32[32,8,128]{2,1,0:T(8,128)}, f32[32,24,128]{2,1,0:T(8,128)}, f32[8,128]{1,0:T(8,128)}) custom-call(s32[64,80]{1,0:T(8,128)} %refs_0_.1, s32[64]{0:T(128)} %refs_1_.1, s32[1,64]{1,0:T(1,128)} %bitcast.16, s32[4,64]{1,0:T(4,128)} %bitcast.15, s32[1,64]{1,0:T(1,128)} %bitcast.17, ...), custom_call_target="tpu_custom_call" | custom-call | tf_op jit(solution)/shard_map/gradients/pallas_call | solution.py:1002
  161.6 13.6 %update.1 = (f32[1]{0:T(128)}, f32[1]{0:T(128)}, f32[2]{0:T(128)}, f32[4,256]{1,0:T(4,128)}, f32[1,128,2304]{2,1,0:T(8,128)}, /*index=5*/f32[1,128,2304]{2,1,0:T...) custom-call(bf16[5376,128]{1,0:T(8,128)(2,1)} %get-tuple-element.49., ...), custom_call_target="tpu_custom_call" | custom-call | tf_op jit(solution)/shard_map/update/pallas_call | solution.py:1229

commit v7 on v6

--- a/solution.py
+++ b/solution.py
@@ -24,8 +24,11 @@
 COLS = MIXW + 2 * FF
 BLOCKS = COLS // LANES
 KEYS = 96
-GROUP = 4
-WIDE = GROUP * LANES
+GROUP = 8
+PACK = 96
+WIDE = GROUP * PACK
+SPAN = GROUP * LANES
+COLUMNS = WIDE // LANES
 PAIRS = HEADS // 2
 FIRST = 4 * WIDTH
 REST = COLS - FIRST
@@ -100,6 +103,32 @@
 
 def diagonal(both):
     return jnp.concatenate([both[:HEAD_DIM, :LANES], both[HEAD_DIM:, LANES:]], 0)
+
+
+def turn(x, shift):
+    return x if shift % LANES == 0 else pltpu.roll(x, shift % LANES, 1)
+
+
+def pack(tables):
+    lane = iota(tables[0].shape, 1)
+    columns = []
+    for first in range(0, len(tables), 4):
+        turned = [turn(tables[first + i], PACK * i) for i in range(4)]
+        for i in range(3):
+            columns.append(jnp.where(lane < PACK - 32 * i, turned[i], turned[i + 1]))
+    return jnp.concatenate(columns, 1)
+
+
+def unpack(x):
+    lane = iota((x.shape[0], LANES), 1)
+    tables = []
+    for first in range(0, x.shape[1] // LANES, 3):
+        a, b, c = [x[:, (first + i) * LANES : (first + i + 1) * LANES] for i in range(3)]
+        tables.append(a)
+        tables.append(jnp.where(lane < 32, turn(a, 32), turn(b, 32)))
+        tables.append(jnp.where(lane < 64, turn(b, 64), turn(c, 64)))
+        tables.append(turn(c, 96))
+    return tables
 
 
 def stack(both):
@@ -177,9 +206,9 @@
     out_ref, out_user_ref, out_ids_ref, out_slot_ref, out_stat_ref = refs[10:15]
     x0_s, x1_s, x2_s, qkv_s, p_s, o_s, r_s, mem_s, dz_s, wn_s, wt_s, ext_s = refs[15:27]
     gain_s, ebias_s, dbias_s, g0_s, ge_s, gbias_s, ggain_s, rows_s, user_s, ids_s = refs[27:37]
-    cross_s, cross_back_s, pc_s, oc_s, rest_s, first_s, codes_s, slot_s, user_low_s, own_slot_s = refs[37:47]
-    stat_s, stat_land, near_first, near_codes, local_sems, sends, recvs = refs[47:54]
-    lands = refs[54:]
+    cross_s, cross_back_s, pc_s, oc_s, rest_s, first_s, codes_s, slot_s, user_low_s, own_slot_s, id_rows_s, hot_s = refs[37:49]
+    stat_s, stat_land, near_first, near_codes, local_sems, sends, recvs = refs[49:56]
+    lands = refs[56:]
     order = stages(dp)
     across = order[-1]
     depth = len(order)
@@ -267,6 +296,12 @@
     ids = ids_s[...] + ((lane & 3) << 8)
     ids = jnp.where(lane < HIST_LEN - 1, ids, jnp.where(lane == HIST_LEN - 1, CODES + row, -1))
     ids_s[...] = ids
+    packed = []
+    for i in range(GROUP):
+        rows = [ids_s[c * GROUP + i : c * GROUP + i + 1, :] for c in range(chunks)]
+        rows += [jnp.zeros((8 - chunks, LANES), jnp.int32)]
+        packed.append(jnp.concatenate(rows, 0))
+    id_rows_s[...] = pack(packed)
     count = targets_ref.shape[1]
     history, token = iota((count, LANES), 0), iota((count, LANES), 1)
     pick = jnp.where((token >> 2) + section * n == history, 1.0, 0.0)
@@ -342,9 +377,15 @@
         ext_s[:D, lanes] = mul_t(eye, high).astype(bf16)
         ext_s[D:, lanes] = mul_t(eye, low).astype(bf16)
 
+    def find(c):
+        ids = id_rows_s[pl.ds(c, 1), :]
+        for first in range(0, CODES + n, LANES):
+            rows = min(LANES, CODES + n - first)
+            hot_s[first : first + rows, :] = onehot(ids - first, rows)
+
     def lookup(c, carry):
-        ids = jnp.concatenate([ids_s[pl.ds(GROUP * c + i, 1), :] for i in range(GROUP)], 1)
-        both = mul(ext_s[...], onehot(ids, CODES + n))
+        find(c)
+        both = mul(ext_s[...], hot_s[...])
         x0_s[c] = both[:D] + both[D:]
         return carry
 
@@ -408,11 +449,20 @@
         column = gain_s[g]
         return column if width == LANES else jnp.concatenate([column] * (width // LANES), 1)
 
+    def at_chunk(c, step, point, points, count):
+        for j in range(point, count, points):
+            pl.when(c == j // points)(functools.partial(step, j))
+
+    def spread_low(x):
+        return jnp.concatenate([part.astype(bf16) for part in unpack(x)], 1)
+
+    def packed(x):
+        return pack([x[:, i * LANES : (i + 1) * LANES] for i in range(GROUP)])
+
     def encode(c, carry):
-        for j in range(depth + 1):
-            pl.when(c == j)(functools.partial(early_step, j))
+        at_chunk(c, early_step, 0, 2, depth + 1)
         x0 = x0_s[c]
-        h = norm_low(x0, inverse_rms(x0), gain(0, WIDE))
+        h = spread_low(x0 * inverse_rms(x0) * gain(0, WIDE))
         for j in range(3):
             part = slice(j * WIDTH, (j + 1) * WIDTH)
             qkv_s[c, part, :] = mul(wt_s[0, part, :], h).astype(bf16)
@@ -429,8 +479,9 @@
                 )
                 p_s[GROUP * c + i, j] = chance
                 o_s[c, part, lanes] = mixed
-        x1 = x0 + mul(wn_s[0, :, 3 * WIDTH : 4 * WIDTH], o_s[c])
+        x1 = x0 + packed(mul(wn_s[0, :, 3 * WIDTH : 4 * WIDTH], o_s[c]))
         x1_s[c] = x1
+        at_chunk(c, early_step, 1, 2, depth + 1)
         pl.when(c == 0)(rest_arrives)
         h = norm_low(x1, inverse_rms(x1), gain(1, WIDE))
         for j in range(2):
@@ -448,18 +499,18 @@
         return carry
 
     def put_wide(ref, c, value):
-        for i in range(GROUP):
-            ref[pl.ds(pl.multiple_of((GROUP * c + i) * D, D), D), :] = value[
+        for i in range(COLUMNS):
+            ref[pl.ds(pl.multiple_of((COLUMNS * c + i) * D, D), D), :] = value[
                 :, i * LANES : (i + 1) * LANES
             ]
 
     def get_wide(ref, c):
         return jnp.concatenate(
-            [ref[pl.ds(pl.multiple_of((GROUP * c + i) * D, D), D), :] for i in range(GROUP)], 1
+            [ref[pl.ds(pl.multiple_of((COLUMNS * c + i) * D, D), D), :] for i in range(COLUMNS)], 1
         )
 
     lax.fori_loop(0, chunks, encode, 0)
-    for j in range(chunks, depth + 1):
+    for j in range(2 * chunks, depth + 1):
         early_step(j)
     out_stat_ref[...] = stat_s[depth, :8, :]
 
@@ -503,10 +554,14 @@
     h1 = norm_low(y1, inverse1, gain(4, LANES))
     cross_s[...] = mul(wt_s[1, 4 * WIDTH : 5 * WIDTH, :], h1).astype(bf16)
 
+    def spreader(g, turned):
+        shape = (LANES, 32 * GROUP) if turned else (32 * GROUP, LANES)
+        row, token = iota(shape, 1 if turned else 0), iota(shape, 0 if turned else 1)
+        hit = token == 4 * GROUP * g + 4 * (row >> 5) + (row & 3)
+        return jnp.where(hit, 1.0, 0.0).astype(bf16)
+
     def rows_of(g, table):
-        row, token = iota((LANES, LANES), 0), iota((LANES, LANES), 1)
-        rep = jnp.where(token == 16 * g + 4 * (row >> 5) + (row & 3), 1.0, 0.0).astype(bf16)
-        rows = mul_t(rep, table)
+        rows = mul_t(spreader(g, False), table)
         mask = (iota(rows.shape, 1) >> 6) == ((iota(rows.shape, 0) & 31) >> 2)
         return jnp.where(mask, rows, 0.0).astype(bf16)
 
@@ -514,32 +569,41 @@
         return (iota(shape, 0) >> 6) == ((iota(shape, 1) & 31) >> 2)
 
     def rows_t_of(g, table):
-        token, row = iota((LANES, LANES), 0), iota((LANES, LANES), 1)
-        rep = jnp.where(token == 16 * g + 4 * (row >> 5) + (row & 3), 1.0, 0.0).astype(bf16)
-        rows = mul(table, rep)
+        rows = mul(table, spreader(g, True))
         return jnp.where(head_mask(rows.shape), rows, 0.0).astype(bf16)
 
     def gather_rows(ref):
         total = jnp.zeros((WIDTH, LANES), f32)
         for g in range(chunks):
-            row, token = iota((LANES, LANES), 0), iota((LANES, LANES), 1)
-            rep = jnp.where(token == 16 * g + 4 * (row >> 5) + (row & 3), 1.0, 0.0).astype(bf16)
-            total = total + mul(ref[g], rep)
+            total = total + mul(ref[g], spreader(g, False))
         return total.astype(bf16)
 
     def blocks_of(table):
-        owner = iota(table.shape, 0) >> 5
-        zero = jnp.zeros_like(table)
-        return jnp.concatenate(
-            [jnp.where(owner == j, table, zero) for j in range(GROUP)], 1
-        ).astype(bf16)
+        rows = []
+        for i in range(GROUP):
+            part = table[32 * i : 32 * i + 32]
+            column, shift = divmod(PACK * i, LANES)
+            part = turn(part, shift)
+            lane = iota(part.shape, 1)
+            zero = jnp.zeros_like(part)
+            columns = [zero] * COLUMNS
+            columns[column] = jnp.where(lane >= shift, part, 0.0)
+            if shift > LANES - PACK:
+                columns[column + 1] = jnp.where(lane < shift, part, 0.0)
+            rows.append(jnp.concatenate(columns, 1))
+        return jnp.concatenate(rows, 0).astype(bf16)
 
     def row_products(rows, ref, g, first):
+        both = mul(rows, ref[g, first : first + WIDTH, :])
         parts = []
-        for j in range(0, GROUP, 2):
-            pair = slice(j * LANES, (j + 2) * LANES)
-            both = mul(rows[32 * j : 32 * j + 64], ref[g, first : first + WIDTH, pair])
-            parts += [both[:32, :LANES], both[32:, LANES:]]
+        for i in range(GROUP):
+            own = both[32 * i : 32 * i + 32]
+            column, shift = divmod(PACK * i, LANES)
+            part = turn(own[:, column * LANES : (column + 1) * LANES], -shift)
+            if shift > LANES - PACK:
+                after = turn(own[:, (column + 1) * LANES : (column + 2) * LANES], -shift)
+                part = jnp.where(iota(part.shape, 1) < LANES - shift, part, after)
+            parts.append(part)
         return jnp.concatenate(parts, 0)
 
     def cross(g, carry):
@@ -596,6 +660,7 @@
     def cross_back(g, carry):
         mixed_rows = rows_of(g, cross_back_s[...])
         back_chance = row_products(mixed_rows, mem_s, g, WIDTH)
+        back_chance = jnp.where(iota(back_chance.shape, 1) < HIST_LEN, back_chance, 0.0)
         chance = pc_s[g]
         inner = jnp.sum(back_chance * chance, axis=1, keepdims=True)
         spread = blocks_of(chance * (back_chance - inner))
@@ -749,11 +814,10 @@
         ggain_s[g] = jnp.zeros((D, LANES), f32)
 
     def fold(x):
-        return sum(x[:, i * LANES : (i + 1) * LANES] for i in range(GROUP))
+        return sum(x[:, i * LANES : (i + 1) * LANES] for i in range(COLUMNS))
 
     def back_rest(c, carry):
-        for j in range(flat_depth + 1):
-            pl.when(c == j)(functools.partial(step1, j))
+        at_chunk(c, step1, 0, 2, flat_depth + 1)
         x2 = get_wide(x2_s, c)
         inverse = inverse_rms(x2)
         back_memory = mem_s[c]
@@ -763,34 +827,42 @@
         )
         ggain_s[2] += fold(gain_grad)
         low = back.astype(bf16)
-        active = r_s[c]
-        add_blocks(26, mul_t(low, active))
-        back_active = mul(wt_s[0, MIXW + FF :, :], low)
-        back_lifted = jnp.where(active.astype(f32) > 0, back_active, 0.0).astype(bf16)
+        add_blocks(26, mul_t(low, r_s[c]))
+        for j in range(4):
+            part = slice(j * FF // 4, (j + 1) * FF // 4)
+            back_active = mul(wt_s[0, MIXW + FF + part.start : MIXW + FF + part.stop, :], low)
+            live = r_s[c, part, :].astype(f32) > 0
+            r_s[c, part, :] = jnp.where(live, back_active, 0.0).astype(bf16)
+        at_chunk(c, step1, 1, 2, flat_depth + 1)
         x1 = x1_s[c]
         inverse = inverse_rms(x1)
-        add_blocks(18, mul_t(norm_low(x1, inverse, gain(1, WIDE)), back_lifted))
+        add_blocks(18, mul_t(norm_low(x1, inverse, gain(1, WIDE)), r_s[c]))
         more, gain_grad = norm_back(
-            x1, inverse, gain(1, WIDE), mul(wn_s[0, :, MIXW : MIXW + FF], back_lifted)
+            x1, inverse, gain(1, WIDE), mul(wn_s[0, :, MIXW : MIXW + FF], r_s[c])
         )
         ggain_s[1] += fold(gain_grad)
         put_wide(x2_s, c, back + more)
         return carry
 
     lax.fori_loop(0, chunks, back_rest, 0)
-    for j in range(chunks, flat_depth + 1):
+    for j in range(2 * chunks, flat_depth + 1):
         step1(j)
     for block in range(REST // D):
         rest_s[0, block * D : (block + 1) * D, :] = g0_s[FIRST // D + block].astype(bf16)
 
+    steps0 = 2 * flat_depth + 2
+
     def back_first(c, carry):
-        for j in range(min(chunks, 2 * flat_depth + 2)):
-            pl.when(c == j)(functools.partial(step0, j))
+        at_chunk(c, step0, 0, 3, steps0)
         back = get_wide(x2_s, c)
-        low = back.astype(bf16)
+        lane = iota((D, LANES), 1)
+        low = [jnp.where(lane < PACK, part, 0.0).astype(bf16) for part in unpack(back)]
+        low = jnp.concatenate(low, 1)
         add_blocks(9, mul_t(low, o_s[c]))
-        back_mixed = mul(wt_s[0, 3 * WIDTH : 4 * WIDTH, :], low).astype(bf16)
+        o_s[c] = mul(wt_s[0, 3 * WIDTH : 4 * WIDTH, :], low).astype(bf16)
         for i in range(GROUP):
+            if i == GROUP // 2:
+                at_chunk(c, step0, 1, 3, steps0)
             lanes = slice(i * LANES, (i + 1) * LANES)
             for j in range(PAIRS):
                 part = slice(j * LANES, (j + 1) * LANES)
@@ -800,24 +872,22 @@
                     qkv_s[c, keys, lanes],
                     qkv_s[c, part, lanes],
                     qkv_s[c, values, lanes].T[:KEYS],
-                    back_mixed[part, lanes],
+                    o_s[c, part, lanes],
                     p_s[GROUP * c + i, j],
                 )
-                mem_s[c, part, lanes] = one
-                mem_s[c, keys, lanes] = two
-                r_s[c, part, lanes] = three
+                qkv_s[c, part, lanes] = one
+                qkv_s[c, keys, lanes] = two
+                qkv_s[c, values, lanes] = three
                 gbias_s[j] += scores
+        at_chunk(c, step0, 2, 3, steps0)
         x0 = x0_s[c]
         inverse = inverse_rms(x0)
-        h = norm_low(x0, inverse, gain(0, WIDE))
-        add_blocks(0, mul_t(h, mem_s[c]))
-        add_blocks(6, mul_t(h, r_s[c, :WIDTH, :]))
-        back_normed = mul(wn_s[0, :, : 2 * WIDTH], mem_s[c])
-        back_normed = back_normed + mul(wn_s[0, :, 2 * WIDTH : 3 * WIDTH], r_s[c, :WIDTH, :])
+        add_blocks(0, mul_t(spread_low(x0 * inverse * gain(0, WIDE)), qkv_s[c]))
+        back_normed = packed(mul(wn_s[0, :, : 3 * WIDTH], qkv_s[c]))
         more, gain_grad = norm_back(x0, inverse, gain(0, WIDE), back_normed)
         ggain_s[0] += fold(gain_grad)
-        ids = jnp.concatenate([ids_s[pl.ds(GROUP * c + i, 1), :] for i in range(GROUP)], 1)
-        spread = mul_t(onehot(ids, CODES + n), split_low(back + more))
+        find(c)
+        spread = mul_t(hot_s[...], split_low(back + more))
         ge_s[...] += spread[:, :D] + spread[:, D:]
         return carry
 
@@ -836,7 +906,7 @@
         user_low_s, out_user_ref.at[span(slot * n, n)], local_sems.at[BLOCKS + 2]
     )
     store_users.start()
-    late = list(range(min(chunks, 2 * flat_depth + 2), 2 * flat_depth + 2))
+    late = list(range(min(3 * chunks, steps0), steps0))
     if late:
         step0(late.pop(0))
 
@@ -1013,10 +1083,10 @@
         scratch_shapes=[
             pltpu.VMEM((chunks, D, WIDE), f32),
             pltpu.VMEM((chunks, D, WIDE), f32),
-            pltpu.VMEM((n * D, LANES), f32),
-            pltpu.VMEM((chunks, 3 * WIDTH, WIDE), bf16),
+            pltpu.VMEM((chunks * COLUMNS * D, LANES), f32),
+            pltpu.VMEM((chunks, 3 * WIDTH, SPAN), bf16),
             pltpu.VMEM((n, PAIRS, KEYS, 2 * LANES), bf16),
-            pltpu.VMEM((chunks, WIDTH, WIDE), bf16),
+            pltpu.VMEM((chunks, WIDTH, SPAN), bf16),
             pltpu.VMEM((chunks, FF, WIDE), bf16),
             pltpu.VMEM((chunks, 2 * WIDTH, WIDE), bf16),
             pltpu.VMEM((3 * WIDTH, 2 * LANES), bf16),
@@ -1035,14 +1105,16 @@
             pltpu.VMEM((n, LANES), jnp.int32),
             pltpu.VMEM((WIDTH, LANES), bf16),
             pltpu.VMEM((WIDTH, LANES), bf16),
-            pltpu.VMEM((chunks, LANES, LANES), f32),
-            pltpu.VMEM((chunks, WIDTH, LANES), bf16),
+            pltpu.VMEM((chunks, 32 * GROUP, LANES), f32),
+            pltpu.VMEM((chunks, WIDTH, 32 * GROUP), bf16),
             pltpu.VMEM((2, REST, D), bf16),
             pltpu.VMEM((2, FIRST, D), bf16),
             pltpu.VMEM((CODES, D), bf16),
             pltpu.VMEM((8, LANES), jnp.int32),
             pltpu.VMEM((n, D), bf16),
             pltpu.VMEM((24, LANES), f32),
+            pltpu.VMEM((8, WIDE), jnp.int32),
+            pltpu.VMEM((CODES + n, WIDE), bf16),
             pltpu.VMEM((depth + 1,) + stat, f32),
             pltpu.VMEM((depth,) + stat, f32),
             pltpu.VMEM((16, held_first[-1], D), bf16),

time: 176 us -> 175 us (level)
  no operation moved by 1% of the time
where the time goes in v7:
time: 175 us
  Pallas kernels  174 us (99%)
    pallas_call x1, Pallas kernels, gradients(): pl.pallas_call(functools.partial(step_kernel, n, dp), out_shape=(jax.Shap...  161 us
    pallas_call x1, Pallas kernels, update(): pl.pallas_call(update_kernel, out_shape=[jax.ShapeDtypeStruct((1,), f32),...  13.6 us

profile of v7, /device:TPU:0, one launch (start us, length us, event | category | flops | bytes accessed | tf_op | source)
XLA Modules:
  0.0 175.1 jit_solution(11125946450690311546)
XLA Ops:
  0.7 160.7 %gradients.1 = (bf16[5376,128]{1,0:T(8,128)(2,1)}, bf16[1024,128]{1,0:T(8,128)(2,1)}, s32[32,8,128]{2,1,0:T(8,128)}, f32[32,24,128]{2,1,0:T(8,128)}, f32[8,128]{1,0:T(8,128)}) custom-call(s32[64,80]{1,0:T(8,128)} %refs_0_.1, s32[64]{0:T(128)} %refs_1_.1, s32[1,64]{1,0:T(1,128)} %bitcast.16, s32[4,64]{1,0:T(4,128)} %bitcast.15, s32[1,64]{1,0:T(1,128)} %bitcast.17, ...), custom_call_target="tpu_custom_call" | custom-call | tf_op jit(solution)/shard_map/gradients/pallas_call | solution.py:1072
  161.4 13.6 %update.1 = (f32[1]{0:T(128)}, f32[1]{0:T(128)}, f32[2]{0:T(128)}, f32[4,256]{1,0:T(4,128)}, f32[1,128,2304]{2,1,0:T(8,128)}, /*index=5*/f32[1,128,2304]{2,1,0:T...) custom-call(bf16[5376,128]{1,0:T(8,128)(2,1)} %get-tuple-element.49., ...), custom_call_target="tpu_custom_call" | custom-call | tf_op jit(solution)/shard_map/update/pallas_call | solution.py:1301

commit v8 on v7

--- a/solution.py
+++ b/solution.py
@@ -25,6 +25,7 @@
 BLOCKS = COLS // LANES
 KEYS = 96
 GROUP = 8
+BATCH = 2
 PACK = 96
 WIDE = GROUP * PACK
 SPAN = GROUP * LANES
@@ -142,27 +143,39 @@
     return jnp.concatenate([table, zero], 0)
 
 
-def attend(keys, query, values, bias):
-    scores = mul(keys, block_diag(query)) + bias
+def columns_of(table, i):
+    return table[:, 2 * i * LANES : 2 * (i + 1) * LANES]
+
+
+def attend(keys, queries, values, bias):
+    scores = [mul(key, block_diag(query)) for key, query in zip(keys, queries)]
+    scores = jnp.concatenate(scores, 1) + bias
     top = jnp.max(scores, axis=0, keepdims=True)
     chance = jnp.exp(scores - top)
     total = jnp.sum(chance, axis=0, keepdims=True)
     chance = (chance * (1.0 / total)).astype(bf16)
-    mixed = diagonal(mul(values, pad_keys(chance))).astype(bf16)
-    return chance, mixed
-
-
-def attend_back(keys_t, query, values, back_mixed, chance):
+    full = pad_keys(chance)
+    mixed = [mul(value, columns_of(full, i)) for i, value in enumerate(values)]
+    return chance, [diagonal(both).astype(bf16) for both in mixed]
+
+
+def attend_back(keys_t, queries, values, back_mixed, chance):
     exact = chance.astype(f32)
-    spread = block_diag(back_mixed)
-    back_chance = mul(values, spread)
+    back_chance = [mul(value, block_diag(back)) for value, back in zip(values, back_mixed)]
+    back_chance = jnp.concatenate(back_chance, 1)
     inner = jnp.sum(back_chance * exact, axis=0, keepdims=True)
     back_scores = exact * (back_chance - inner)
     low = pad_keys(back_scores.astype(bf16))
-    back_query = diagonal(mul(keys_t, low)).astype(bf16)
-    back_keys = diagonal(mul_t(query, stack(low))).astype(bf16)
-    back_values = diagonal(mul_t(back_mixed, stack(pad_keys(chance)))).astype(bf16)
-    return back_query, back_keys, back_values, back_scores
+    full = pad_keys(chance)
+    count = range(len(queries))
+    back_query = [mul(keys_t[i], columns_of(low, i)) for i in count]
+    back_keys = [mul_t(queries[i], stack(columns_of(low, i))) for i in count]
+    back_values = [mul_t(back_mixed[i], stack(columns_of(full, i))) for i in count]
+    results = [
+        [diagonal(both).astype(bf16) for both in part]
+        for part in (back_query, back_keys, back_values)
+    ]
+    return *results, back_scores
 
 
 def split_low(x):
@@ -206,9 +219,9 @@
     out_ref, out_user_ref, out_ids_ref, out_slot_ref, out_stat_ref = refs[10:15]
     x0_s, x1_s, x2_s, qkv_s, p_s, o_s, r_s, mem_s, dz_s, wn_s, wt_s, ext_s = refs[15:27]
     gain_s, ebias_s, dbias_s, g0_s, ge_s, gbias_s, ggain_s, rows_s, user_s, ids_s = refs[27:37]
-    cross_s, cross_back_s, pc_s, oc_s, rest_s, first_s, codes_s, slot_s, user_low_s, own_slot_s, id_rows_s, hot_s = refs[37:49]
-    stat_s, stat_land, near_first, near_codes, local_sems, sends, recvs = refs[49:56]
-    lands = refs[56:]
+    cross_s, cross_back_s, pc_s, oc_s, rest_s, first_s, codes_s, slot_s, user_low_s, own_slot_s, id_rows_s, hot_s, dqkv_s = refs[37:50]
+    stat_s, stat_land, near_first, near_codes, local_sems, sends, recvs = refs[50:57]
+    lands = refs[57:]
     order = stages(dp)
     across = order[-1]
     depth = len(order)
@@ -407,22 +420,22 @@
     buckets = nearby + jnp.where(key > query, 16, 0)
     real = iota((KEYS, LANES), 0) < HIST_LEN
     for head in range(HEADS):
-        lanes = slice((head % 2) * LANES, (head % 2 + 1) * LANES)
+        lanes = slice(head * LANES, (head + 1) * LANES)
 
         def choose(b, table):
             return jnp.where(buckets == b, bias_ref[head, 0, b], table)
 
         table = lax.fori_loop(0, BUCKETS, choose, jnp.zeros((KEYS, LANES), f32))
-        ebias_s[head // 2, :, lanes] = jnp.where(real, table, -1e30)
+        ebias_s[:, lanes] = jnp.where(real, table, -1e30)
     key, query = iota((LANES, LANES), 0), iota((LANES, LANES), 1)
     offset = query - key
     seen = ((key >> 2) == (query >> 2)) & (offset >= 0)
     for head in range(HEADS):
-        lanes = slice((head % 2) * LANES, (head % 2 + 1) * LANES)
+        lanes = slice(head * LANES, (head + 1) * LANES)
         table = jnp.full((LANES, LANES), -1e30, f32)
         for b in range(LEVELS):
             table = jnp.where(seen & (offset == b), bias_ref[head, 1, b], table)
-        dbias_s[head // 2, :, lanes] = table
+        dbias_s[:, lanes] = table
 
     def transpose_weights(which, first, last):
         for block in range(first, last):
@@ -459,6 +472,9 @@
     def packed(x):
         return pack([x[:, i * LANES : (i + 1) * LANES] for i in range(GROUP)])
 
+    def part_of(j):
+        return slice(j * LANES, (j + 1) * LANES)
+
     def encode(c, carry):
         at_chunk(c, early_step, 0, 2, depth + 1)
         x0 = x0_s[c]
@@ -466,19 +482,19 @@
         for j in range(3):
             part = slice(j * WIDTH, (j + 1) * WIDTH)
             qkv_s[c, part, :] = mul(wt_s[0, part, :], h).astype(bf16)
-        for i in range(GROUP):
-            lanes = slice(i * LANES, (i + 1) * LANES)
-            for j in range(PAIRS):
-                part = slice(j * LANES, (j + 1) * LANES)
-                keys = slice(WIDTH + j * LANES, WIDTH + (j + 1) * LANES)
-                chance, mixed = attend(
-                    qkv_s[c, keys, lanes].T[:KEYS],
-                    qkv_s[c, part, lanes],
-                    qkv_s[c, 2 * WIDTH + j * LANES : 2 * WIDTH + (j + 1) * LANES, lanes],
-                    ebias_s[j],
-                )
-                p_s[GROUP * c + i, j] = chance
-                o_s[c, part, lanes] = mixed
+        for first in range(0, GROUP, BATCH):
+            queries, keys, values = [], [], []
+            for i in range(first, first + BATCH):
+                lanes = slice(i * LANES, (i + 1) * LANES)
+                queries += [qkv_s[c, part_of(j), lanes] for j in range(PAIRS)]
+                keys += [qkv_s[c, part_of(PAIRS + j), lanes].T[:KEYS] for j in range(PAIRS)]
+                values += [qkv_s[c, part_of(2 * PAIRS + j), lanes] for j in range(PAIRS)]
+            bias = jnp.concatenate([ebias_s[...]] * BATCH, 1)
+            chance, mixed = attend(keys, queries, values, bias)
+            for i in range(BATCH):
+                lanes = slice((first + i) * LANES, (first + i + 1) * LANES)
+                p_s[GROUP * c + first + i] = chance[:, i * HEADS * LANES : (i + 1) * HEADS * LANES]
+                o_s[c, :, lanes] = jnp.concatenate(mixed[i * PAIRS : (i + 1) * PAIRS], 0)
         x1 = x0 + packed(mul(wn_s[0, :, 3 * WIDTH : 4 * WIDTH], o_s[c]))
         x1_s[c] = x1
         at_chunk(c, early_step, 1, 2, depth + 1)
@@ -535,20 +551,14 @@
     h0 = norm_low(y0, inverse0, gain(3, LANES))
     dz_s[:, :LANES] = mul(wt_s[1, : 3 * WIDTH, :], h0).astype(bf16)
     both = mul(mul_t(eye, h0).astype(bf16), wn_s[1, :, WIDTH : 3 * WIDTH]).astype(bf16)
-    self_chance = []
-    mixed_parts = []
-    for j in range(PAIRS):
-        part = slice(j * LANES, (j + 1) * LANES)
-        chance, mixed = attend(
-            both[:, part],
-            dz_s[part, :LANES],
-            dz_s[2 * WIDTH + j * LANES : 2 * WIDTH + (j + 1) * LANES, :LANES],
-            dbias_s[j],
-        )
-        self_chance.append(chance)
-        mixed_parts.append(mixed)
+    self_chance, mixed = attend(
+        [both[:, part_of(j)] for j in range(PAIRS)],
+        [dz_s[part_of(j), :LANES] for j in range(PAIRS)],
+        [dz_s[part_of(2 * PAIRS + j), :LANES] for j in range(PAIRS)],
+        dbias_s[...],
+    )
     self_values = both[:, WIDTH:]
-    self_mixed = jnp.concatenate(mixed_parts, 0)
+    self_mixed = jnp.concatenate(mixed, 0)
     y1 = y0 + mul(wn_s[1, :, 3 * WIDTH : 4 * WIDTH], self_mixed)
     inverse1 = inverse_rms(y1)
     h1 = norm_low(y1, inverse1, gain(4, LANES))
@@ -681,22 +691,14 @@
     low = back.astype(bf16)
     put_blocks(9, mul_t(low, self_mixed))
     back_mixed = mul(wt_s[1, 3 * WIDTH : 4 * WIDTH, :], low).astype(bf16)
-    self_scores = []
-    for j in range(PAIRS):
-        part = slice(j * LANES, (j + 1) * LANES)
-        keys = slice(WIDTH + j * LANES, WIDTH + (j + 1) * LANES)
-        values = slice(2 * WIDTH + j * LANES, 2 * WIDTH + (j + 1) * LANES)
-        one, two, three, scores = attend_back(
-            dz_s[keys, :LANES],
-            dz_s[part, :LANES],
-            self_values[:, part],
-            back_mixed[part],
-            self_chance[j],
-        )
-        dz_s[part, LANES : 2 * LANES] = one
-        dz_s[keys, LANES : 2 * LANES] = two
-        dz_s[values, LANES : 2 * LANES] = three
-        self_scores.append(scores)
+    *back_parts, self_scores = attend_back(
+        [dz_s[part_of(PAIRS + j), :LANES] for j in range(PAIRS)],
+        [dz_s[part_of(j), :LANES] for j in range(PAIRS)],
+        [self_values[:, part_of(j)] for j in range(PAIRS)],
+        [back_mixed[part_of(j)] for j in range(PAIRS)],
+        self_chance,
+    )
+    dz_s[:, LANES:] = jnp.concatenate([x for part in back_parts for x in part], 0)
     put_blocks(0, mul_t(h0, dz_s[:WIDTH, LANES : 2 * LANES]) * HEAD_DIM**-0.5)
     put_blocks(3, mul_t(h0, dz_s[WIDTH:, LANES : 2 * LANES]))
     more, gain_grad = norm_back(
@@ -709,9 +711,9 @@
     ge_s[CODES:, :] = jnp.zeros((n, D), f32)
     rows_s[...] = jnp.zeros_like(rows_s)
     for head in range(HEADS):
-        lanes = slice((head % 2) * LANES, (head % 2 + 1) * LANES)
+        lanes = slice(head * LANES, (head + 1) * LANES)
         for b in range(LEVELS):
-            hit = jnp.where(offset == b, self_scores[head // 2][:, lanes], 0.0)
+            hit = jnp.where(offset == b, self_scores[:, lanes], 0.0)
             rows_s[head, BUCKETS + b : BUCKETS + b + 1, :] = jnp.sum(hit, axis=0, keepdims=True)
 
     def reducing(buffer, kept, held, upto):
@@ -860,30 +862,31 @@
         low = jnp.concatenate(low, 1)
         add_blocks(9, mul_t(low, o_s[c]))
         o_s[c] = mul(wt_s[0, 3 * WIDTH : 4 * WIDTH, :], low).astype(bf16)
-        for i in range(GROUP):
-            if i == GROUP // 2:
+        for first in range(0, GROUP, BATCH):
+            if first == GROUP // 2:
                 at_chunk(c, step0, 1, 3, steps0)
-            lanes = slice(i * LANES, (i + 1) * LANES)
-            for j in range(PAIRS):
-                part = slice(j * LANES, (j + 1) * LANES)
-                keys = slice(WIDTH + j * LANES, WIDTH + (j + 1) * LANES)
-                values = slice(2 * WIDTH + j * LANES, 2 * WIDTH + (j + 1) * LANES)
-                one, two, three, scores = attend_back(
-                    qkv_s[c, keys, lanes],
-                    qkv_s[c, part, lanes],
-                    qkv_s[c, values, lanes].T[:KEYS],
-                    o_s[c, part, lanes],
-                    p_s[GROUP * c + i, j],
-                )
-                qkv_s[c, part, lanes] = one
-                qkv_s[c, keys, lanes] = two
-                qkv_s[c, values, lanes] = three
-                gbias_s[j] += scores
+            queries, keys, values, backs = [], [], [], []
+            for i in range(first, first + BATCH):
+                lanes = slice(i * LANES, (i + 1) * LANES)
+                queries += [qkv_s[c, part_of(j), lanes] for j in range(PAIRS)]
+                keys += [qkv_s[c, part_of(PAIRS + j), lanes] for j in range(PAIRS)]
+                values += [qkv_s[c, part_of(2 * PAIRS + j), lanes].T[:KEYS] for j in range(PAIRS)]
+                backs += [o_s[c, part_of(j), lanes] for j in range(PAIRS)]
+            chance = [p_s[GROUP * c + first + i] for i in range(BATCH)]
+            *results, scores = attend_back(
+                keys, queries, values, backs, jnp.concatenate(chance, 1)
+            )
+            for i in range(BATCH):
+                lanes = slice((first + i) * LANES, (first + i + 1) * LANES)
+                own = slice(i * PAIRS, (i + 1) * PAIRS)
+                dqkv_s[:, lanes] = jnp.concatenate([x for part in results for x in part[own]], 0)
+            width = HEADS * LANES
+            gbias_s[...] += sum(scores[:, i * width : (i + 1) * width] for i in range(BATCH))
         at_chunk(c, step0, 2, 3, steps0)
         x0 = x0_s[c]
         inverse = inverse_rms(x0)
-        add_blocks(0, mul_t(spread_low(x0 * inverse * gain(0, WIDE)), qkv_s[c]))
-        back_normed = packed(mul(wn_s[0, :, : 3 * WIDTH], qkv_s[c]))
+        add_blocks(0, mul_t(spread_low(x0 * inverse * gain(0, WIDE)), dqkv_s[...]))
+        back_normed = packed(mul(wn_s[0, :, : 3 * WIDTH], dqkv_s[...]))
         more, gain_grad = norm_back(x0, inverse, gain(0, WIDE), back_normed)
         ggain_s[0] += fold(gain_grad)
         find(c)
@@ -918,8 +921,8 @@
 
     def bucket_sums(b, carry):
         for head in range(HEADS):
-            lanes = slice((head % 2) * LANES, (head % 2 + 1) * LANES)
-            hit = jnp.where(buckets == b, gbias_s[head // 2, :, lanes], 0.0)
+            lanes = slice(head * LANES, (head + 1) * LANES)
+            hit = jnp.where(buckets == b, gbias_s[:, lanes], 0.0)
             rows_s[head, pl.ds(b, 1), :] = jnp.sum(hit, axis=0, keepdims=True)
         return carry
 
@@ -1085,7 +1088,7 @@
             pltpu.VMEM((chunks, D, WIDE), f32),
             pltpu.VMEM((chunks * COLUMNS * D, LANES), f32),
             pltpu.VMEM((chunks, 3 * WIDTH, SPAN), bf16),
-            pltpu.VMEM((n, PAIRS, KEYS, 2 * LANES), bf16),
+            pltpu.VMEM((n, KEYS, HEADS * LANES), bf16),
             pltpu.VMEM((chunks, WIDTH, SPAN), bf16),
             pltpu.VMEM((chunks, FF, WIDE), bf16),
             pltpu.VMEM((chunks, 2 * WIDTH, WIDE), bf16),
@@ -1094,11 +1097,11 @@
             pltpu.VMEM((2, COLS, D), bf16),
             pltpu.VMEM((2 * D, CODES + n), bf16),
             pltpu.VMEM((7, D, LANES), f32),
-            pltpu.VMEM((PAIRS, KEYS, 2 * LANES), f32),
-            pltpu.VMEM((PAIRS, LANES, 2 * LANES), f32),
+            pltpu.VMEM((KEYS, HEADS * LANES), f32),
+            pltpu.VMEM((LANES, HEADS * LANES), f32),
             pltpu.VMEM((BLOCKS, D, LANES), f32),
             pltpu.VMEM((CODES + n, D), f32),
-            pltpu.VMEM((PAIRS, KEYS, 2 * LANES), f32),
+            pltpu.VMEM((KEYS, HEADS * LANES), f32),
             pltpu.VMEM((7, D, LANES), f32),
             pltpu.VMEM((HEADS, 2 * BUCKETS, LANES), f32),
             pltpu.VMEM((n, D), f32),
@@ -1115,6 +1118,7 @@
             pltpu.VMEM((24, LANES), f32),
             pltpu.VMEM((8, WIDE), jnp.int32),
             pltpu.VMEM((CODES + n, WIDE), bf16),
+            pltpu.VMEM((3 * WIDTH, SPAN), bf16),
             pltpu.VMEM((depth + 1,) + stat, f32),
             pltpu.VMEM((depth,) + stat, f32),
             pltpu.VMEM((16, held_first[-1], D), bf16),

time: 175 us -> 167 us (0.954)
  Pallas kernels: 174 us -> 166 us
    pallas_call x1, Pallas kernels: 161 us -> 152 us  [gradients(): pl.pallas_call(functools.partial(step_kernel, n, dp), out_shape=(jax.Shap...]
where the time goes in v8:
time: 167 us
  Pallas kernels  166 us (99%)
    pallas_call x1, Pallas kernels, gradients(): pl.pallas_call(functools.partial(step_kernel, n, dp), out_shape=(jax.Shap...  152 us
    pallas_call x1, Pallas kernels, update(): pl.pallas_call(update_kernel, out_shape=[jax.ShapeDtypeStruct((1,), f32),...  13.8 us

profile of v8, /device:TPU:0, one launch (start us, length us, event | category | flops | bytes accessed | tf_op | source)
XLA Modules:
  0.0 166.6 jit_solution(3973117086949770072)
XLA Ops:
  0.7 152.0 %gradients.1 = (bf16[5376,128]{1,0:T(8,128)(2,1)}, bf16[1024,128]{1,0:T(8,128)(2,1)}, s32[32,8,128]{2,1,0:T(8,128)}, f32[32,24,128]{2,1,0:T(8,128)}, f32[8,128]{1,0:T(8,128)}) custom-call(s32[64,80]{1,0:T(8,128)} %refs_0_.1, s32[64]{0:T(128)} %refs_1_.1, s32[1,64]{1,0:T(1,128)} %bitcast.16, s32[4,64]{1,0:T(4,128)} %bitcast.15, s32[1,64]{1,0:T(1,128)} %bitcast.17, ...), custom_call_target="tpu_custom_call" | custom-call | tf_op jit(solution)/shard_map/gradients/pallas_call | solution.py:1075
  152.6 13.8 %update.1 = (f32[1]{0:T(128)}, f32[1]{0:T(128)}, f32[2]{0:T(128)}, f32[4,256]{1,0:T(4,128)}, f32[1,128,2304]{2,1,0:T(8,128)}, /*index=5*/f32[1,128,2304]{2,1,0:T...) custom-call(bf16[5376,128]{1,0:T(8,128)(2,1)} %get-tuple-element.49., ...), custom_call_target="tpu_custom_call" | custom-call | tf_op jit(solution)/shard_map/update/pallas_call | solution.py:1305

commit v9 on v8

--- a/solution.py
+++ b/solution.py
@@ -26,6 +26,7 @@
 KEYS = 96
 GROUP = 8
 BATCH = 2
+NEAR = 3
 PACK = 96
 WIDE = GROUP * PACK
 SPAN = GROUP * LANES
@@ -185,8 +186,7 @@
 
 def stages(dp):
     bits = [2**k for k in range(dp.bit_length() - 1)]
-    near = bits[1:4]
-    return [("dp", bit) for bit in bits[:1] + bits[4:] + near] + [("pipe", 1)]
+    return [("dp", bit) for bit in bits[:2] + bits[4:] + bits[2:4]] + [("pipe", 1)]
 
 
 def side_of(stage):
@@ -203,7 +203,7 @@
     held = [rows]
     depth = len(stages(dp)) - 1
     for k in range(depth + across):
-        later = min(3, depth - 1 - k) + across if k < depth else 0
+        later = min(NEAR - 1, depth - 1 - k) + across if k < depth else 0
         half = held[-1] // 2
         held.append(half if half % (16 * 2**later) == 0 else held[-1])
     return held
@@ -244,7 +244,7 @@
     def remote(source, target, stage):
         return remote_to(source, target, partner_of(stage))
 
-    near, far = order[-4:], order[:-4]
+    near, far = order[-NEAR:], order[:-NEAR]
     masks = range(1, 2 ** len(near))
 
     def device_of(mask):
@@ -281,7 +281,6 @@
         pl.semaphore_signal(barrier, inc=1, device_id=partner_of(stage), device_id_type=MESH)
     for mask in masks:
         pl.semaphore_signal(barrier, inc=1, device_id=device_of(mask), device_id_type=MESH)
-    pl.semaphore_wait(barrier, len(far) + len(masks))
 
     scale = HEAD_DIM**-0.5
     cross_scale = jnp.where(section == 1, scale, 1.0).astype(f32)
@@ -294,6 +293,7 @@
         elif 12 <= block < 15:
             value = value * cross_scale
         wn_s[section, :, block * LANES : (block + 1) * LANES] = value.astype(bf16)
+    pl.semaphore_wait(barrier, len(far) + len(masks))
     half = D // 2
     mine = span(side_of(order[0]) * half, half)
     pieces = (slice(0, FIRST), slice(FIRST, COLS))
@@ -375,7 +375,7 @@
         user_s[pl.ds(i, 1), :] = x2_s[pl.ds(CODES + users_ref[section * n + i], 1), :]
         return carry
 
-    lax.fori_loop(0, n, fetch, 0)
+    lax.fori_loop(0, n, fetch, 0, unroll=8)
     for block in range(CODES // LANES + 1):
         if block < CODES // LANES:
             rows = x2_s[block * LANES : (block + 1) * LANES, :]
@@ -404,6 +404,13 @@
 
     lax.fori_loop(0, chunks, lookup, 0)
 
+    beside = []
+    for piece in pieces:
+        came = wn_s.at[1 - section, mine, piece]
+        beside.append(remote(came, came, order[0]))
+    over[0].wait()
+    beside[0].start()
+
     for g in range(7):
         gain_s[g] = jnp.broadcast_to(gains_ref[g : g + 1, :], (LANES, LANES)).T
 
@@ -425,7 +432,7 @@
         def choose(b, table):
             return jnp.where(buckets == b, bias_ref[head, 0, b], table)
 
-        table = lax.fori_loop(0, BUCKETS, choose, jnp.zeros((KEYS, LANES), f32))
+        table = lax.fori_loop(0, BUCKETS, choose, jnp.zeros((KEYS, LANES), f32), unroll=True)
         ebias_s[:, lanes] = jnp.where(real, table, -1e30)
     key, query = iota((LANES, LANES), 0), iota((LANES, LANES), 1)
     offset = query - key
@@ -442,12 +449,6 @@
             place = slice(block * LANES, (block + 1) * LANES)
             wt_s[which, place, :] = wn_s[which, :, place].T
 
-    beside = []
-    for piece in pieces:
-        came = wn_s.at[1 - section, mine, piece]
-        beside.append(remote(came, came, order[0]))
-    over[0].wait()
-    beside[0].start()
     transpose_weights(section, 0, BLOCKS)
     beside[0].wait()
     transpose_weights(1 - section, 0, FIRST // LANES)
@@ -627,7 +628,7 @@
         oc_s[g] = jnp.where(head_mask(mixed.shape), mixed, 0.0).astype(bf16)
         return carry
 
-    lax.fori_loop(0, chunks, cross, 0)
+    lax.fori_loop(0, chunks, cross, 0, unroll=True)
     cross_mixed = gather_rows(oc_s)
     y2 = y1 + mul(wn_s[1, :, 5 * WIDTH : 6 * WIDTH], cross_mixed)
     inverse2 = inverse_rms(y2)
@@ -680,7 +681,7 @@
         oc_s[g] = jnp.where(head_mask(total.shape), total, 0.0).astype(bf16)
         return carry
 
-    lax.fori_loop(0, chunks, cross_back, 0)
+    lax.fori_loop(0, chunks, cross_back, 0, unroll=True)
     back_query = gather_rows(oc_s)
     put_blocks(12, mul_t(h1, back_query) * HEAD_DIM**-0.5)
     more, gain_grad = norm_back(
@@ -926,7 +927,7 @@
             rows_s[head, pl.ds(b, 1), :] = jnp.sum(hit, axis=0, keepdims=True)
         return carry
 
-    lax.fori_loop(0, BUCKETS, bucket_sums, 0)
+    lax.fori_loop(0, BUCKETS, bucket_sums, 0, unroll=4)
     for head in range(HEADS):
         sums = mul_exact_t(ones, rows_s[head])
         own_slot_s[8 + head : 9 + head, : 2 * BUCKETS] = sums[:1]
@@ -948,7 +949,7 @@
     for mask in masks:
         source = first_s.at[0, span(first_at + shift_of(mask, first_left), size)]
         copy = remote_to(source, near_first.at[mask], device_of(mask))
-        (crossing_first if mask >> 3 else inside).append(copy)
+        (crossing_first if mask >> (NEAR - 1) else inside).append(copy)
     for mask in masks:
         source = codes_s.at[span(codes_at + shift_of(mask, codes_left), code_size)]
         everyone.append(remote_to(source, near_codes.at[mask], device_of(mask)))
@@ -1020,7 +1021,7 @@
     code_place = out_ref.at[span(COLS + mine_codes, code_size)]
     for mask in masks:
         device = device_of(mask)
-        if not mask >> 3:
+        if not mask >> (NEAR - 1):
             copies.append(remote_to(place, place, device))
         copies.append(remote_to(code_place, code_place, device))
     for copy in copies:
@@ -1044,7 +1045,7 @@
             place = out_ref.at[span(COLS + codes_at, held_codes[k + 1])]
             copies.append(remote(place, place, stage))
             codes_at = codes_at - side_of(stage) * held_codes[k + 1]
-        slots = 16 * 2**j
+        slots = 2 ** (NEAR + j)
         first_slot = lax.div(slot, slots) * slots
         held = out_slot_ref.at[pl.ds(first_slot, slots)]
         copies.append(remote(held, held, stage))
@@ -1067,7 +1068,7 @@
     hbm = pl.BlockSpec(memory_space=pl.ANY)
     stat = (16, LANES)
     held_rest, held_first, held_codes = shares(dp, REST), shares(dp, FIRST), shares(dp, CODES, 1)
-    plane, far = depth - 1, depth - 4
+    plane, far = depth - 1, depth - NEAR
     sizes = [*held_rest[1:] * 2, *held_first[1:]]
     sizes += [*held_first[1 : far + 1], *held_codes[1 : far + 1], held_rest[-1], held_first[-1]]
     lands = [pltpu.VMEM((rows, D), bf16) for rows in sizes]
@@ -1121,8 +1122,8 @@
             pltpu.VMEM((3 * WIDTH, SPAN), bf16),
             pltpu.VMEM((depth + 1,) + stat, f32),
             pltpu.VMEM((depth,) + stat, f32),
-            pltpu.VMEM((16, held_first[-1], D), bf16),
-            pltpu.VMEM((16, held_codes[-1], D), bf16),
+            pltpu.VMEM((2**NEAR, held_first[-1], D), bf16),
+            pltpu.VMEM((2**NEAR, held_codes[-1], D), bf16),
             pltpu.SemaphoreType.DMA((BLOCKS + 4,)),
             pltpu.SemaphoreType.DMA((copies,)),
             pltpu.SemaphoreType.DMA((copies,)),
@@ -1141,7 +1142,10 @@
     unbiased_moment = moment * (1 / (1 - beta_one**STEP))
     unbiased_square = square * (1 / (1 - beta_two**STEP))
     root = unbiased_square * lax.rsqrt(unbiased_square)
-    step = unbiased_moment / (root + adam_eps) + decay * weight
+    divisor = root + adam_eps
+    inverse = pl.reciprocal(divisor, approx=True)
+    inverse = inverse * (2.0 - divisor * inverse)
+    step = unbiased_moment * inverse + decay * weight
     return weight - rate * step, moment, square
 
 

time: 167 us -> 165 us (0.988)
  Pallas kernels: 166 us -> 163 us
    pallas_call x1, Pallas kernels: 152 us -> 149 us  [gradients(): pl.pallas_call(functools.partial(step_kernel, n, dp), out_shape=(jax.Shap...]
where the time goes in v9:
time: 165 us; the launch traced here: 164 us
  Pallas kernels  163 us (99%)
    pallas_call x1, Pallas kernels, gradients(): pl.pallas_call(functools.partial(step_kernel, n, dp), out_shape=(jax.Shap...  149 us
    pallas_call x1, Pallas kernels, update(): pl.pallas_call(update_kernel, out_shape=[jax.ShapeDtypeStruct((1,), f32),...  13.8 us

profile of v9, /device:TPU:0, one launch (start us, length us, event | category | flops | bytes accessed | tf_op | source)
XLA Modules:
  0.0 163.9 jit_solution(3151742976021906228)
XLA Ops:
  0.7 149.2 %gradients.1 = (bf16[5376,128]{1,0:T(8,128)(2,1)}, bf16[1024,128]{1,0:T(8,128)(2,1)}, s32[32,8,128]{2,1,0:T(8,128)}, f32[32,24,128]{2,1,0:T(8,128)}, f32[8,128]{1,0:T(8,128)}) custom-call(s32[64,80]{1,0:T(8,128)} %refs_0_.1, s32[64]{0:T(128)} %refs_1_.1, s32[1,64]{1,0:T(1,128)} %bitcast.16, s32[4,64]{1,0:T(4,128)} %bitcast.15, s32[1,64]{1,0:T(1,128)} %bitcast.17, ...), custom_call_target="tpu_custom_call" | custom-call | tf_op jit(solution)/shard_map/gradients/pallas_call | solution.py:1076
  149.9 13.8 %update.1 = (f32[1]{0:T(128)}, f32[1]{0:T(128)}, f32[2]{0:T(128)}, f32[4,256]{1,0:T(4,128)}, f32[1,128,2304]{2,1,0:T(8,128)}, /*index=5*/f32[1,128,2304]{2,1,0:T...) custom-call(bf16[5376,128]{1,0:T(8,128)(2,1)} %get-tuple-element.49., ...), custom_call_target="tpu_custom_call" | custom-call | tf_op jit(solution)/shard_map/update/pallas_call | solution.py:1309

commit v10 on v9

--- a/solution.py
+++ b/solution.py
@@ -473,6 +473,9 @@
     def packed(x):
         return pack([x[:, i * LANES : (i + 1) * LANES] for i in range(GROUP)])
 
+    def lanes_of(i):
+        return pl.ds(pl.multiple_of(i * LANES, LANES), LANES)
+
     def part_of(j):
         return slice(j * LANES, (j + 1) * LANES)
 
@@ -483,19 +486,23 @@
         for j in range(3):
             part = slice(j * WIDTH, (j + 1) * WIDTH)
             qkv_s[c, part, :] = mul(wt_s[0, part, :], h).astype(bf16)
-        for first in range(0, GROUP, BATCH):
+        def attention(b, carry):
             queries, keys, values = [], [], []
-            for i in range(first, first + BATCH):
-                lanes = slice(i * LANES, (i + 1) * LANES)
+            for i in range(BATCH):
+                lanes = lanes_of(b * BATCH + i)
                 queries += [qkv_s[c, part_of(j), lanes] for j in range(PAIRS)]
                 keys += [qkv_s[c, part_of(PAIRS + j), lanes].T[:KEYS] for j in range(PAIRS)]
                 values += [qkv_s[c, part_of(2 * PAIRS + j), lanes] for j in range(PAIRS)]
             bias = jnp.concatenate([ebias_s[...]] * BATCH, 1)
             chance, mixed = attend(keys, queries, values, bias)
             for i in range(BATCH):
-                lanes = slice((first + i) * LANES, (first + i + 1) * LANES)
-                p_s[GROUP * c + first + i] = chance[:, i * HEADS * LANES : (i + 1) * HEADS * LANES]
-                o_s[c, :, lanes] = jnp.concatenate(mixed[i * PAIRS : (i + 1) * PAIRS], 0)
+                own = slice(i * HEADS * LANES, (i + 1) * HEADS * LANES)
+                p_s[GROUP * c + b * BATCH + i] = chance[:, own]
+                both = jnp.concatenate(mixed[i * PAIRS : (i + 1) * PAIRS], 0)
+                o_s[c, :, lanes_of(b * BATCH + i)] = both
+            return carry
+
+        lax.fori_loop(0, GROUP // BATCH, attention, 0)
         x1 = x0 + packed(mul(wn_s[0, :, 3 * WIDTH : 4 * WIDTH], o_s[c]))
         x1_s[c] = x1
         at_chunk(c, early_step, 1, 2, depth + 1)
@@ -863,26 +870,30 @@
         low = jnp.concatenate(low, 1)
         add_blocks(9, mul_t(low, o_s[c]))
         o_s[c] = mul(wt_s[0, 3 * WIDTH : 4 * WIDTH, :], low).astype(bf16)
-        for first in range(0, GROUP, BATCH):
-            if first == GROUP // 2:
-                at_chunk(c, step0, 1, 3, steps0)
+        def attention(b, carry):
+            for j in range(1, steps0, 3):
+                now = (c == j // 3) & (b == GROUP // BATCH // 2)
+                pl.when(now)(functools.partial(step0, j))
             queries, keys, values, backs = [], [], [], []
-            for i in range(first, first + BATCH):
-                lanes = slice(i * LANES, (i + 1) * LANES)
+            for i in range(BATCH):
+                lanes = lanes_of(b * BATCH + i)
                 queries += [qkv_s[c, part_of(j), lanes] for j in range(PAIRS)]
                 keys += [qkv_s[c, part_of(PAIRS + j), lanes] for j in range(PAIRS)]
                 values += [qkv_s[c, part_of(2 * PAIRS + j), lanes].T[:KEYS] for j in range(PAIRS)]
                 backs += [o_s[c, part_of(j), lanes] for j in range(PAIRS)]
-            chance = [p_s[GROUP * c + first + i] for i in range(BATCH)]
+            chance = [p_s[GROUP * c + b * BATCH + i] for i in range(BATCH)]
             *results, scores = attend_back(
                 keys, queries, values, backs, jnp.concatenate(chance, 1)
             )
             for i in range(BATCH):
-                lanes = slice((first + i) * LANES, (first + i + 1) * LANES)
                 own = slice(i * PAIRS, (i + 1) * PAIRS)
-                dqkv_s[:, lanes] = jnp.concatenate([x for part in results for x in part[own]], 0)
+                both = jnp.concatenate([x for part in results for x in part[own]], 0)
+                dqkv_s[:, lanes_of(b * BATCH + i)] = both
             width = HEADS * LANES
             gbias_s[...] += sum(scores[:, i * width : (i + 1) * width] for i in range(BATCH))
+            return carry
+
+        lax.fori_loop(0, GROUP // BATCH, attention, 0)
         at_chunk(c, step0, 2, 3, steps0)
         x0 = x0_s[c]
         inverse = inverse_rms(x0)

time: 165 us -> 168 us (1.018)
  Pallas kernels: 163 us -> 167 us
    pallas_call x1, Pallas kernels: 149 us -> 153 us  [gradients(): pl.pallas_call(functools.partial(step_kernel, n, dp), out_shape=(jax.Shap...]
where the time goes in v10:
time: 168 us
  Pallas kernels  167 us (99%)
    pallas_call x1, Pallas kernels, gradients(): pl.pallas_call(functools.partial(step_kernel, n, dp), out_shape=(jax.Shap...  153 us
    pallas_call x1, Pallas kernels, update(): pl.pallas_call(update_kernel, out_shape=[jax.ShapeDtypeStruct((1,), f32),...  13.8 us

profile of v10, /device:TPU:0, one launch (start us, length us, event | category | flops | bytes accessed | tf_op | source)
XLA Modules:
  0.0 167.8 jit_solution(11538616347491454267)
XLA Ops:
  0.7 153.1 %gradients.1 = (bf16[5376,128]{1,0:T(8,128)(2,1)}, bf16[1024,128]{1,0:T(8,128)(2,1)}, s32[32,8,128]{2,1,0:T(8,128)}, f32[32,24,128]{2,1,0:T(8,128)}, f32[8,128]{1,0:T(8,128)}) custom-call(s32[64,80]{1,0:T(8,128)} %refs_0_.1, s32[64]{0:T(128)} %refs_1_.1, s32[1,64]{1,0:T(1,128)} %bitcast.16, s32[4,64]{1,0:T(4,128)} %bitcast.15, s32[1,64]{1,0:T(1,128)} %bitcast.17, ...), custom_call_target="tpu_custom_call" | custom-call | tf_op jit(solution)/shard_map/gradients/pallas_call | solution.py:1087
  153.8 13.8 %update.1 = (f32[1]{0:T(128)}, f32[1]{0:T(128)}, f32[2]{0:T(128)}, f32[4,256]{1,0:T(4,128)}, f32[1,128,2304]{2,1,0:T(8,128)}, /*index=5*/f32[1,128,2304]{2,1,0:T...) custom-call(bf16[5376,128]{1,0:T(8,128)(2,1)} %get-tuple-element.49., ...), custom_call_target="tpu_custom_call" | custom-call | tf_op jit(solution)/shard_map/update/pallas_call | solution.py:1320

commit v11 on v9

--- a/solution.py
+++ b/solution.py
@@ -217,11 +217,13 @@
     codes_ref, users_ref, user_row_ref, targets_ref, domains_ref, bias_ref, gains_ref = refs[:7]
     mixer_ref, feed_ref, embed_ref = refs[7:10]
     out_ref, out_user_ref, out_ids_ref, out_slot_ref, out_stat_ref = refs[10:15]
-    x0_s, x1_s, x2_s, qkv_s, p_s, o_s, r_s, mem_s, dz_s, wn_s, wt_s, ext_s = refs[15:27]
-    gain_s, ebias_s, dbias_s, g0_s, ge_s, gbias_s, ggain_s, rows_s, user_s, ids_s = refs[27:37]
-    cross_s, cross_back_s, pc_s, oc_s, rest_s, first_s, codes_s, slot_s, user_low_s, own_slot_s, id_rows_s, hot_s, dqkv_s = refs[37:50]
-    stat_s, stat_land, near_first, near_codes, local_sems, sends, recvs = refs[50:57]
-    lands = refs[57:]
+    x0_s, x1_s, qkv_s, p_s, o_s, r_s, mem_s, dqkv_s = [refs[15 + 2 * i : 17 + 2 * i] for i in range(8)]
+    refs = refs[31:]
+    x2_s, dz_s, wn_s, wt_s, ext_s = refs[:5]
+    gain_s, ebias_s, dbias_s, g0_s, ge_s, gbias_s, ggain_s, rows_s, user_s, ids_s = refs[5:15]
+    cross_s, cross_back_s, pc_s, oc_s, rest_s, first_s, codes_s, slot_s, user_low_s, own_slot_s, id_rows_s, hot_s = refs[15:27]
+    stat_s, stat_land, near_first, near_codes, local_sems, sends, recvs = refs[27:34]
+    lands = refs[34:]
     order = stages(dp)
     across = order[-1]
     depth = len(order)
@@ -396,13 +398,13 @@
             rows = min(LANES, CODES + n - first)
             hot_s[first : first + rows, :] = onehot(ids - first, rows)
 
-    def lookup(c, carry):
+    def lookup(c):
         find(c)
         both = mul(ext_s[...], hot_s[...])
-        x0_s[c] = both[:D] + both[D:]
-        return carry
-
-    lax.fori_loop(0, chunks, lookup, 0)
+        x0_s[c % 2][c // 2] = both[:D] + both[D:]
+
+    for c in range(chunks):
+        lookup(c)
 
     beside = []
     for piece in pieces:
@@ -463,9 +465,15 @@
         column = gain_s[g]
         return column if width == LANES else jnp.concatenate([column] * (width // LANES), 1)
 
-    def at_chunk(c, step, point, points, count):
-        for j in range(point, count, points):
-            pl.when(c == j // points)(functools.partial(step, j))
+    def lockstep(steps, point=None):
+        for number, _ in enumerate(zip(*steps)):
+            if point is not None:
+                point(number)
+
+    def at_time(t, steps):
+        for time, step in enumerate(steps):
+            if step is not None:
+                pl.when(t == time)(step)
 
     def spread_low(x):
         return jnp.concatenate([part.astype(bf16) for part in unpack(x)], 1)
@@ -476,43 +484,73 @@
     def part_of(j):
         return slice(j * LANES, (j + 1) * LANES)
 
-    def encode(c, carry):
-        at_chunk(c, early_step, 0, 2, depth + 1)
-        x0 = x0_s[c]
+    def encode_steps(t, half):
+        c = 2 * t + half
+        qkv, o, r = qkv_s[half], o_s[half], r_s[half]
+        x0 = x0_s[half][t]
         h = spread_low(x0 * inverse_rms(x0) * gain(0, WIDE))
+        yield
         for j in range(3):
             part = slice(j * WIDTH, (j + 1) * WIDTH)
-            qkv_s[c, part, :] = mul(wt_s[0, part, :], h).astype(bf16)
+            qkv[t, part, :] = mul(wt_s[0, part, :], h).astype(bf16)
+        yield
         for first in range(0, GROUP, BATCH):
             queries, keys, values = [], [], []
             for i in range(first, first + BATCH):
                 lanes = slice(i * LANES, (i + 1) * LANES)
-                queries += [qkv_s[c, part_of(j), lanes] for j in range(PAIRS)]
-                keys += [qkv_s[c, part_of(PAIRS + j), lanes].T[:KEYS] for j in range(PAIRS)]
-                values += [qkv_s[c, part_of(2 * PAIRS + j), lanes] for j in range(PAIRS)]
+                queries += [qkv[t, part_of(j), lanes] for j in range(PAIRS)]
+                keys += [qkv[t, part_of(PAIRS + j), lanes].T[:KEYS] for j in range(PAIRS)]
+                values += [qkv[t, part_of(2 * PAIRS + j), lanes] for j in range(PAIRS)]
             bias = jnp.concatenate([ebias_s[...]] * BATCH, 1)
             chance, mixed = attend(keys, queries, values, bias)
             for i in range(BATCH):
                 lanes = slice((first + i) * LANES, (first + i + 1) * LANES)
-                p_s[GROUP * c + first + i] = chance[:, i * HEADS * LANES : (i + 1) * HEADS * LANES]
-                o_s[c, :, lanes] = jnp.concatenate(mixed[i * PAIRS : (i + 1) * PAIRS], 0)
-        x1 = x0 + packed(mul(wn_s[0, :, 3 * WIDTH : 4 * WIDTH], o_s[c]))
-        x1_s[c] = x1
-        at_chunk(c, early_step, 1, 2, depth + 1)
-        pl.when(c == 0)(rest_arrives)
+                own = slice(i * HEADS * LANES, (i + 1) * HEADS * LANES)
+                p_s[half][t, first + i] = chance[:, own]
+                o[t, :, lanes] = jnp.concatenate(mixed[i * PAIRS : (i + 1) * PAIRS], 0)
+            yield
+        x1 = x0 + packed(mul(wn_s[0, :, 3 * WIDTH : 4 * WIDTH], o[t]))
+        x1_s[half][t] = x1
+        yield
         h = norm_low(x1, inverse_rms(x1), gain(1, WIDE))
         for j in range(2):
             part = slice(j * FF // 2, (j + 1) * FF // 2)
             lifted = mul(wt_s[0, MIXW + j * FF // 2 : MIXW + (j + 1) * FF // 2, :], h)
-            r_s[c, part, :] = jnp.maximum(lifted, 0.0).astype(bf16)
-        x2 = x1 + mul(wn_s[0, :, MIXW + FF :], r_s[c])
+            r[t, part, :] = jnp.maximum(lifted, 0.0).astype(bf16)
+        yield
+        x2 = x1 + mul(wn_s[0, :, MIXW + FF :], r[t])
         put_wide(x2_s, c, x2)
         e = norm_low(x2, inverse_rms(x2), gain(2, WIDE))
+        yield
         for j in range(2):
             part = slice(j * WIDTH, (j + 1) * WIDTH)
-            mem_s[c, part, :] = mul(
+            mem_s[half][t, part, :] = mul(
                 wt_s[0, 4 * WIDTH + j * WIDTH : 4 * WIDTH + (j + 1) * WIDTH, :], e
             ).astype(bf16)
+        yield
+
+    attention = GROUP // BATCH
+    pairs = chunks // 2
+
+    def early_at(place, places):
+        return [
+            functools.partial(early_step, place + places * t)
+            if place + places * t <= depth
+            else None
+            for t in range(pairs)
+        ]
+
+    def encode(t, carry):
+        at_time(t, early_at(0, 3))
+
+        def point(number):
+            if number == attention // 2:
+                at_time(t, early_at(1, 3))
+            if number == attention + 2:
+                pl.when(t == 0)(rest_arrives)
+                at_time(t, early_at(2, 3))
+
+        lockstep([encode_steps(t, 0), encode_steps(t, 1)], point)
         return carry
 
     def put_wide(ref, c, value):
@@ -526,8 +564,8 @@
             [ref[pl.ds(pl.multiple_of((COLUMNS * c + i) * D, D), D), :] for i in range(COLUMNS)], 1
         )
 
-    lax.fori_loop(0, chunks, encode, 0)
-    for j in range(2 * chunks, depth + 1):
+    lax.fori_loop(0, pairs, encode, 0)
+    for j in range(3 * pairs, depth + 1):
         early_step(j)
     out_stat_ref[...] = stat_s[depth, :8, :]
 
@@ -604,8 +642,8 @@
             rows.append(jnp.concatenate(columns, 1))
         return jnp.concatenate(rows, 0).astype(bf16)
 
-    def row_products(rows, ref, g, first):
-        both = mul(rows, ref[g, first : first + WIDTH, :])
+    def row_products(rows, g, first):
+        both = mul(rows, mem_s[g % 2][g // 2, first : first + WIDTH, :])
         parts = []
         for i in range(GROUP):
             own = both[32 * i : 32 * i + 32]
@@ -617,18 +655,18 @@
             parts.append(part)
         return jnp.concatenate(parts, 0)
 
-    def cross(g, carry):
+    def cross(g):
         queries = rows_of(g, cross_s[...])
-        scores = row_products(queries, mem_s, g, 0)
+        scores = row_products(queries, g, 0)
         scores = jnp.where(iota(scores.shape, 1) < HIST_LEN, scores, -1e30)
         chance = jnp.exp(scores - jnp.max(scores, axis=1, keepdims=True))
         chance = chance * (1.0 / jnp.sum(chance, axis=1, keepdims=True))
         pc_s[g] = chance
-        mixed = mul_t(mem_s[g, WIDTH:, :], blocks_of(chance))
+        mixed = mul_t(mem_s[g % 2][g // 2, WIDTH:, :], blocks_of(chance))
         oc_s[g] = jnp.where(head_mask(mixed.shape), mixed, 0.0).astype(bf16)
-        return carry
-
-    lax.fori_loop(0, chunks, cross, 0, unroll=True)
+
+    for g in range(chunks):
+        cross(g)
     cross_mixed = gather_rows(oc_s)
     y2 = y1 + mul(wn_s[1, :, 5 * WIDTH : 6 * WIDTH], cross_mixed)
     inverse2 = inverse_rms(y2)
@@ -668,20 +706,20 @@
     put_blocks(15, mul_t(low, cross_mixed))
     cross_back_s[...] = mul(wt_s[1, 5 * WIDTH : 6 * WIDTH, :], low).astype(bf16)
 
-    def cross_back(g, carry):
+    def cross_back(g):
         mixed_rows = rows_of(g, cross_back_s[...])
-        back_chance = row_products(mixed_rows, mem_s, g, WIDTH)
+        back_chance = row_products(mixed_rows, g, WIDTH)
         back_chance = jnp.where(iota(back_chance.shape, 1) < HIST_LEN, back_chance, 0.0)
         chance = pc_s[g]
         inner = jnp.sum(back_chance * chance, axis=1, keepdims=True)
         spread = blocks_of(chance * (back_chance - inner))
-        total = mul_t(mem_s[g, :WIDTH, :], spread)
-        mem_s[g, :WIDTH, :] = mul(rows_t_of(g, cross_s[...]), spread).astype(bf16)
-        mem_s[g, WIDTH:, :] = mul(rows_t_of(g, cross_back_s[...]), blocks_of(chance)).astype(bf16)
+        total = mul_t(mem_s[g % 2][g // 2, :WIDTH, :], spread)
+        mem_s[g % 2][g // 2, :WIDTH, :] = mul(rows_t_of(g, cross_s[...]), spread).astype(bf16)
+        mem_s[g % 2][g // 2, WIDTH:, :] = mul(rows_t_of(g, cross_back_s[...]), blocks_of(chance)).astype(bf16)
         oc_s[g] = jnp.where(head_mask(total.shape), total, 0.0).astype(bf16)
-        return carry
-
-    lax.fori_loop(0, chunks, cross_back, 0, unroll=True)
+
+    for g in range(chunks):
+        cross_back(g)
     back_query = gather_rows(oc_s)
     put_blocks(12, mul_t(h1, back_query) * HEAD_DIM**-0.5)
     more, gain_grad = norm_back(
@@ -819,83 +857,119 @@
     def fold(x):
         return sum(x[:, i * LANES : (i + 1) * LANES] for i in range(COLUMNS))
 
-    def back_rest(c, carry):
-        at_chunk(c, step1, 0, 2, flat_depth + 1)
+    def rest_steps(t, half):
+        c = 2 * t + half
+        r = r_s[half]
         x2 = get_wide(x2_s, c)
         inverse = inverse_rms(x2)
-        back_memory = mem_s[c]
+        back_memory = mem_s[half][t]
         add_blocks(12, mul_t(norm_low(x2, inverse, gain(2, WIDE)), back_memory))
-        back, gain_grad = norm_back(
-            x2, inverse, gain(2, WIDE), mul(wn_s[0, :, 4 * WIDTH : 6 * WIDTH], back_memory)
-        )
+        back_normed = mul(wn_s[0, :, 4 * WIDTH : 6 * WIDTH], back_memory)
+        yield
+        back, gain_grad = norm_back(x2, inverse, gain(2, WIDE), back_normed)
         ggain_s[2] += fold(gain_grad)
         low = back.astype(bf16)
-        add_blocks(26, mul_t(low, r_s[c]))
+        yield
+        add_blocks(26, mul_t(low, r[t]))
         for j in range(4):
             part = slice(j * FF // 4, (j + 1) * FF // 4)
             back_active = mul(wt_s[0, MIXW + FF + part.start : MIXW + FF + part.stop, :], low)
-            live = r_s[c, part, :].astype(f32) > 0
-            r_s[c, part, :] = jnp.where(live, back_active, 0.0).astype(bf16)
-        at_chunk(c, step1, 1, 2, flat_depth + 1)
-        x1 = x1_s[c]
+            live = r[t, part, :].astype(f32) > 0
+            r[t, part, :] = jnp.where(live, back_active, 0.0).astype(bf16)
+        yield
+        x1 = x1_s[half][t]
         inverse = inverse_rms(x1)
-        add_blocks(18, mul_t(norm_low(x1, inverse, gain(1, WIDE)), r_s[c]))
-        more, gain_grad = norm_back(
-            x1, inverse, gain(1, WIDE), mul(wn_s[0, :, MIXW : MIXW + FF], r_s[c])
-        )
+        add_blocks(18, mul_t(norm_low(x1, inverse, gain(1, WIDE)), r[t]))
+        back_normed = mul(wn_s[0, :, MIXW : MIXW + FF], r[t])
+        yield
+        more, gain_grad = norm_back(x1, inverse, gain(1, WIDE), back_normed)
         ggain_s[1] += fold(gain_grad)
         put_wide(x2_s, c, back + more)
+        yield
+
+    places1 = {0: 0, 1: 1, 3: 2, 5: 3}
+    places0 = {0: 0, 1: 1, 2: 2, 3: 3, 4: 4, 5: 5, 6: 6, 7: 7, 9: 8}
+    steps0 = 2 * flat_depth + 2
+
+    def placed(places, step, place, each):
+        return [
+            functools.partial(step, places[place + each * t])
+            if place + each * t in places
+            else None
+            for t in range(pairs)
+        ]
+
+    def back_rest(t, carry):
+        at_time(t, placed(places1, step1, 0, 3))
+
+        def point(number):
+            if number in (1, 3):
+                at_time(t, placed(places1, step1, (number + 1) // 2, 3))
+
+        lockstep([rest_steps(t, 0), rest_steps(t, 1)], point)
         return carry
 
-    lax.fori_loop(0, chunks, back_rest, 0)
-    for j in range(2 * chunks, flat_depth + 1):
-        step1(j)
+    lax.fori_loop(0, pairs, back_rest, 0)
     for block in range(REST // D):
         rest_s[0, block * D : (block + 1) * D, :] = g0_s[FIRST // D + block].astype(bf16)
 
-    steps0 = 2 * flat_depth + 2
-
-    def back_first(c, carry):
-        at_chunk(c, step0, 0, 3, steps0)
+    for j in range(4, flat_depth + 1):
+        step1(j)
+
+    def first_steps(t, half):
+        c = 2 * t + half
+        qkv, o, dqkv = qkv_s[half], o_s[half], dqkv_s[half]
         back = get_wide(x2_s, c)
         lane = iota((D, LANES), 1)
         low = [jnp.where(lane < PACK, part, 0.0).astype(bf16) for part in unpack(back)]
         low = jnp.concatenate(low, 1)
-        add_blocks(9, mul_t(low, o_s[c]))
-        o_s[c] = mul(wt_s[0, 3 * WIDTH : 4 * WIDTH, :], low).astype(bf16)
+        yield
+        add_blocks(9, mul_t(low, o[t]))
+        o[t] = mul(wt_s[0, 3 * WIDTH : 4 * WIDTH, :], low).astype(bf16)
+        yield
         for first in range(0, GROUP, BATCH):
-            if first == GROUP // 2:
-                at_chunk(c, step0, 1, 3, steps0)
             queries, keys, values, backs = [], [], [], []
             for i in range(first, first + BATCH):
                 lanes = slice(i * LANES, (i + 1) * LANES)
-                queries += [qkv_s[c, part_of(j), lanes] for j in range(PAIRS)]
-                keys += [qkv_s[c, part_of(PAIRS + j), lanes] for j in range(PAIRS)]
-                values += [qkv_s[c, part_of(2 * PAIRS + j), lanes].T[:KEYS] for j in range(PAIRS)]
-                backs += [o_s[c, part_of(j), lanes] for j in range(PAIRS)]
-            chance = [p_s[GROUP * c + first + i] for i in range(BATCH)]
+                queries += [qkv[t, part_of(j), lanes] for j in range(PAIRS)]
+                keys += [qkv[t, part_of(PAIRS + j), lanes] for j in range(PAIRS)]
+                values += [qkv[t, part_of(2 * PAIRS + j), lanes].T[:KEYS] for j in range(PAIRS)]
+                backs += [o[t, part_of(j), lanes] for j in range(PAIRS)]
+            chance = [p_s[half][t, first + i] for i in range(BATCH)]
             *results, scores = attend_back(
                 keys, queries, values, backs, jnp.concatenate(chance, 1)
             )
             for i in range(BATCH):
                 lanes = slice((first + i) * LANES, (first + i + 1) * LANES)
                 own = slice(i * PAIRS, (i + 1) * PAIRS)
-                dqkv_s[:, lanes] = jnp.concatenate([x for part in results for x in part[own]], 0)
+                dqkv[:, lanes] = jnp.concatenate([x for part in results for x in part[own]], 0)
             width = HEADS * LANES
             gbias_s[...] += sum(scores[:, i * width : (i + 1) * width] for i in range(BATCH))
-        at_chunk(c, step0, 2, 3, steps0)
-        x0 = x0_s[c]
+            yield
+        x0 = x0_s[half][t]
         inverse = inverse_rms(x0)
-        add_blocks(0, mul_t(spread_low(x0 * inverse * gain(0, WIDE)), dqkv_s[...]))
-        back_normed = packed(mul(wn_s[0, :, : 3 * WIDTH], dqkv_s[...]))
+        add_blocks(0, mul_t(spread_low(x0 * inverse * gain(0, WIDE)), dqkv[...]))
+        back_normed = packed(mul(wn_s[0, :, : 3 * WIDTH], dqkv[...]))
+        yield
         more, gain_grad = norm_back(x0, inverse, gain(0, WIDE), back_normed)
         ggain_s[0] += fold(gain_grad)
         find(c)
         spread = mul_t(hot_s[...], split_low(back + more))
         ge_s[...] += spread[:, :D] + spread[:, D:]
+        yield
+
+    def back_first(t, carry):
+        at_time(t, placed(places0, step0, 0, 5))
+
+        def point(number):
+            place = {1: 1, attention // 2 + 1: 2, attention + 1: 3, attention + 2: 4}.get(number)
+            if place is not None:
+                at_time(t, placed(places0, step0, place, 5))
+
+        lockstep([first_steps(t, 0), first_steps(t, 1)], point)
         return carry
 
-    lax.fori_loop(0, chunks, back_first, 0)
+    lax.fori_loop(0, pairs, back_first, 0)
 
     for block in range(FIRST // D):
         value = g0_s[block]
@@ -910,7 +984,7 @@
         user_low_s, out_user_ref.at[span(slot * n, n)], local_sems.at[BLOCKS + 2]
     )
     store_users.start()
-    late = list(range(min(3 * chunks, steps0), steps0))
+    late = list(range(9, steps0))
     if late:
         step0(late.pop(0))
 
@@ -1085,14 +1159,21 @@
         in_specs=[vmem, smem, vmem, vmem, vmem, smem, vmem, hbm, hbm, hbm],
         out_specs=(vmem, hbm, hbm, hbm, vmem),
         scratch_shapes=[
-            pltpu.VMEM((chunks, D, WIDE), f32),
-            pltpu.VMEM((chunks, D, WIDE), f32),
+            pltpu.VMEM(shape, dtype)
+            for shape, dtype in (
+                ((chunks // 2, D, WIDE), f32),
+                ((chunks // 2, D, WIDE), f32),
+                ((chunks // 2, 3 * WIDTH, SPAN), bf16),
+                ((chunks // 2, GROUP, KEYS, HEADS * LANES), bf16),
+                ((chunks // 2, WIDTH, SPAN), bf16),
+                ((chunks // 2, FF, WIDE), bf16),
+                ((chunks // 2, 2 * WIDTH, WIDE), bf16),
+                ((3 * WIDTH, SPAN), bf16),
+            )
+            for _ in range(2)
+        ]
+        + [
             pltpu.VMEM((chunks * COLUMNS * D, LANES), f32),
-            pltpu.VMEM((chunks, 3 * WIDTH, SPAN), bf16),
-            pltpu.VMEM((n, KEYS, HEADS * LANES), bf16),
-            pltpu.VMEM((chunks, WIDTH, SPAN), bf16),
-            pltpu.VMEM((chunks, FF, WIDE), bf16),
-            pltpu.VMEM((chunks, 2 * WIDTH, WIDE), bf16),
             pltpu.VMEM((3 * WIDTH, 2 * LANES), bf16),
             pltpu.VMEM((2, D, COLS), bf16),
             pltpu.VMEM((2, COLS, D), bf16),
@@ -1119,7 +1200,6 @@
             pltpu.VMEM((24, LANES), f32),
             pltpu.VMEM((8, WIDE), jnp.int32),
             pltpu.VMEM((CODES + n, WIDE), bf16),
-            pltpu.VMEM((3 * WIDTH, SPAN), bf16),
             pltpu.VMEM((depth + 1,) + stat, f32),
             pltpu.VMEM((depth,) + stat, f32),
             pltpu.VMEM((2**NEAR, held_first[-1], D), bf16),

time: 165 us -> 170 us (1.030); the launches traced: 164 us -> 167 us
  Pallas kernels: 163 us -> 166 us
    pallas_call x1, Pallas kernels: 149 us -> 152 us  [gradients(): pl.pallas_call(functools.partial(step_kernel, n, dp), out_shape=(jax.Shap...]
where the time goes in v11:
time: 170 us; the launch traced here: 167 us
  Pallas kernels  166 us (98%)
    pallas_call x1, Pallas kernels, gradients(): pl.pallas_call(functools.partial(step_kernel, n, dp), out_shape=(jax.Shap...  152 us
    pallas_call x1, Pallas kernels, update(): pl.pallas_call(update_kernel, out_shape=[jax.ShapeDtypeStruct((1,), f32),...  13.6 us

profile of v11, /device:TPU:0, one launch (start us, length us, event | category | flops | bytes accessed | tf_op | source)
XLA Modules:
  0.0 166.9 jit_solution(9664487371647329537)
XLA Ops:
  0.7 152.4 %gradients.1 = (bf16[5376,128]{1,0:T(8,128)(2,1)}, bf16[1024,128]{1,0:T(8,128)(2,1)}, s32[32,8,128]{2,1,0:T(8,128)}, f32[32,24,128]{2,1,0:T(8,128)}, f32[8,128]{1,0:T(8,128)}) custom-call(s32[64,80]{1,0:T(8,128)} %refs_0_.1, s32[64]{0:T(128)} %refs_1_.1, s32[1,64]{1,0:T(1,128)} %bitcast.16, s32[4,64]{1,0:T(4,128)} %bitcast.15, s32[1,64]{1,0:T(1,128)} %bitcast.17, ...), custom_call_target="tpu_custom_call" | custom-call | tf_op jit(solution)/shard_map/gradients/pallas_call | solution.py:1150
  153.1 13.6 %update.1 = (f32[1]{0:T(128)}, f32[1]{0:T(128)}, f32[2]{0:T(128)}, f32[4,256]{1,0:T(4,128)}, f32[1,128,2304]{2,1,0:T(8,128)}, /*index=5*/f32[1,128,2304]{2,1,0:T...) custom-call(bf16[5376,128]{1,0:T(8,128)(2,1)} %get-tuple-element.49., ...), custom_call_target="tpu_custom_call" | custom-call | tf_op jit(solution)/shard_map/update/pallas_call | solution.py:1389

commit v12 on v11

--- a/solution.py
+++ b/solution.py
@@ -217,13 +217,14 @@
     codes_ref, users_ref, user_row_ref, targets_ref, domains_ref, bias_ref, gains_ref = refs[:7]
     mixer_ref, feed_ref, embed_ref = refs[7:10]
     out_ref, out_user_ref, out_ids_ref, out_slot_ref, out_stat_ref = refs[10:15]
-    x0_s, x1_s, qkv_s, p_s, o_s, r_s, mem_s, dqkv_s = [refs[15 + 2 * i : 17 + 2 * i] for i in range(8)]
-    refs = refs[31:]
+    x0_s, *doubles = refs[15], *[refs[16 + 2 * i : 18 + 2 * i] for i in range(9)]
+    x1_s, qkv_s, p_s, o_s, r_s, mem_s, dqkv_s, pc_s, oc_s = doubles
+    refs = refs[34:]
     x2_s, dz_s, wn_s, wt_s, ext_s = refs[:5]
     gain_s, ebias_s, dbias_s, g0_s, ge_s, gbias_s, ggain_s, rows_s, user_s, ids_s = refs[5:15]
-    cross_s, cross_back_s, pc_s, oc_s, rest_s, first_s, codes_s, slot_s, user_low_s, own_slot_s, id_rows_s, hot_s = refs[15:27]
-    stat_s, stat_land, near_first, near_codes, local_sems, sends, recvs = refs[27:34]
-    lands = refs[34:]
+    cross_s, cross_back_s, rest_s, first_s, codes_s, slot_s, user_low_s, own_slot_s, id_rows_s, hot_s = refs[15:25]
+    stat_s, stat_land, near_first, near_codes, local_sems, sends, recvs = refs[25:32]
+    lands = refs[32:]
     order = stages(dp)
     across = order[-1]
     depth = len(order)
@@ -288,13 +289,14 @@
     cross_scale = jnp.where(section == 1, scale, 1.0).astype(f32)
     for copy in locals_in:
         copy.wait()
-    for block in range(BLOCKS):
-        value = g0_s[block]
-        if block < 3:
-            value = value * scale
-        elif 12 <= block < 15:
-            value = value * cross_scale
-        wn_s[section, :, block * LANES : (block + 1) * LANES] = value.astype(bf16)
+    def cast_weights(block, carry):
+        factor = jnp.where((block >= 12) & (block < 15), cross_scale, 1.0)
+        factor = jnp.where(block < 3, scale, factor)
+        lanes = pl.ds(pl.multiple_of(block * LANES, LANES), LANES)
+        wn_s[section, :, lanes] = (g0_s[block] * factor).astype(bf16)
+        return carry
+
+    lax.fori_loop(0, BLOCKS, cast_weights, 0, unroll=2)
     pl.semaphore_wait(barrier, len(far) + len(masks))
     half = D // 2
     mine = span(side_of(order[0]) * half, half)
@@ -377,7 +379,7 @@
         user_s[pl.ds(i, 1), :] = x2_s[pl.ds(CODES + users_ref[section * n + i], 1), :]
         return carry
 
-    lax.fori_loop(0, n, fetch, 0, unroll=8)
+    lax.fori_loop(0, n, fetch, 0, unroll=4)
     for block in range(CODES // LANES + 1):
         if block < CODES // LANES:
             rows = x2_s[block * LANES : (block + 1) * LANES, :]
@@ -398,13 +400,13 @@
             rows = min(LANES, CODES + n - first)
             hot_s[first : first + rows, :] = onehot(ids - first, rows)
 
-    def lookup(c):
+    def lookup(c, carry):
         find(c)
         both = mul(ext_s[...], hot_s[...])
-        x0_s[c % 2][c // 2] = both[:D] + both[D:]
-
-    for c in range(chunks):
-        lookup(c)
+        x0_s[c] = both[:D] + both[D:]
+        return carry
+
+    lax.fori_loop(0, chunks, lookup, 0)
 
     beside = []
     for piece in pieces:
@@ -434,7 +436,7 @@
         def choose(b, table):
             return jnp.where(buckets == b, bias_ref[head, 0, b], table)
 
-        table = lax.fori_loop(0, BUCKETS, choose, jnp.zeros((KEYS, LANES), f32), unroll=True)
+        table = lax.fori_loop(0, BUCKETS, choose, jnp.zeros((KEYS, LANES), f32), unroll=8)
         ebias_s[:, lanes] = jnp.where(real, table, -1e30)
     key, query = iota((LANES, LANES), 0), iota((LANES, LANES), 1)
     offset = query - key
@@ -447,9 +449,12 @@
         dbias_s[:, lanes] = table
 
     def transpose_weights(which, first, last):
-        for block in range(first, last):
-            place = slice(block * LANES, (block + 1) * LANES)
+        def one(block, carry):
+            place = pl.ds(pl.multiple_of(block * LANES, LANES), LANES)
             wt_s[which, place, :] = wn_s[which, :, place].T
+            return carry
+
+        lax.fori_loop(first, last, one, 0, unroll=2)
 
     transpose_weights(section, 0, BLOCKS)
     beside[0].wait()
@@ -487,7 +492,7 @@
     def encode_steps(t, half):
         c = 2 * t + half
         qkv, o, r = qkv_s[half], o_s[half], r_s[half]
-        x0 = x0_s[half][t]
+        x0 = x0_s[c]
         h = spread_low(x0 * inverse_rms(x0) * gain(0, WIDE))
         yield
         for j in range(3):
@@ -624,7 +629,7 @@
     def gather_rows(ref):
         total = jnp.zeros((WIDTH, LANES), f32)
         for g in range(chunks):
-            total = total + mul(ref[g], spreader(g, False))
+            total = total + mul(ref[g % 2][g // 2], spreader(g, False))
         return total.astype(bf16)
 
     def blocks_of(table):
@@ -642,8 +647,8 @@
             rows.append(jnp.concatenate(columns, 1))
         return jnp.concatenate(rows, 0).astype(bf16)
 
-    def row_products(rows, g, first):
-        both = mul(rows, mem_s[g % 2][g // 2, first : first + WIDTH, :])
+    def row_products(rows, keys):
+        both = mul(rows, keys)
         parts = []
         for i in range(GROUP):
             own = both[32 * i : 32 * i + 32]
@@ -655,18 +660,25 @@
             parts.append(part)
         return jnp.concatenate(parts, 0)
 
-    def cross(g):
+    def cross_steps(t, half):
+        g = 2 * t + half
         queries = rows_of(g, cross_s[...])
-        scores = row_products(queries, g, 0)
+        yield
+        scores = row_products(queries, mem_s[half][t, :WIDTH, :])
         scores = jnp.where(iota(scores.shape, 1) < HIST_LEN, scores, -1e30)
         chance = jnp.exp(scores - jnp.max(scores, axis=1, keepdims=True))
         chance = chance * (1.0 / jnp.sum(chance, axis=1, keepdims=True))
-        pc_s[g] = chance
-        mixed = mul_t(mem_s[g % 2][g // 2, WIDTH:, :], blocks_of(chance))
-        oc_s[g] = jnp.where(head_mask(mixed.shape), mixed, 0.0).astype(bf16)
-
-    for g in range(chunks):
-        cross(g)
+        pc_s[half][t] = chance
+        yield
+        mixed = mul_t(mem_s[half][t, WIDTH:, :], blocks_of(chance))
+        oc_s[half][t] = jnp.where(head_mask(mixed.shape), mixed, 0.0).astype(bf16)
+        yield
+
+    def cross(t, carry):
+        lockstep([cross_steps(t, 0), cross_steps(t, 1)])
+        return carry
+
+    lax.fori_loop(0, pairs, cross, 0)
     cross_mixed = gather_rows(oc_s)
     y2 = y1 + mul(wn_s[1, :, 5 * WIDTH : 6 * WIDTH], cross_mixed)
     inverse2 = inverse_rms(y2)
@@ -706,20 +718,31 @@
     put_blocks(15, mul_t(low, cross_mixed))
     cross_back_s[...] = mul(wt_s[1, 5 * WIDTH : 6 * WIDTH, :], low).astype(bf16)
 
-    def cross_back(g):
+    def cross_back_steps(t, half):
+        g = 2 * t + half
+        memory = mem_s[half]
         mixed_rows = rows_of(g, cross_back_s[...])
-        back_chance = row_products(mixed_rows, g, WIDTH)
+        queries_t = rows_t_of(g, cross_s[...])
+        mixed_t = rows_t_of(g, cross_back_s[...])
+        yield
+        back_chance = row_products(mixed_rows, memory[t, WIDTH:, :])
         back_chance = jnp.where(iota(back_chance.shape, 1) < HIST_LEN, back_chance, 0.0)
-        chance = pc_s[g]
+        chance = pc_s[half][t]
         inner = jnp.sum(back_chance * chance, axis=1, keepdims=True)
+        yield
         spread = blocks_of(chance * (back_chance - inner))
-        total = mul_t(mem_s[g % 2][g // 2, :WIDTH, :], spread)
-        mem_s[g % 2][g // 2, :WIDTH, :] = mul(rows_t_of(g, cross_s[...]), spread).astype(bf16)
-        mem_s[g % 2][g // 2, WIDTH:, :] = mul(rows_t_of(g, cross_back_s[...]), blocks_of(chance)).astype(bf16)
-        oc_s[g] = jnp.where(head_mask(total.shape), total, 0.0).astype(bf16)
-
-    for g in range(chunks):
-        cross_back(g)
+        total = mul_t(memory[t, :WIDTH, :], spread)
+        oc_s[half][t] = jnp.where(head_mask(total.shape), total, 0.0).astype(bf16)
+        yield
+        memory[t, :WIDTH, :] = mul(queries_t, spread).astype(bf16)
+        memory[t, WIDTH:, :] = mul(mixed_t, blocks_of(chance)).astype(bf16)
+        yield
+
+    def cross_back(t, carry):
+        lockstep([cross_back_steps(t, 0), cross_back_steps(t, 1)])
+        return carry
+
+    lax.fori_loop(0, pairs, cross_back, 0)
     back_query = gather_rows(oc_s)
     put_blocks(12, mul_t(h1, back_query) * HEAD_DIM**-0.5)
     more, gain_grad = norm_back(
@@ -910,9 +933,12 @@
         return carry
 
     lax.fori_loop(0, pairs, back_rest, 0)
-    for block in range(REST // D):
-        rest_s[0, block * D : (block + 1) * D, :] = g0_s[FIRST // D + block].astype(bf16)
-
+    def cast_rest(block, carry):
+        place = pl.ds(pl.multiple_of(block * D, D), D)
+        rest_s[0, place, :] = g0_s[FIRST // D + block].astype(bf16)
+        return carry
+
+    lax.fori_loop(0, REST // D, cast_rest, 0, unroll=2)
     for j in range(4, flat_depth + 1):
         step1(j)
 
@@ -946,7 +972,7 @@
             width = HEADS * LANES
             gbias_s[...] += sum(scores[:, i * width : (i + 1) * width] for i in range(BATCH))
             yield
-        x0 = x0_s[half][t]
+        x0 = x0_s[c]
         inverse = inverse_rms(x0)
         add_blocks(0, mul_t(spread_low(x0 * inverse * gain(0, WIDE)), dqkv[...]))
         back_normed = packed(mul(wn_s[0, :, : 3 * WIDTH], dqkv[...]))
@@ -971,11 +997,13 @@
 
     lax.fori_loop(0, pairs, back_first, 0)
 
-    for block in range(FIRST // D):
-        value = g0_s[block]
-        if block < 3:
-            value = value * HEAD_DIM**-0.5
-        first_s[0, block * D : (block + 1) * D, :] = value.astype(bf16)
+    def cast_first(block, carry):
+        place = pl.ds(pl.multiple_of(block * D, D), D)
+        factor = jnp.where(block < 3, scale, 1.0)
+        first_s[0, place, :] = (g0_s[block] * factor).astype(bf16)
+        return carry
+
+    lax.fori_loop(0, FIRST // D, cast_first, 0, unroll=2)
     codes_s[...] = ge_s[:CODES, :].astype(bf16)
     begin(first0[0], 0)
     begin(codes[0], 0)
@@ -1001,7 +1029,7 @@
             rows_s[head, pl.ds(b, 1), :] = jnp.sum(hit, axis=0, keepdims=True)
         return carry
 
-    lax.fori_loop(0, BUCKETS, bucket_sums, 0, unroll=4)
+    lax.fori_loop(0, BUCKETS, bucket_sums, 0, unroll=2)
     for head in range(HEADS):
         sums = mul_exact_t(ones, rows_s[head])
         own_slot_s[8 + head : 9 + head, : 2 * BUCKETS] = sums[:1]
@@ -1158,10 +1186,10 @@
         ),
         in_specs=[vmem, smem, vmem, vmem, vmem, smem, vmem, hbm, hbm, hbm],
         out_specs=(vmem, hbm, hbm, hbm, vmem),
-        scratch_shapes=[
+        scratch_shapes=[pltpu.VMEM((chunks, D, WIDE), f32)]
+        + [
             pltpu.VMEM(shape, dtype)
             for shape, dtype in (
-                ((chunks // 2, D, WIDE), f32),
                 ((chunks // 2, D, WIDE), f32),
                 ((chunks // 2, 3 * WIDTH, SPAN), bf16),
                 ((chunks // 2, GROUP, KEYS, HEADS * LANES), bf16),
@@ -1169,6 +1197,8 @@
                 ((chunks // 2, FF, WIDE), bf16),
                 ((chunks // 2, 2 * WIDTH, WIDE), bf16),
                 ((3 * WIDTH, SPAN), bf16),
+                ((chunks // 2, 32 * GROUP, LANES), f32),
+                ((chunks // 2, WIDTH, 32 * GROUP), bf16),
             )
             for _ in range(2)
         ]
@@ -1190,8 +1220,6 @@
             pltpu.VMEM((n, LANES), jnp.int32),
             pltpu.VMEM((WIDTH, LANES), bf16),
             pltpu.VMEM((WIDTH, LANES), bf16),
-            pltpu.VMEM((chunks, 32 * GROUP, LANES), f32),
-            pltpu.VMEM((chunks, WIDTH, 32 * GROUP), bf16),
             pltpu.VMEM((2, REST, D), bf16),
             pltpu.VMEM((2, FIRST, D), bf16),
             pltpu.VMEM((CODES, D), bf16),
@@ -1210,7 +1238,7 @@
         ]
         + lands,
         compiler_params=pltpu.CompilerParams(
-            collective_id=0, has_side_effects=True, vmem_limit_bytes=63 * 2**20
+            collective_id=0, has_side_effects=True, vmem_limit_bytes=127 * 2**19
         ),
         name="gradients",
     )(codes, users, users.reshape(1, -1), targets, domains, bias, gains, mixer, feed, embedding)
@@ -1258,10 +1286,13 @@
                 total = total + ids_ref[part * slots + group * fit + other, :1, :]
             lanes.append(total)
         ids = jnp.concatenate(lanes, 1)
-        for block in range(users // USER_ROWS):
-            place = slice(block * USER_ROWS, (block + 1) * USER_ROWS)
+        def block_rows(block, carry):
+            place = pl.ds(pl.multiple_of(block * USER_ROWS, 8), USER_ROWS)
             hit = iota((USER_ROWS, span), 0) + block * USER_ROWS == ids
             user_grad[place, :] += mul(jnp.where(hit, 1.0, 0.0).astype(bf16), rows)
+            return carry
+
+        lax.fori_loop(0, users // USER_ROWS, block_rows, 0)
         return carry
 
     lax.fori_loop(0, user_ref.shape[0] // span, scatter, 0)
@@ -1335,7 +1366,7 @@
             hold[first][place],
             hold[first + 1][place],
             hold[first + 2][place],
-            factor * slope,
+            factor * slope.astype(f32),
             rate_matrix,
             decay_matrix,
         )
@@ -1343,36 +1374,46 @@
             hold[first + i][place] = outs[i]
         low_hold[kind][place] = outs[0].astype(bf16)
 
-    def block_of(block):
-        first = FIRST // D
-        place = block - first if block >= first else REST // D + block
-        return grad_ref[place * D : (place + 1) * D, :].astype(f32)
-
+    def rows_from(start, count):
+        return pl.ds(pl.multiple_of(start, 16), count)
+
+    def columns(kind, first, count, row):
+        def one(i, carry):
+            lanes = pl.ds(pl.multiple_of((first + i) * LANES, LANES), LANES)
+            step(kind, (0, slice(None), lanes), grad_ref[rows_from(row + i * D, D), :])
+            return carry
+
+        lax.fori_loop(0, count, one, 0)
+        store(kind, (0, slice(None), slice(first * LANES, (first + count) * LANES)))
+
+    def lines(first, count, size, source, row):
+        def one(i, carry):
+            place = (rows_from(first + i * size, size), slice(None))
+            step(2, place, source[rows_from(row + i * size, size), :])
+            return carry
+
+        lax.fori_loop(0, count, one, 0)
+        store(2, (slice(first, first + count * size), slice(None)))
+
+    skip = FIRST // LANES
     for i in range(3):
         loads[i].wait()
-    for part in range(6):
-        for block in range(3 * part, 3 * part + 3):
-            lanes = slice(block * LANES, (block + 1) * LANES)
-            step(0, (0, slice(None), lanes), block_of(block))
-        store(0, (0, slice(None), slice(3 * part * LANES, 3 * (part + 1) * LANES)))
+    columns(0, 0, skip // 2, REST)
+    columns(0, skip // 2, skip // 2, REST + skip // 2 * D)
+    columns(0, skip, MIXW // LANES - skip, 0)
     for i in range(3, 6):
         loads[i].wait()
-    for part in range(4):
-        for block in range(4 * part, 4 * part + 4):
-            lanes = slice(block * LANES, (block + 1) * LANES)
-            step(1, (0, slice(None), lanes), block_of(MIXW // LANES + block))
-        store(1, (0, slice(None), slice(4 * part * LANES, 4 * (part + 1) * LANES)))
+    for part in range(2):
+        first = part * FF // LANES
+        columns(1, first, FF // LANES, (MIXW // LANES - skip + first) * D)
     for i in range(6, 9):
         loads[i].wait()
-    for part in range(4):
-        rows = slice(part * CODEBOOK, (part + 1) * CODEBOOK)
-        step(2, (rows, slice(None)), grad_ref[COLS + rows.start : COLS + rows.stop, :].astype(f32))
-        store(2, (rows, slice(None)))
-    for part in range(users // USER_ROWS):
-        rows = slice(part * USER_ROWS, (part + 1) * USER_ROWS)
-        place = (slice(CODES + part * USER_ROWS, CODES + (part + 1) * USER_ROWS), slice(None))
-        step(2, place, user_grad[rows, :])
-        store(2, place)
+    for part in range(2):
+        lines(part * CODES // 2, 4, LANES, grad_ref, COLS + part * CODES // 2)
+    parts = users // USER_ROWS
+    lines(CODES, parts // 2, USER_ROWS, user_grad, 0)
+    done = parts // 2 * USER_ROWS
+    lines(CODES + done, parts - parts // 2, USER_ROWS, user_grad, done)
     for copy in stores:
         copy.wait()
 

time: 170 us -> 155 us (0.912); the launches traced: 167 us -> 154 us
  Pallas kernels: 166 us -> 153 us
    pallas_call x1, Pallas kernels: 152 us -> 139 us  [gradients(): pl.pallas_call(functools.partial(step_kernel, n, dp), out_shape=(jax.Shap...]
where the time goes in v12:
time: 155 us; the launch traced here: 154 us
  Pallas kernels  153 us (99%)
    pallas_call x1, Pallas kernels, gradients(): pl.pallas_call(functools.partial(step_kernel, n, dp), out_shape=(jax.Shap...  139 us
    pallas_call x1, Pallas kernels, update(): pl.pallas_call(update_kernel, out_shape=[jax.ShapeDtypeStruct((1,), f32),...  14.7 us

profile of v12, /device:TPU:0, one launch (start us, length us, event | category | flops | bytes accessed | tf_op | source)
XLA Modules:
  0.0 154.3 jit_solution(3506367926780875750)
XLA Ops:
  0.7 138.8 %gradients.1 = (bf16[5376,128]{1,0:T(8,128)(2,1)}, bf16[1024,128]{1,0:T(8,128)(2,1)}, s32[32,8,128]{2,1,0:T(8,128)}, f32[32,24,128]{2,1,0:T(8,128)}, f32[8,128]{1,0:T(8,128)}) custom-call(s32[64,80]{1,0:T(8,128)} %refs_0_.1, s32[64]{0:T(128)} %refs_1_.1, s32[1,64]{1,0:T(1,128)} %bitcast.16, s32[4,64]{1,0:T(4,128)} %bitcast.15, s32[1,64]{1,0:T(1,128)} %bitcast.17, ...), custom_call_target="tpu_custom_call" | custom-call | tf_op jit(solution)/shard_map/gradients/pallas_call | solution.py:1178
  139.5 14.7 %update.1 = (f32[1]{0:T(128)}, f32[1]{0:T(128)}, f32[2]{0:T(128)}, f32[4,256]{1,0:T(4,128)}, f32[1,128,2304]{2,1,0:T(8,128)}, /*index=5*/f32[1,128,2304]{2,1,0:T...) custom-call(bf16[5376,128]{1,0:T(8,128)(2,1)} %get-tuple-element.49., ...), custom_call_target="tpu_custom_call" | custom-call | tf_op jit(solution)/shard_map/update/pallas_call | solution.py:1430

commit v13 on v12

--- a/solution.py
+++ b/solution.py
@@ -189,6 +189,19 @@
     return [("dp", bit) for bit in bits[:2] + bits[4:] + bits[2:4]] + [("pipe", 1)]
 
 
+def code_stages(dp):
+    order = stages(dp)
+    return order[:1] + order[2:-NEAR] + order[-1:] + order[1:2] + order[-NEAR:-1]
+
+
+def high_low(x, parts):
+    rows = []
+    for _ in range(parts):
+        rows.append(x.astype(bf16))
+        x = x - rows[-1].astype(f32)
+    return jnp.concatenate(rows, 0)
+
+
 def side_of(stage):
     axis, bit = stage
     return lax.rem(lax.div(lax.axis_index(axis), bit), 2)
@@ -216,15 +229,17 @@
 def step_kernel(n, dp, *refs):
     codes_ref, users_ref, user_row_ref, targets_ref, domains_ref, bias_ref, gains_ref = refs[:7]
     mixer_ref, feed_ref, embed_ref = refs[7:10]
-    out_ref, out_user_ref, out_ids_ref, out_slot_ref, out_stat_ref = refs[10:15]
-    x0_s, *doubles = refs[15], *[refs[16 + 2 * i : 18 + 2 * i] for i in range(9)]
+    out_ref, out_ids_ref, out_slot_ref, out_stat_ref = refs[10:14]
+    refs = refs[14:]
+    x0_s, *doubles = refs[0], *[refs[1 + 2 * i : 3 + 2 * i] for i in range(9)]
     x1_s, qkv_s, p_s, o_s, r_s, mem_s, dqkv_s, pc_s, oc_s = doubles
-    refs = refs[34:]
+    refs = refs[19:]
     x2_s, dz_s, wn_s, wt_s, ext_s = refs[:5]
     gain_s, ebias_s, dbias_s, g0_s, ge_s, gbias_s, ggain_s, rows_s, user_s, ids_s = refs[5:15]
-    cross_s, cross_back_s, rest_s, first_s, codes_s, slot_s, user_low_s, own_slot_s, id_rows_s, hot_s = refs[15:25]
-    stat_s, stat_land, near_first, near_codes, local_sems, sends, recvs = refs[25:32]
-    lands = refs[32:]
+    cross_s, cross_back_s, rest_s, first_s, codes_s, slot_s, own_slot_s, squares_s, id_rows_s, hot_s = refs[15:25]
+    stat_s, stat_land, small_s, small_land, near_first, near_codes = refs[25:31]
+    local_sems, sends, recvs = refs[31:34]
+    lands = refs[34:]
     order = stages(dp)
     across = order[-1]
     depth = len(order)
@@ -248,16 +263,18 @@
         return remote_to(source, target, partner_of(stage))
 
     near, far = order[-NEAR:], order[:-NEAR]
-    masks = range(1, 2 ** len(near))
-
-    def device_of(mask):
+    route = code_stages(dp)
+    code_near, code_far = route[-NEAR:], route[:-NEAR]
+    masks = range(1, 2**NEAR)
+
+    def device_of(mask, near=near):
         place = {"dp": lax.axis_index("dp"), "pipe": lax.axis_index("pipe")}
         for i, (axis, bit) in enumerate(near):
             if mask >> i & 1:
                 place[axis] = place[axis] + bit * (1 - 2 * side_of((axis, bit)))
         return place
 
-    def shift_of(mask, lefts):
+    def shift_of(mask, lefts, near=near):
         total = 0
         for i, left in enumerate(lefts):
             side = side_of(near[i])
@@ -280,10 +297,11 @@
     load_embed.start()
 
     barrier = pltpu.get_barrier_semaphore()
-    for stage in far:
-        pl.semaphore_signal(barrier, inc=1, device_id=partner_of(stage), device_id_type=MESH)
-    for mask in masks:
-        pl.semaphore_signal(barrier, inc=1, device_id=device_of(mask), device_id_type=MESH)
+    greeted = [partner_of(stage) for stage in far if stage != code_near[0]]
+    greeted += [device_of(mask) for mask in masks]
+    greeted += [device_of(mask, code_near) for mask in masks if mask & 1]
+    for device in greeted:
+        pl.semaphore_signal(barrier, inc=1, device_id=device, device_id_type=MESH)
 
     scale = HEAD_DIM**-0.5
     cross_scale = jnp.where(section == 1, scale, 1.0).astype(f32)
@@ -297,7 +315,7 @@
         return carry
 
     lax.fori_loop(0, BLOCKS, cast_weights, 0, unroll=2)
-    pl.semaphore_wait(barrier, len(far) + len(masks))
+    pl.semaphore_wait(barrier, len(greeted))
     half = D // 2
     mine = span(side_of(order[0]) * half, half)
     pieces = (slice(0, FIRST), slice(FIRST, COLS))
@@ -341,7 +359,7 @@
     for r in range(8):
         stat_s[0, r : r + 1, :] = histogram[:1, r * LANES : (r + 1) * LANES]
     slot = 0
-    for k, stage in enumerate(order):
+    for k, stage in enumerate(route):
         slot = slot + side_of(stage) * 2 ** (depth - 1 - k)
     owner = iota((8, LANES), 1) // n
     own_users = jnp.broadcast_to(own_users, (8, LANES)).astype(jnp.int32)
@@ -354,7 +372,7 @@
         return pl.ds(lax.div(slot, 2**j) * 2**j, 2**j)
 
     early = []
-    for j, stage in enumerate(reversed(order)):
+    for j, stage in enumerate(reversed(route)):
         held = out_ids_ref.at[slots_of(j)]
         early.append(
             (
@@ -778,9 +796,9 @@
             hit = jnp.where(offset == b, self_scores[:, lanes], 0.0)
             rows_s[head, BUCKETS + b : BUCKETS + b + 1, :] = jnp.sum(hit, axis=0, keepdims=True)
 
-    def reducing(buffer, kept, held, upto):
+    def reducing(buffer, kept, held, stages):
         steps, at = [], 0
-        for k, stage in enumerate(order[:upto]):
+        for k, stage in enumerate(stages):
             rows, left = held[k], held[k + 1]
             side = side_of(stage)
             if left < rows:
@@ -813,11 +831,11 @@
     ):
         land[name], rest = rest[:number], rest[number:]
     land_rest, land_first = rest
-    rest1 = reducing(rest_s.at[1], land["rest1"], held_rest, flat_depth)
-    first1 = reducing(first_s.at[1], land["first1"], held_first, flat_depth)
-    rest0 = reducing(rest_s.at[0], land["rest0"], held_rest, flat_depth)
-    first0 = reducing(first_s.at[0], land["first0"], held_first, len(far))
-    codes = reducing(codes_s, land["codes"], held_codes, len(far))
+    rest1 = reducing(rest_s.at[1], land["rest1"], held_rest, order[:-1])
+    first1 = reducing(first_s.at[1], land["first1"], held_first, order[:-1])
+    rest0 = reducing(rest_s.at[0], land["rest0"], held_rest, order[:-1])
+    first0 = reducing(first_s.at[0], land["first0"], held_first, far)
+    codes = reducing(codes_s, land["codes"], held_codes, code_far)
 
     def step1(k):
         if k > 0:
@@ -866,7 +884,7 @@
             cross_rest.start()
         if k == flat_depth + 1:
             squares = settle(cross_rest, rest_s, land_rest, rest1[1], rest1[2][-1], 0)
-            own_slot_s[16:17, :] = squares / (dp * rest1[2][-1] // REST)
+            squares_s[0:1, :] = squares / (dp * rest1[2][-1] // REST)
         if k > flat_depth + 1 and gather_rest[k - flat_depth - 2] is not None:
             gather_rest[k - flat_depth - 2].wait()
         if flat_depth < k < 2 * flat_depth + 1 and gather_rest[k - flat_depth - 1] is not None:
@@ -1007,20 +1025,17 @@
     codes_s[...] = ge_s[:CODES, :].astype(bf16)
     begin(first0[0], 0)
     begin(codes[0], 0)
-    user_low_s[...] = ge_s[CODES:, :].astype(bf16)
-    store_users = pltpu.make_async_copy(
-        user_low_s, out_user_ref.at[span(slot * n, n)], local_sems.at[BLOCKS + 2]
-    )
-    store_users.start()
+    code_size = held_codes[-1]
+    own_slot_s[code_size : code_size + n, :] = ge_s[CODES:, :].astype(bf16)
     late = list(range(9, steps0))
     if late:
         step0(late.pop(0))
 
     ones = jnp.ones((8, LANES), f32)
-    own_slot_s[8:16, :] = jnp.zeros((8, LANES), f32)
+    small_s[0, 8:16, :] = jnp.zeros((8, LANES), f32)
     for g in range(7):
-        own_slot_s[g : g + 1, :] = mul_exact_t(ones, ggain_s[g])[:1]
-    own_slot_s[7:8, :] = jnp.broadcast_to(loss, (1, LANES))
+        small_s[0, g : g + 1, :] = mul_exact_t(ones, ggain_s[g])[:1]
+    small_s[0, 7:8, :] = jnp.broadcast_to(loss, (1, LANES))
 
     def bucket_sums(b, carry):
         for head in range(HEADS):
@@ -1032,8 +1047,11 @@
     lax.fori_loop(0, BUCKETS, bucket_sums, 0, unroll=2)
     for head in range(HEADS):
         sums = mul_exact_t(ones, rows_s[head])
-        own_slot_s[8 + head : 9 + head, : 2 * BUCKETS] = sums[:1]
-    own_slot_s[19:, :] = jnp.zeros((5, LANES), f32)
+        small_s[0, 8 + head : 9 + head, : 2 * BUCKETS] = sums[:1]
+    small_steps = [
+        remote(small_s.at[k], small_land.at[k], stage) for k, stage in enumerate(code_far)
+    ]
+    small_steps[0].start()
 
     for k in range(len(far)):
         finish(first0[0], first_s.at[0], land["first0"], k)
@@ -1041,23 +1059,24 @@
         if k + 1 < len(far):
             begin(first0[0], k + 1)
             begin(codes[0], k + 1)
+        small_steps[k].wait()
+        small_s[k + 1] = small_s[k] + small_land[k]
+        if k + 1 < len(far):
+            small_steps[k + 1].start()
 
     first_at, first_left = first0[1], held_first[len(far) + 1 :]
     codes_at, codes_left = codes[1], held_codes[len(far) + 1 :]
-    size, code_size = first_left[-1], codes_left[-1]
+    size = first_left[-1]
     mine_first = first_at + shift_of(0, first_left)
-    mine_codes = codes_at + shift_of(0, codes_left)
+    mine_codes = codes_at + shift_of(0, codes_left, code_near)
     inside, crossing_first, everyone = [], [], []
     for mask in masks:
         source = first_s.at[0, span(first_at + shift_of(mask, first_left), size)]
         copy = remote_to(source, near_first.at[mask], device_of(mask))
         (crossing_first if mask >> (NEAR - 1) else inside).append(copy)
     for mask in masks:
-        source = codes_s.at[span(codes_at + shift_of(mask, codes_left), code_size)]
-        everyone.append(remote_to(source, near_codes.at[mask], device_of(mask)))
-    store_users.wait()
-    held = out_user_ref.at[span(slot * n, n)]
-    users_out = [remote_to(held, held, device_of(mask)) for mask in masks]
+        source = codes_s.at[span(codes_at + shift_of(mask, codes_left, code_near), code_size)]
+        everyone.append(remote_to(source, near_codes.at[mask], device_of(mask, code_near)))
 
     @pl.when(section == 0)
     def _():
@@ -1070,17 +1089,19 @@
         for copy in crossing_first:
             copy.start()
 
-    for copy in everyone + users_out:
+    for copy in everyone:
         copy.start()
     for step in late:
         step0(step)
+    rows = code_size + n
+    own_slot_s[rows + 16 :, :] = high_low(small_s[len(far)], 2)
 
     def keep_first(value):
         value = value.astype(bf16)
         out_ref[span(REST + mine_first, size), :] = value
         value = value.astype(f32)
         squares = jnp.sum(value * value, axis=0, keepdims=True)
-        own_slot_s[17:18, :] = squares / (dp * size // FIRST)
+        squares_s[1:2, :] = squares / (dp * size // FIRST)
 
     @pl.when(section == 0)
     def _():
@@ -1102,57 +1123,42 @@
         value = first_s[1, span(mine_first, size), :].astype(f32)
         keep_first(value + land_first[...].astype(f32))
 
+    place = out_ref.at[span(REST + mine_first, size)]
+    copies = [
+        remote_to(place, place, device_of(mask)) for mask in masks if not mask >> (NEAR - 1)
+    ]
+    for copy in copies:
+        copy.start()
     for copy in everyone:
         copy.wait()
     value = codes_s[span(mine_codes, code_size), :].astype(f32)
     for mask in masks:
         value = value + near_codes[mask].astype(f32)
     value = value.astype(bf16)
-    out_ref[span(COLS + mine_codes, code_size), :] = value
+    own_slot_s[:code_size, :] = value
     value = value.astype(f32)
     squares = jnp.sum(value * value, axis=0, keepdims=True)
-    own_slot_s[18:19, :] = squares / (2 * dp * code_size // CODES)
-
-    store_slot = pltpu.make_async_copy(
-        own_slot_s, out_slot_ref.at[slot], local_sems.at[BLOCKS + 3]
-    )
+    squares_s[2:3, :] = squares / (2 * dp * code_size // CODES)
+    squares_s[3:, :] = jnp.zeros((5, LANES), f32)
+    own_slot_s[rows : rows + 16, :] = high_low(squares_s[...], 2)
+    kept_slot = out_slot_ref.at[slot]
+    store_slot = pltpu.make_async_copy(own_slot_s, kept_slot, local_sems.at[BLOCKS + 2])
     store_slot.start()
-
-    copies = []
-    place = out_ref.at[span(REST + mine_first, size)]
-    code_place = out_ref.at[span(COLS + mine_codes, code_size)]
-    for mask in masks:
-        device = device_of(mask)
-        if not mask >> (NEAR - 1):
-            copies.append(remote_to(place, place, device))
-        copies.append(remote_to(code_place, code_place, device))
-    for copy in copies:
+    slots_out = [remote_to(own_slot_s, kept_slot, device_of(mask, code_near)) for mask in masks]
+    for copy in slots_out:
         copy.start()
     store_slot.wait()
-    held = out_slot_ref.at[slot]
-    slots_out = [remote_to(held, held, device_of(mask)) for mask in masks]
-    for copy in slots_out:
-        copy.start()
-    copies += slots_out
-    for copy in copies + users_out:
+    for copy in copies + slots_out:
         copy.wait()
     for j, k in enumerate(reversed(range(len(far)))):
-        stage = far[k]
         copies = []
         if held_first[k + 1] < held_first[k]:
             place = out_ref.at[span(REST + first_at, held_first[k + 1])]
-            copies.append(remote(place, place, stage))
-            first_at = first_at - side_of(stage) * held_first[k + 1]
-        if held_codes[k + 1] < held_codes[k]:
-            place = out_ref.at[span(COLS + codes_at, held_codes[k + 1])]
-            copies.append(remote(place, place, stage))
-            codes_at = codes_at - side_of(stage) * held_codes[k + 1]
+            copies.append(remote(place, place, far[k]))
+            first_at = first_at - side_of(far[k]) * held_first[k + 1]
         slots = 2 ** (NEAR + j)
-        first_slot = lax.div(slot, slots) * slots
-        held = out_slot_ref.at[pl.ds(first_slot, slots)]
-        copies.append(remote(held, held, stage))
-        held = out_user_ref.at[span(first_slot * n, slots * n)]
-        copies.append(remote(held, held, stage))
+        held = out_slot_ref.at[pl.ds(lax.div(slot, slots) * slots, slots), pl.ds(0, rows + 16)]
+        copies.append(remote(held, held, code_far[k]))
         for copy in copies:
             copy.start()
         for copy in copies:
@@ -1171,6 +1177,7 @@
     stat = (16, LANES)
     held_rest, held_first, held_codes = shares(dp, REST), shares(dp, FIRST), shares(dp, CODES, 1)
     plane, far = depth - 1, depth - NEAR
+    slot_rows = held_codes[-1] + n + 16 + 32
     sizes = [*held_rest[1:] * 2, *held_first[1:]]
     sizes += [*held_first[1 : far + 1], *held_codes[1 : far + 1], held_rest[-1], held_first[-1]]
     lands = [pltpu.VMEM((rows, D), bf16) for rows in sizes]
@@ -1178,14 +1185,13 @@
     return pl.pallas_call(
         functools.partial(step_kernel, n, dp),
         out_shape=(
-            jax.ShapeDtypeStruct((COLS + CODES, D), bf16),
-            jax.ShapeDtypeStruct((devices * n, D), bf16),
+            jax.ShapeDtypeStruct((COLS, D), bf16),
             jax.ShapeDtypeStruct((devices, 8, LANES), jnp.int32),
-            jax.ShapeDtypeStruct((devices, 24, LANES), f32),
+            jax.ShapeDtypeStruct((devices, slot_rows, LANES), bf16),
             jax.ShapeDtypeStruct((8, LANES), f32),
         ),
         in_specs=[vmem, smem, vmem, vmem, vmem, smem, vmem, hbm, hbm, hbm],
-        out_specs=(vmem, hbm, hbm, hbm, vmem),
+        out_specs=(vmem, hbm, hbm, vmem),
         scratch_shapes=[pltpu.VMEM((chunks, D, WIDE), f32)]
         + [
             pltpu.VMEM(shape, dtype)
@@ -1224,15 +1230,17 @@
             pltpu.VMEM((2, FIRST, D), bf16),
             pltpu.VMEM((CODES, D), bf16),
             pltpu.VMEM((8, LANES), jnp.int32),
-            pltpu.VMEM((n, D), bf16),
-            pltpu.VMEM((24, LANES), f32),
+            pltpu.VMEM((slot_rows, LANES), bf16),
+            pltpu.VMEM((8, LANES), f32),
             pltpu.VMEM((8, WIDE), jnp.int32),
             pltpu.VMEM((CODES + n, WIDE), bf16),
             pltpu.VMEM((depth + 1,) + stat, f32),
             pltpu.VMEM((depth,) + stat, f32),
+            pltpu.VMEM((far + 1, 16, LANES), f32),
+            pltpu.VMEM((far, 16, LANES), f32),
             pltpu.VMEM((2**NEAR, held_first[-1], D), bf16),
             pltpu.VMEM((2**NEAR, held_codes[-1], D), bf16),
-            pltpu.SemaphoreType.DMA((BLOCKS + 4,)),
+            pltpu.SemaphoreType.DMA((BLOCKS + 3,)),
             pltpu.SemaphoreType.DMA((copies,)),
             pltpu.SemaphoreType.DMA((copies,)),
         ]
@@ -1257,60 +1265,89 @@
     return weight - rate * step, moment, square
 
 
-def update_kernel(*refs):
-    parts_in, big_in, small_in, refs = refs[:5], refs[5:14], refs[14:20], refs[20:]
+def update_kernel(n, dp, *refs):
+    parts_in, big_in, small_in, refs = refs[:4], refs[4:13], refs[13:19], refs[19:]
     loss_ref, norm_ref, section_ref, hist_ref = refs[:4]
     big_out, small_out, low_out, refs = refs[4:13], refs[13:19], refs[19:22], refs[22:]
-    parts, hold, low_hold = refs[:5], refs[5:14], refs[14:17]
-    user_grad, part_sems, in_sems, out_sems = refs[17:]
-    grad_ref, user_ref, ids_ref, slot_ref, stat_ref = parts
-    arrivals = [pltpu.make_async_copy(parts_in[i], parts[i], part_sems.at[i]) for i in range(5)]
+    parts, hold, low_hold = refs[:4], refs[4:13], refs[13:16]
+    user_grad, code_grad, part_sems, in_sems, out_sems = refs[16:]
+    grad_ref, ids_ref, slot_ref, stat_ref = parts
+    arrivals = [pltpu.make_async_copy(parts_in[i], parts[i], part_sems.at[i]) for i in range(4)]
     loads = [pltpu.make_async_copy(big_in[i], hold[i], in_sems.at[i]) for i in range(9)]
     for load in arrivals[1:] + arrivals[:1] + loads:
         load.start()
     for arrival in arrivals:
         arrival.wait()
+    devices = slot_ref.shape[0]
+    held = shares(dp, CODES, 1)
+    code_size = held[-1]
 
     users = user_grad.shape[0]
-    span = min(1024, user_ref.shape[0])
-    slots = span // LANES * (ids_ref.shape[0] * LANES // user_ref.shape[0])
-    fit = ids_ref.shape[0] * LANES // user_ref.shape[0]
+    fit = LANES // n
+    each = min(1024 // n, devices)
+    span_rows = each * n
     user_grad[...] = jnp.zeros_like(user_grad)
 
     def scatter(part, carry):
-        rows = user_ref[pl.ds(pl.multiple_of(part * span, span), span), :]
+        first = part * each
+        rows = [slot_ref[first + i, code_size : code_size + n, :] for i in range(each)]
+        rows = jnp.concatenate(rows, 0)
         lanes = []
-        for group in range(span // LANES):
-            total = ids_ref[part * slots + group * fit, :1, :]
-            for other in range(1, fit):
-                total = total + ids_ref[part * slots + group * fit + other, :1, :]
-            lanes.append(total)
+        for group in range(each // fit):
+            lanes.append(
+                sum(ids_ref[first + group * fit + other, :1, :] for other in range(fit))
+            )
         ids = jnp.concatenate(lanes, 1)
+
         def block_rows(block, carry):
             place = pl.ds(pl.multiple_of(block * USER_ROWS, 8), USER_ROWS)
-            hit = iota((USER_ROWS, span), 0) + block * USER_ROWS == ids
+            hit = iota((USER_ROWS, span_rows), 0) + block * USER_ROWS == ids
             user_grad[place, :] += mul(jnp.where(hit, 1.0, 0.0).astype(bf16), rows)
             return carry
 
         lax.fori_loop(0, users // USER_ROWS, block_rows, 0)
         return carry
 
-    lax.fori_loop(0, user_ref.shape[0] // span, scatter, 0)
+    lax.fori_loop(0, devices // each, scatter, 0)
 
     def total(x):
         return jnp.sum(jnp.sum(x, axis=0, keepdims=True), axis=1, keepdims=True)
 
-    def slot_sum(first):
-        def add(i, value):
-            return value + slot_ref[2 * i + first]
-
-        zero = jnp.zeros(slot_ref.shape[1:], f32)
-        return lax.fori_loop(0, slot_ref.shape[0] // 2, add, zero)
-
-    even, odd = slot_sum(0), slot_sum(1)
-    section_squares = [total(x[16:17] + x[17:18]) for x in (even, odd)]
-    small = even[:16] + odd[:16]
-    rest = total(even[18:19] + odd[18:19])
+    route = code_stages(dp)
+    depth = len(route)
+    near = 2**NEAR
+    top = code_size + n
+
+    def squares_of(slot):
+        value = slot_ref[slot, top : top + 16, :].astype(f32)
+        return value[:8] + value[8:]
+
+    def add(i, sums):
+        first = 2 * near * i
+        return tuple(
+            total + sum(squares_of(first + side * near + j) for j in range(near))
+            for side, total in enumerate(sums)
+        )
+
+    zero = jnp.zeros((8, LANES), f32)
+    even, odd = lax.fori_loop(0, devices // (2 * near), add, (zero, zero))
+    section_squares = [total(x[0:1] + x[1:2]) for x in (even, odd)]
+    rest = total(even[2:3] + odd[2:3])
+    first = 0
+    for k, stage in enumerate(route[:-NEAR]):
+        first = first + side_of(stage) * 2 ** (depth - 1 - k)
+    small = jnp.zeros((16, LANES), f32)
+    for i in range(near):
+        value = slot_ref[first + i, top + 16 :, :].astype(f32)
+        small = small + (value[:16] + value[16:])
+    for slot in range(devices):
+        at, kept = 0, True
+        for k in range(depth):
+            if slot >> (depth - 1 - k) & 1:
+                kept = kept and held[k + 1] < held[k]
+                at += held[k + 1]
+        if kept:
+            code_grad[at : at + code_size, :] = slot_ref[slot, :code_size, :]
     user_values = user_grad[...]
     rest = rest + total(user_values * user_values)
     lane, line = iota(small.shape, 1), iota(small.shape, 0)
@@ -1409,7 +1446,7 @@
     for i in range(6, 9):
         loads[i].wait()
     for part in range(2):
-        lines(part * CODES // 2, 4, LANES, grad_ref, COLS + part * CODES // 2)
+        lines(part * CODES // 2, 4, LANES, code_grad, part * CODES // 2)
     parts = users // USER_ROWS
     lines(CODES, parts // 2, USER_ROWS, user_grad, 0)
     done = parts // 2 * USER_ROWS
@@ -1418,7 +1455,7 @@
         copy.wait()
 
 
-def update(reduced, mixers, feeds, embeds, gains, biases):
+def update(n, dp, reduced, mixers, feeds, embeds, gains, biases):
     vmem = pl.BlockSpec(memory_space=pltpu.VMEM)
     smem = pl.BlockSpec(memory_space=pltpu.SMEM)
     hbm = pl.BlockSpec(memory_space=pl.ANY)
@@ -1428,7 +1465,7 @@
     users = embeds[0].shape[0] - CODES
     pieces = 4 * (6 + 4 + 4 + users // USER_ROWS)
     return pl.pallas_call(
-        update_kernel,
+        functools.partial(update_kernel, n, dp),
         out_shape=[
             jax.ShapeDtypeStruct((1,), f32),
             jax.ShapeDtypeStruct((1,), f32),
@@ -1437,14 +1474,15 @@
         ]
         + [jax.ShapeDtypeStruct(x.shape, f32) for x in big + small]
         + low,
-        in_specs=[hbm] * 14 + [vmem] * 6,
+        in_specs=[hbm] * 13 + [vmem] * 6,
         out_specs=[smem] * 3 + [vmem] + [hbm] * 9 + [vmem] * 6 + [hbm] * 3,
         scratch_shapes=[pltpu.VMEM(x.shape, x.dtype) for x in reduced]
         + [pltpu.VMEM(x.shape, f32) for x in big]
         + [pltpu.VMEM(x.shape, bf16) for x in low]
         + [
             pltpu.VMEM((users, D), f32),
-            pltpu.SemaphoreType.DMA((5,)),
+            pltpu.VMEM((CODES, D), bf16),
+            pltpu.SemaphoreType.DMA((4,)),
             pltpu.SemaphoreType.DMA((9,)),
             pltpu.SemaphoreType.DMA((pieces,)),
         ],
@@ -1491,6 +1529,8 @@
         lax.axis_size("dp"),
     )
     outs = update(
+        history_codes.shape[0] // 2,
+        lax.axis_size("dp"),
         reduced,
         (mixer, mixer_moment, mixer_square),
         (feed, feed_moment, feed_square),

time: 155 us -> 149 us (0.961)
  Pallas kernels: 153 us -> 148 us
    pallas_call x1, Pallas kernels: 139 us -> 134 us  [gradients(): pl.pallas_call(functools.partial(step_kernel, n, dp), out_shape=(jax.Shap...]
where the time goes in v13:
time: 149 us
  Pallas kernels  148 us (99%)
    pallas_call x1, Pallas kernels, gradients(): pl.pallas_call(functools.partial(step_kernel, n, dp), out_shape=(jax.Shap...  134 us
    pallas_call x1, Pallas kernels, update(): pl.pallas_call(functools.partial(update_kernel, n, dp), out_shape=[jax.Sh...  14.5 us

profile of v13, /device:TPU:0, one launch (start us, length us, event | category | flops | bytes accessed | tf_op | source)
XLA Modules:
  0.0 149.2 jit_solution(6301732324236641215)
XLA Ops:
  0.7 133.8 %gradients.1 = (bf16[4352,128]{1,0:T(8,128)(2,1)}, s32[32,8,128]{2,1,0:T(8,128)}, bf16[32,112,128]{2,1,0:T(8,128)(2,1)}, f32[8,128]{1,0:T(8,128)}) custom-call(s32[64,80]{1,0:T(8,128)} %refs_0_.1, s32[64]{0:T(128)} %refs_1_.1, s32[1,64]{1,0:T(1,128)} %bitcast.16, s32[4,64]{1,0:T(4,128)} %bitcast.15, s32[1,64]{1,0:T(1,128)} %bitcast.17, ...), custom_call_target="tpu_custom_call" | custom-call | tf_op jit(solution)/shard_map/gradients/pallas_call | solution.py:1185
  134.5 14.5 %update.1 = (f32[1]{0:T(128)}, f32[1]{0:T(128)}, f32[2]{0:T(128)}, f32[4,256]{1,0:T(4,128)}, f32[1,128,2304]{2,1,0:T(8,128)}, /*index=5*/f32[1,128,2304]{2,1,0:T...) custom-call(bf16[4352,128]{1,0:T(8,128)(2,1)} %get-tuple-element.48., ...), custom_call_target="tpu_custom_call" | custom-call | tf_op jit(solution)/shard_map/update/pallas_call | solution.py:1467

commit v14 on v13

--- a/solution.py
+++ b/solution.py
@@ -303,29 +303,6 @@
     for device in greeted:
         pl.semaphore_signal(barrier, inc=1, device_id=device, device_id_type=MESH)
 
-    scale = HEAD_DIM**-0.5
-    cross_scale = jnp.where(section == 1, scale, 1.0).astype(f32)
-    for copy in locals_in:
-        copy.wait()
-    def cast_weights(block, carry):
-        factor = jnp.where((block >= 12) & (block < 15), cross_scale, 1.0)
-        factor = jnp.where(block < 3, scale, factor)
-        lanes = pl.ds(pl.multiple_of(block * LANES, LANES), LANES)
-        wn_s[section, :, lanes] = (g0_s[block] * factor).astype(bf16)
-        return carry
-
-    lax.fori_loop(0, BLOCKS, cast_weights, 0, unroll=2)
-    pl.semaphore_wait(barrier, len(greeted))
-    half = D // 2
-    mine = span(side_of(order[0]) * half, half)
-    pieces = (slice(0, FIRST), slice(FIRST, COLS))
-    over = [
-        remote(wn_s.at[section, mine, piece], wn_s.at[section, mine, piece], across)
-        for piece in pieces
-    ]
-    for copy in over:
-        copy.start()
-
     ids_s[:, : HIST_LEN - 1] = codes_ref[pl.ds(pl.multiple_of(section * n, 8), n), :]
     lane, row = iota((n, LANES), 1), iota((n, LANES), 0)
     ids = ids_s[...] + ((lane & 3) << 8)
@@ -371,6 +348,62 @@
     def slots_of(j):
         return pl.ds(lax.div(slot, 2**j) * 2**j, 2**j)
 
+    for g in range(7):
+        gain_s[g] = jnp.broadcast_to(gains_ref[g : g + 1, :], (LANES, LANES)).T
+
+    def positions(axis):
+        index = iota((KEYS, LANES), axis)
+        return jnp.where(index == HIST_LEN - 1, 0, index + 1)
+
+    key, query = positions(0), positions(1)
+    distance = jnp.abs(query - key)
+    remoteness = jnp.zeros_like(distance)
+    for edge in (12, 16, 23, 32, 46, 64, 91):
+        remoteness = remoteness + (distance >= edge).astype(jnp.int32)
+    nearby = jnp.minimum(jnp.where(distance < 8, distance, 8 + remoteness), 15)
+    buckets = nearby + jnp.where(key > query, 16, 0)
+    real = iota((KEYS, LANES), 0) < HIST_LEN
+    for head in range(HEADS):
+        lanes = slice(head * LANES, (head + 1) * LANES)
+
+        def choose(b, table):
+            return jnp.where(buckets == b, bias_ref[head, 0, b], table)
+
+        table = lax.fori_loop(0, BUCKETS, choose, jnp.zeros((KEYS, LANES), f32), unroll=8)
+        ebias_s[:, lanes] = jnp.where(real, table, -1e30)
+    key, query = iota((LANES, LANES), 0), iota((LANES, LANES), 1)
+    offset = query - key
+    seen = ((key >> 2) == (query >> 2)) & (offset >= 0)
+    for head in range(HEADS):
+        lanes = slice(head * LANES, (head + 1) * LANES)
+        table = jnp.full((LANES, LANES), -1e30, f32)
+        for b in range(LEVELS):
+            table = jnp.where(seen & (offset == b), bias_ref[head, 1, b], table)
+        dbias_s[:, lanes] = table
+
+    scale = HEAD_DIM**-0.5
+    cross_scale = jnp.where(section == 1, scale, 1.0).astype(f32)
+    for copy in locals_in:
+        copy.wait()
+    def cast_weights(block, carry):
+        factor = jnp.where((block >= 12) & (block < 15), cross_scale, 1.0)
+        factor = jnp.where(block < 3, scale, factor)
+        lanes = pl.ds(pl.multiple_of(block * LANES, LANES), LANES)
+        wn_s[section, :, lanes] = (g0_s[block] * factor).astype(bf16)
+        return carry
+
+    lax.fori_loop(0, BLOCKS, cast_weights, 0, unroll=2)
+    pl.semaphore_wait(barrier, len(greeted))
+    half = D // 2
+    mine = span(side_of(order[0]) * half, half)
+    pieces = (slice(0, FIRST), slice(FIRST, COLS))
+    over = [
+        remote(wn_s.at[section, mine, piece], wn_s.at[section, mine, piece], across)
+        for piece in pieces
+    ]
+    for copy in over:
+        copy.start()
+
     early = []
     for j, stage in enumerate(reversed(route)):
         held = out_ids_ref.at[slots_of(j)]
@@ -433,39 +466,6 @@
     over[0].wait()
     beside[0].start()
 
-    for g in range(7):
-        gain_s[g] = jnp.broadcast_to(gains_ref[g : g + 1, :], (LANES, LANES)).T
-
-    def positions(axis):
-        index = iota((KEYS, LANES), axis)
-        return jnp.where(index == HIST_LEN - 1, 0, index + 1)
-
-    key, query = positions(0), positions(1)
-    distance = jnp.abs(query - key)
-    remoteness = jnp.zeros_like(distance)
-    for edge in (12, 16, 23, 32, 46, 64, 91):
-        remoteness = remoteness + (distance >= edge).astype(jnp.int32)
-    nearby = jnp.minimum(jnp.where(distance < 8, distance, 8 + remoteness), 15)
-    buckets = nearby + jnp.where(key > query, 16, 0)
-    real = iota((KEYS, LANES), 0) < HIST_LEN
-    for head in range(HEADS):
-        lanes = slice(head * LANES, (head + 1) * LANES)
-
-        def choose(b, table):
-            return jnp.where(buckets == b, bias_ref[head, 0, b], table)
-
-        table = lax.fori_loop(0, BUCKETS, choose, jnp.zeros((KEYS, LANES), f32), unroll=8)
-        ebias_s[:, lanes] = jnp.where(real, table, -1e30)
-    key, query = iota((LANES, LANES), 0), iota((LANES, LANES), 1)
-    offset = query - key
-    seen = ((key >> 2) == (query >> 2)) & (offset >= 0)
-    for head in range(HEADS):
-        lanes = slice(head * LANES, (head + 1) * LANES)
-        table = jnp.full((LANES, LANES), -1e30, f32)
-        for b in range(LEVELS):
-            table = jnp.where(seen & (offset == b), bias_ref[head, 1, b], table)
-        dbias_s[:, lanes] = table
-
     def transpose_weights(which, first, last):
         def one(block, carry):
             place = pl.ds(pl.multiple_of(block * LANES, LANES), LANES)
@@ -478,9 +478,11 @@
     beside[0].wait()
     transpose_weights(1 - section, 0, FIRST // LANES)
 
-    def rest_arrives():
+    def rest_passes():
         over[1].wait()
         beside[1].start()
+
+    def rest_arrives():
         beside[1].wait()
         transpose_weights(1 - section, FIRST // LANES, BLOCKS)
 
@@ -568,6 +570,7 @@
 
         def point(number):
             if number == attention // 2:
+                pl.when(t == 0)(rest_passes)
                 at_time(t, early_at(1, 3))
             if number == attention + 2:
                 pl.when(t == 0)(rest_arrives)
@@ -928,8 +931,8 @@
         put_wide(x2_s, c, back + more)
         yield
 
-    places1 = {0: 0, 1: 1, 3: 2, 5: 3}
-    places0 = {0: 0, 1: 1, 2: 2, 3: 3, 4: 4, 5: 5, 6: 6, 7: 7, 9: 8}
+    places1 = {0: 0, 1: 1, 4: 2}
+    places0 = {0: 0, 1: 1, 3: 2, 4: 3, 5: 4, 6: 5, 7: 6, 8: 7}
     steps0 = 2 * flat_depth + 2
 
     def placed(places, step, place, each):
@@ -957,9 +960,6 @@
         return carry
 
     lax.fori_loop(0, REST // D, cast_rest, 0, unroll=2)
-    for j in range(4, flat_depth + 1):
-        step1(j)
-
     def first_steps(t, half):
         c = 2 * t + half
         qkv, o, dqkv = qkv_s[half], o_s[half], dqkv_s[half]
@@ -1002,13 +1002,21 @@
         ge_s[...] += spread[:, :D] + spread[:, D:]
         yield
 
+    def both_steps(k):
+        if k == 0:
+            step1(3)
+        if k == 1:
+            for j in range(4, flat_depth + 1):
+                step1(j)
+        step0(k)
+
     def back_first(t, carry):
-        at_time(t, placed(places0, step0, 0, 5))
+        at_time(t, placed(places0, both_steps, 0, 5))
 
         def point(number):
             place = {1: 1, attention // 2 + 1: 2, attention + 1: 3, attention + 2: 4}.get(number)
             if place is not None:
-                at_time(t, placed(places0, step0, place, 5))
+                at_time(t, placed(places0, both_steps, place, 5))
 
         lockstep([first_steps(t, 0), first_steps(t, 1)], point)
         return carry
@@ -1027,31 +1035,28 @@
     begin(codes[0], 0)
     code_size = held_codes[-1]
     own_slot_s[code_size : code_size + n, :] = ge_s[CODES:, :].astype(bf16)
-    late = list(range(9, steps0))
+    late = list(range(8, steps0))
     if late:
         step0(late.pop(0))
 
-    ones = jnp.ones((8, LANES), f32)
-    small_s[0, 8:16, :] = jnp.zeros((8, LANES), f32)
-    for g in range(7):
-        small_s[0, g : g + 1, :] = mul_exact_t(ones, ggain_s[g])[:1]
-    small_s[0, 7:8, :] = jnp.broadcast_to(loss, (1, LANES))
-
-    def bucket_sums(b, carry):
+    def sum_small():
+        ones = jnp.ones((8, LANES), f32)
+        small_s[0, 8:16, :] = jnp.zeros((8, LANES), f32)
+        for g in range(7):
+            small_s[0, g : g + 1, :] = mul_exact_t(ones, ggain_s[g])[:1]
+        small_s[0, 7:8, :] = jnp.broadcast_to(loss, (1, LANES))
+
+        def bucket_sums(b, carry):
+            for head in range(HEADS):
+                lanes = slice(head * LANES, (head + 1) * LANES)
+                hit = jnp.where(buckets == b, gbias_s[:, lanes], 0.0)
+                rows_s[head, pl.ds(b, 1), :] = jnp.sum(hit, axis=0, keepdims=True)
+            return carry
+
+        lax.fori_loop(0, BUCKETS, bucket_sums, 0, unroll=2)
         for head in range(HEADS):
-            lanes = slice(head * LANES, (head + 1) * LANES)
-            hit = jnp.where(buckets == b, gbias_s[:, lanes], 0.0)
-            rows_s[head, pl.ds(b, 1), :] = jnp.sum(hit, axis=0, keepdims=True)
-        return carry
-
-    lax.fori_loop(0, BUCKETS, bucket_sums, 0, unroll=2)
-    for head in range(HEADS):
-        sums = mul_exact_t(ones, rows_s[head])
-        small_s[0, 8 + head : 9 + head, : 2 * BUCKETS] = sums[:1]
-    small_steps = [
-        remote(small_s.at[k], small_land.at[k], stage) for k, stage in enumerate(code_far)
-    ]
-    small_steps[0].start()
+            sums = mul_exact_t(ones, rows_s[head])
+            small_s[0, 8 + head : 9 + head, : 2 * BUCKETS] = sums[:1]
 
     for k in range(len(far)):
         finish(first0[0], first_s.at[0], land["first0"], k)
@@ -1059,10 +1064,8 @@
         if k + 1 < len(far):
             begin(first0[0], k + 1)
             begin(codes[0], k + 1)
-        small_steps[k].wait()
-        small_s[k + 1] = small_s[k] + small_land[k]
-        if k + 1 < len(far):
-            small_steps[k + 1].start()
+        if k == 0:
+            sum_small()
 
     first_at, first_left = first0[1], held_first[len(far) + 1 :]
     codes_at, codes_left = codes[1], held_codes[len(far) + 1 :]
@@ -1093,6 +1096,11 @@
         copy.start()
     for step in late:
         step0(step)
+    for k, stage in enumerate(code_far):
+        copy = remote(small_s.at[k], small_land.at[k], stage)
+        copy.start()
+        copy.wait()
+        small_s[k + 1] = small_s[k] + small_land[k]
     rows = code_size + n
     own_slot_s[rows + 16 :, :] = high_low(small_s[len(far)], 2)
 

time: 149 us -> 143 us (0.960)
  Pallas kernels: 148 us -> 142 us
    pallas_call x1, Pallas kernels: 134 us -> 128 us  [gradients(): pl.pallas_call(functools.partial(step_kernel, n, dp), out_shape=(jax.Shap...]
where the time goes in v14:
time: 143 us
  Pallas kernels  142 us (99%)
    pallas_call x1, Pallas kernels, gradients(): pl.pallas_call(functools.partial(step_kernel, n, dp), out_shape=(jax.Shap...  128 us
    pallas_call x1, Pallas kernels, update(): pl.pallas_call(functools.partial(update_kernel, n, dp), out_shape=[jax.Sh...  14.5 us

profile of v14, /device:TPU:0, one launch (start us, length us, event | category | flops | bytes accessed | tf_op | source)
XLA Modules:
  0.0 143.0 jit_solution(14082762621505720134)
XLA Ops:
  0.7 127.6 %gradients.1 = (bf16[4352,128]{1,0:T(8,128)(2,1)}, s32[32,8,128]{2,1,0:T(8,128)}, bf16[32,112,128]{2,1,0:T(8,128)(2,1)}, f32[8,128]{1,0:T(8,128)}) custom-call(s32[64,80]{1,0:T(8,128)} %refs_0_.1, s32[64]{0:T(128)} %refs_1_.1, s32[1,64]{1,0:T(1,128)} %bitcast.16, s32[4,64]{1,0:T(4,128)} %bitcast.15, s32[1,64]{1,0:T(1,128)} %bitcast.17, ...), custom_call_target="tpu_custom_call" | custom-call | tf_op jit(solution)/shard_map/gradients/pallas_call | solution.py:1193
  128.3 14.5 %update.1 = (f32[1]{0:T(128)}, f32[1]{0:T(128)}, f32[2]{0:T(128)}, f32[4,256]{1,0:T(4,128)}, f32[1,128,2304]{2,1,0:T(8,128)}, /*index=5*/f32[1,128,2304]{2,1,0:T...) custom-call(bf16[4352,128]{1,0:T(8,128)(2,1)} %get-tuple-element.48., ...), custom_call_target="tpu_custom_call" | custom-call | tf_op jit(solution)/shard_map/update/pallas_call | solution.py:1475

commit v15 on v14

--- a/solution.py
+++ b/solution.py
@@ -177,11 +177,6 @@
         for part in (back_query, back_keys, back_values)
     ]
     return *results, back_scores
-
-
-def split_low(x):
-    high = x.astype(bf16)
-    return jnp.concatenate([high, (x - high.astype(f32)).astype(bf16)], 0)
 
 
 def stages(dp):
@@ -789,8 +784,7 @@
     )
     ggain_s[3] = gain_grad
     back = back + more
-    spread = mul_t(start, split_low(back))
-    ge_s[:CODES, :] = table_grad + spread[:, :D] + spread[:, D:]
+    ge_s[:CODES, :] = table_grad + mul_t(start, back.astype(bf16))
     ge_s[CODES:, :] = jnp.zeros((n, D), f32)
     rows_s[...] = jnp.zeros_like(rows_s)
     for head in range(HEADS):
@@ -998,8 +992,7 @@
         more, gain_grad = norm_back(x0, inverse, gain(0, WIDE), back_normed)
         ggain_s[0] += fold(gain_grad)
         find(c)
-        spread = mul_t(hot_s[...], split_low(back + more))
-        ge_s[...] += spread[:, :D] + spread[:, D:]
+        ge_s[...] += mul_t(hot_s[...], (back + more).astype(bf16))
         yield
 
     def both_steps(k):
@@ -1372,6 +1365,73 @@
         lanes = slice((row % 2) * LANES, (row % 2 + 1) * LANES)
         hist_ref[row // 2 : row // 2 + 1, lanes] = stat_ref[row : row + 1, :]
 
+    stores = []
+
+    def store(kind, place):
+        first = 3 * kind
+        pieces = [(hold[first + i], big_out[first + i]) for i in range(3)]
+        pieces.append((low_hold[kind], low_out[kind]))
+        for source, target in pieces:
+            copy = pltpu.make_async_copy(
+                source.at[place], target.at[place], out_sems.at[len(stores)]
+            )
+            copy.start()
+            stores.append(copy)
+
+    def step(kind, place, slope):
+        first = 3 * kind
+        outs = adam(
+            hold[first][place],
+            hold[first + 1][place],
+            hold[first + 2][place],
+            factor * slope.astype(f32),
+            rate_matrix,
+            decay_matrix,
+        )
+        for i in range(3):
+            hold[first + i][place] = outs[i]
+        low_hold[kind][place] = outs[0].astype(bf16)
+
+    def rows_from(start, count):
+        return pl.ds(pl.multiple_of(start, 16), count)
+
+    def columns(kind, first, count, row):
+        def one(i, carry):
+            lanes = pl.ds(pl.multiple_of((first + i) * LANES, LANES), LANES)
+            step(kind, (0, slice(None), lanes), grad_ref[rows_from(row + i * D, D), :])
+            return carry
+
+        lax.fori_loop(0, count, one, 0)
+        store(kind, (0, slice(None), slice(first * LANES, (first + count) * LANES)))
+
+    def lines(first, count, size, source, row):
+        def one(i, carry):
+            place = (rows_from(first + i * size, size), slice(None))
+            step(2, place, source[rows_from(row + i * size, size), :])
+            return carry
+
+        lax.fori_loop(0, count, one, 0)
+        store(2, (slice(first, first + count * size), slice(None)))
+
+    skip = FIRST // LANES
+    for i in range(3):
+        loads[i].wait()
+    columns(0, 0, skip // 2, REST)
+    columns(0, skip // 2, skip // 2, REST + skip // 2 * D)
+    columns(0, skip, MIXW // LANES - skip, 0)
+    for i in range(3, 6):
+        loads[i].wait()
+    for part in range(2):
+        first = part * FF // LANES
+        columns(1, first, FF // LANES, (MIXW // LANES - skip + first) * D)
+    for i in range(6, 9):
+        loads[i].wait()
+    for part in range(2):
+        lines(part * CODES // 2, 4, LANES, code_grad, part * CODES // 2)
+    parts = users // USER_ROWS
+    lines(CODES, parts // 2, USER_ROWS, user_grad, 0)
+    done = parts // 2 * USER_ROWS
+    lines(CODES + done, parts - parts // 2, USER_ROWS, user_grad, done)
     outs = adam(
         small_in[0][...], small_in[1][...], small_in[2][...], factor * small[:7], rate_gain, 0.0
     )
@@ -1392,73 +1452,6 @@
             for ref, value in zip(small_out[3:], outs):
                 ref[head, one, :] = value
 
-    stores = []
-
-    def store(kind, place):
-        first = 3 * kind
-        pieces = [(hold[first + i], big_out[first + i]) for i in range(3)]
-        pieces.append((low_hold[kind], low_out[kind]))
-        for source, target in pieces:
-            copy = pltpu.make_async_copy(
-                source.at[place], target.at[place], out_sems.at[len(stores)]
-            )
-            copy.start()
-            stores.append(copy)
-
-    def step(kind, place, slope):
-        first = 3 * kind
-        outs = adam(
-            hold[first][place],
-            hold[first + 1][place],
-            hold[first + 2][place],
-            factor * slope.astype(f32),
-            rate_matrix,
-            decay_matrix,
-        )
-        for i in range(3):
-            hold[first + i][place] = outs[i]
-        low_hold[kind][place] = outs[0].astype(bf16)
-
-    def rows_from(start, count):
-        return pl.ds(pl.multiple_of(start, 16), count)
-
-    def columns(kind, first, count, row):
-        def one(i, carry):
-            lanes = pl.ds(pl.multiple_of((first + i) * LANES, LANES), LANES)
-            step(kind, (0, slice(None), lanes), grad_ref[rows_from(row + i * D, D), :])
-            return carry
-
-        lax.fori_loop(0, count, one, 0)
-        store(kind, (0, slice(None), slice(first * LANES, (first + count) * LANES)))
-
-    def lines(first, count, size, source, row):
-        def one(i, carry):
-            place = (rows_from(first + i * size, size), slice(None))
-            step(2, place, source[rows_from(row + i * size, size), :])
-            return carry
-
-        lax.fori_loop(0, count, one, 0)
-        store(2, (slice(first, first + count * size), slice(None)))
-
-    skip = FIRST // LANES
-    for i in range(3):
-        loads[i].wait()
-    columns(0, 0, skip // 2, REST)
-    columns(0, skip // 2, skip // 2, REST + skip // 2 * D)
-    columns(0, skip, MIXW // LANES - skip, 0)
-    for i in range(3, 6):
-        loads[i].wait()
-    for part in range(2):
-        first = part * FF // LANES
-        columns(1, first, FF // LANES, (MIXW // LANES - skip + first) * D)
-    for i in range(6, 9):
-        loads[i].wait()
-    for part in range(2):
-        lines(part * CODES // 2, 4, LANES, code_grad, part * CODES // 2)
-    parts = users // USER_ROWS
-    lines(CODES, parts // 2, USER_ROWS, user_grad, 0)
-    done = parts // 2 * USER_ROWS
-    lines(CODES + done, parts - parts // 2, USER_ROWS, user_grad, done)
     for copy in stores:
         copy.wait()
 

time: 143 us -> 143 us (level)
  no operation moved by 1% of the time
where the time goes in v15:
time: 143 us
  Pallas kernels  142 us (99%)
    pallas_call x1, Pallas kernels, gradients(): pl.pallas_call(functools.partial(step_kernel, n, dp), out_shape=(jax.Shap...  128 us
    pallas_call x1, Pallas kernels, update(): pl.pallas_call(functools.partial(update_kernel, n, dp), out_shape=[jax.Sh...  14.5 us

profile of v15, /device:TPU:0, one launch (start us, length us, event | category | flops | bytes accessed | tf_op | source)
XLA Modules:
  0.0 143.1 jit_solution(9858524260817326416)
XLA Ops:
  0.7 127.7 %gradients.1 = (bf16[4352,128]{1,0:T(8,128)(2,1)}, s32[32,8,128]{2,1,0:T(8,128)}, bf16[32,112,128]{2,1,0:T(8,128)(2,1)}, f32[8,128]{1,0:T(8,128)}) custom-call(s32[64,80]{1,0:T(8,128)} %refs_0_.1, s32[64]{0:T(128)} %refs_1_.1, s32[1,64]{1,0:T(1,128)} %bitcast.16, s32[4,64]{1,0:T(4,128)} %bitcast.15, s32[1,64]{1,0:T(1,128)} %bitcast.17, ...), custom_call_target="tpu_custom_call" | custom-call | tf_op jit(solution)/shard_map/gradients/pallas_call | solution.py:1186
  128.4 14.5 %update.1 = (f32[1]{0:T(128)}, f32[1]{0:T(128)}, f32[2]{0:T(128)}, f32[4,256]{1,0:T(4,128)}, f32[1,128,2304]{2,1,0:T(8,128)}, /*index=5*/f32[1,128,2304]{2,1,0:T...) custom-call(bf16[4352,128]{1,0:T(8,128)(2,1)} %get-tuple-element.48., ...), custom_call_target="tpu_custom_call" | custom-call | tf_op jit(solution)/shard_map/update/pallas_call | solution.py:1468
